TPU v7x, 32 devices: a whole 2x2x4 slice. The times are simulated.
32 devices in a mesh: dp: 8 (over z, y), fsdp: 4 (over x, core).
Axes of the slice: x: 2, y: 2, z: 4, core: 2. Of those that a mesh axis runs over, the one named last changes fastest.
Arguments:
- tokens: bfloat16 [16384, 1024], P(('dp', 'fsdp')), may hold values from -6 to 6
- cotangent: bfloat16 [16384, 1024], P(('dp', 'fsdp')), may hold values from -6 to 6
- group: int32 [8], P('dp'), may hold values from 0 to 1, as said below
- images: int32 [8, 4], P('dp', 'fsdp'), may hold values from 1 to 10, as said below
- counts: int32 [2], replicated, may hold values from 100 to 999
- ln_gain: bfloat16 [2, 1024], P(None, 'fsdp'), may hold values from 0.19921875 to 1.796875
- ln_bias: bfloat16 [2, 1024], P(None, 'fsdp'), may hold values from -3 to 3
- w_qkv: bfloat16 [1024, 3072], P(None, 'fsdp'), may hold values from -0.25 to 0.25
- qv_bias: bfloat16 [2, 1024], P(None, 'fsdp'), may hold values from -3 to 3
- w_out: bfloat16 [1024, 1024], P(None, 'fsdp'), may hold values from -0.75 to 0.75
- out_bias: bfloat16 [2, 1024], P(None, 'fsdp'), may hold values from -3 to 3
- w_up: bfloat16 [1024, 4096], P(None, 'fsdp'), may hold values from -0.1875 to 0.1875
- up_bias: bfloat16 [4096], P('fsdp'), may hold values from -3 to 3
- w_down: bfloat16 [4096, 1024], P('fsdp'), may hold values from -0.125 to 0.125
Outputs:
- output: bfloat16 [16384, 1024], P(('dp', 'fsdp'))
- grad_tokens: bfloat16 [16384, 1024], P(('dp', 'fsdp'))
- g_ln_gain: float32 [2, 1024], P(None, 'fsdp')
- g_ln_bias: float32 [2, 1024], P(None, 'fsdp')
- g_w_qkv: float32 [1024, 3072], P(None, 'fsdp')
- g_qv_bias: float32 [2, 1024], P(None, 'fsdp')
- g_w_out: float32 [1024, 1024], P(None, 'fsdp')
- g_out_bias: float32 [2, 1024], P(None, 'fsdp')
- g_w_up: float32 [1024, 4096], P(None, 'fsdp')
- g_up_bias: float32 [4096], P('fsdp')
- g_w_down: float32 [4096, 1024], P('fsdp')
Inputs may be any that keep to these rules, and one draw needn't show every extreme that they name: `group`: exactly half of the 8 entries are 1. A device of group 0 holds at most 10 images of 50 tokens, one of group 1 at most 3 images of 145 tokens; the devices of fsdp index 0 hold exactly that most.
All inputs are finite; a program needn't handle non-finite values.
Results may differ from a plain program's by a relative error of at most 0.015.
Values may be sent and summed in bfloat16 or wider, within the bound.
A program may use at most 256 MiB of HBM per device.

v0:
```python
from functools import partial

import jax
import jax.numpy as jnp
from jax import lax
from jax.sharding import PartitionSpec as P

D = 1024
HEADS = 16
HDIM = 64
LEN0 = 50
LEN1 = 145


EPSILON = 1e-06


def layer_norm(inputs, gain_row, shift_row):
    center = inputs - jnp.mean(inputs, axis=-1, keepdims=True)
    spread = jnp.mean(center * center, axis=-1, keepdims=True)
    return center * lax.rsqrt(spread + EPSILON) * gain_row + shift_row


def dot_plain(first_op, second_op):
    return jnp.dot(first_op, second_op, preferred_element_type=jnp.float32)


def dot_right_t(first_op, second_op):
    return lax.dot_general(
        first_op, second_op, (((1,), (1,)), ((), ())), preferred_element_type=jnp.float32
    )


def dot_left_t(first_op, second_op):
    return lax.dot_general(
        first_op, second_op, (((0,), (0,)), ((), ())), preferred_element_type=jnp.float32
    )


def segment_ids(group_id, image_count, row_count):
    length = jnp.where(group_id == 0, LEN0, LEN1).astype(jnp.int32)
    position = jnp.arange(row_count, dtype=jnp.int32)
    image_index = position // length
    in_image = image_index < image_count
    return (jnp.where(in_image, image_index, row_count), in_image)


def block_scores(query_part, key_rows, segment_part, segment):
    scores = jnp.einsum(
        "qhd,khd->hqk", query_part, key_rows, preferred_element_type=jnp.float32
    ) * HDIM ** (-0.5)
    allowed = segment_part[:, None] == segment[None, :]
    return jnp.where(allowed[None], scores, -1e30)


def attend_forward(queries, key_rows, values, segment, block_rows):
    row_count = queries.shape[0]

    def attend_block(offset):
        scores = block_scores(queries, key_rows, segment, segment)
        highest = jnp.max(scores, axis=-1, keepdims=True)
        weights = jnp.exp(scores - highest)
        totals = jnp.sum(weights, axis=-1, keepdims=True)
        low_weights = (weights / totals).astype(jnp.bfloat16)
        mixture = jnp.einsum(
            "hqk,khd->qhd", low_weights, values, preferred_element_type=jnp.float32
        )
        return (mixture, (highest + jnp.log(totals))[..., 0])

    offsets = jnp.arange(row_count // block_rows, dtype=jnp.int32) * block_rows
    mixture, log_total = lax.map(attend_block, offsets)
    return (mixture.reshape(row_count, D), log_total)


def attend_backward(queries, key_rows, values, grad_mix, segment, log_total, block_rows):
    row_count = queries.shape[0]

    def visit(carry, record):
        grad_keys, grad_values = carry
        offset, log_part = record
        scores = block_scores(queries, key_rows, segment, segment)
        weights = jnp.exp(scores - log_part[..., None])
        low_weights = weights.astype(jnp.bfloat16)
        grad_weights = jnp.einsum(
            "qhd,khd->hqk", grad_mix, values, preferred_element_type=jnp.float32
        )
        inner = jnp.sum(weights * grad_weights, axis=-1, keepdims=True)
        grad_scores = (weights * (grad_weights - inner)).astype(jnp.bfloat16)
        grad_query = jnp.einsum(
            "hqk,khd->qhd", grad_scores, key_rows, preferred_element_type=jnp.float32
        ) * HDIM ** (-0.5)
        grad_keys = grad_keys + jnp.einsum(
            "hqk,qhd->khd", grad_scores, queries, preferred_element_type=jnp.float32
        ) * HDIM ** (-0.5)
        grad_values = grad_values + jnp.einsum(
            "hqk,qhd->khd", low_weights, grad_mix, preferred_element_type=jnp.float32
        )
        return ((grad_keys, grad_values), grad_query)

    offsets = jnp.arange(row_count // block_rows, dtype=jnp.int32) * block_rows
    empty_grad = jnp.zeros((row_count, HEADS, HDIM), jnp.float32)
    (grad_keys, grad_values), grad_query = lax.scan(
        visit, (empty_grad, empty_grad), (offsets, log_total)
    )
    return (
        grad_query.reshape(row_count, D),
        grad_keys.reshape(row_count, D),
        grad_values.reshape(row_count, D),
    )


def local(
    tokens,
    cotangent,
    group,
    images,
    counts,
    ln_gain,
    ln_bias,
    w_qkv,
    qv_bias,
    w_out,
    out_bias,
    w_up,
    up_bias,
    w_down,
):
    row_count = tokens.shape[0]
    block_rows = 512
    group_id = group[0]
    segment, in_image = segment_ids(group_id, images[0, 0], row_count)
    gains_low, shifts_low, qkv_full, qv_low, proj_full, outb_low = (
        lax.all_gather(ln_gain, "fsdp", axis=1, tiled=True),
        lax.all_gather(ln_bias, "fsdp", axis=1, tiled=True),
        lax.all_gather(w_qkv, "fsdp", axis=1, tiled=True),
        lax.all_gather(qv_bias, "fsdp", axis=1, tiled=True),
        lax.all_gather(w_out, "fsdp", axis=1, tiled=True),
        lax.all_gather(out_bias, "fsdp", axis=1, tiled=True),
    )
    gains = gains_low.astype(jnp.float32)
    shifts = shifts_low.astype(jnp.float32)
    qv_full = qv_low.astype(jnp.float32)
    outb_full = outb_low.astype(jnp.float32)
    inputs = tokens.astype(jnp.float32)
    normed = layer_norm(inputs, gains[0], shifts[0]).astype(jnp.bfloat16)
    projected = dot_plain(normed, qkv_full)
    queries = (projected[:, :D] + qv_full[0]).astype(jnp.bfloat16).reshape(row_count, HEADS, HDIM)
    key_rows = projected[:, D : 2 * D].astype(jnp.bfloat16).reshape(row_count, HEADS, HDIM)
    values = (
        (projected[:, 2 * D :] + qv_full[1]).astype(jnp.bfloat16).reshape(row_count, HEADS, HDIM)
    )
    attended, log_total = attend_forward(queries, key_rows, values, segment, block_rows)
    attended = attended.astype(jnp.bfloat16)
    middle = inputs + dot_plain(attended, proj_full) + outb_full[0]
    up_full, upb_low, down_full = (
        lax.all_gather(w_up, "fsdp", axis=1, tiled=True),
        lax.all_gather(up_bias, "fsdp", axis=0, tiled=True),
        lax.all_gather(w_down, "fsdp", axis=0, tiled=True),
    )
    normed_mlp = layer_norm(middle, gains[1], shifts[1]).astype(jnp.bfloat16)
    hidden_pre = dot_plain(normed_mlp, up_full) + upb_low.astype(jnp.float32)
    hidden = jax.nn.gelu(hidden_pre, approximate=False).astype(jnp.bfloat16)
    output = (middle + dot_plain(hidden, down_full) + outb_full[1]).astype(jnp.bfloat16)
    up_full, down_full = (
        lax.all_gather(w_up, "fsdp", axis=1, tiled=True),
        lax.all_gather(w_down, "fsdp", axis=0, tiled=True),
    )
    grad_out = cotangent.astype(jnp.float32) * in_image[:, None].astype(jnp.float32)
    grad_low = grad_out.astype(jnp.bfloat16)
    grad_hidden = dot_right_t(grad_low, down_full)
    gelu_value, gelu_pull = jax.vjp(partial(jax.nn.gelu, approximate=False), hidden_pre)
    grad_pre = gelu_pull(grad_hidden)[0].astype(jnp.bfloat16)
    grad_normed_mlp = dot_right_t(grad_pre, up_full)
    norm_value, norm_pull = jax.vjp(layer_norm, middle, gains[1], shifts[1])
    grad_mid_norm, grad_gain_mlp, grad_shift_mlp = norm_pull(grad_normed_mlp)
    grad_middle = grad_out + grad_mid_norm
    grad_branch = grad_middle.astype(jnp.bfloat16)
    qkv_full, proj_full = (
        lax.all_gather(w_qkv, "fsdp", axis=1, tiled=True),
        lax.all_gather(w_out, "fsdp", axis=1, tiled=True),
    )
    grad_attended = (
        dot_right_t(grad_branch, proj_full).astype(jnp.bfloat16).reshape(row_count, HEADS, HDIM)
    )
    grad_query, grad_keys, grad_values = attend_backward(
        queries, key_rows, values, grad_attended, segment, log_total, block_rows
    )
    grad_mixed = jnp.concatenate([grad_query, grad_keys, grad_values], axis=1).astype(jnp.bfloat16)
    grad_normed = dot_right_t(grad_mixed, qkv_full)
    first_value, first_pull = jax.vjp(layer_norm, inputs, gains[0], shifts[0])
    grad_in_norm, grad_gain_attn, grad_shift_attn = first_pull(grad_normed)
    grad_tokens = (grad_middle + grad_in_norm).astype(jnp.bfloat16)
    mixed_float = grad_mixed.astype(jnp.float32)
    grad_gains = jnp.stack([grad_gain_attn, grad_gain_mlp])
    grad_shifts = jnp.stack([grad_shift_attn, grad_shift_mlp])
    grad_qv = jnp.stack(
        [jnp.sum(mixed_float[:, :D], axis=0), jnp.sum(mixed_float[:, 2 * D :], axis=0)]
    )
    grad_outb = jnp.stack(
        [
            jnp.sum(grad_branch.astype(jnp.float32), axis=0),
            jnp.sum(grad_low.astype(jnp.float32), axis=0),
        ]
    )
    grad_upb = jnp.sum(grad_pre.astype(jnp.float32), axis=0)
    shards = (
        lax.psum_scatter(
            grad_gains.astype(jnp.bfloat16), "fsdp", scatter_dimension=1, tiled=True
        ).astype(jnp.float32),
        lax.psum_scatter(
            grad_shifts.astype(jnp.bfloat16), "fsdp", scatter_dimension=1, tiled=True
        ).astype(jnp.float32),
        lax.psum_scatter(
            dot_left_t(normed, grad_mixed).astype(jnp.bfloat16),
            "fsdp",
            scatter_dimension=1,
            tiled=True,
        ).astype(jnp.float32),
        lax.psum_scatter(
            grad_qv.astype(jnp.bfloat16), "fsdp", scatter_dimension=1, tiled=True
        ).astype(jnp.float32),
        lax.psum_scatter(
            dot_left_t(attended, grad_branch).astype(jnp.bfloat16),
            "fsdp",
            scatter_dimension=1,
            tiled=True,
        ).astype(jnp.float32),
        lax.psum_scatter(
            grad_outb.astype(jnp.bfloat16), "fsdp", scatter_dimension=1, tiled=True
        ).astype(jnp.float32),
        lax.psum_scatter(
            dot_left_t(normed_mlp, grad_pre).astype(jnp.bfloat16),
            "fsdp",
            scatter_dimension=1,
            tiled=True,
        ).astype(jnp.float32),
        lax.psum_scatter(
            grad_upb.astype(jnp.bfloat16), "fsdp", scatter_dimension=0, tiled=True
        ).astype(jnp.float32),
        lax.psum_scatter(
            dot_left_t(hidden, grad_low).astype(jnp.bfloat16),
            "fsdp",
            scatter_dimension=0,
            tiled=True,
        ).astype(jnp.float32),
    )
    weights_raw = counts.astype(jnp.float32)
    shares = (
        weights_raw
        / (weights_raw[0] + weights_raw[1])
        / (lax.axis_size("dp") * lax.axis_size("fsdp") // 2)
    )
    factor = jnp.where(group_id == 0, shares[0], shares[1])
    merged = lax.psum(
        (
            shards[0] * factor,
            shards[1] * factor,
            shards[2] * factor,
            shards[3] * factor,
            shards[4] * factor,
            shards[5] * factor,
            shards[6] * factor,
            shards[7] * factor,
            shards[8] * factor,
        ),
        "dp",
    )
    return (
        output,
        grad_tokens,
        merged[0],
        merged[1],
        merged[2],
        merged[3],
        merged[4],
        merged[5],
        merged[6],
        merged[7],
        merged[8],
    )


def solution(mesh):
    return jax.shard_map(
        local,
        mesh=mesh,
        in_specs=(
            P(("dp", "fsdp"), None),
            P(("dp", "fsdp"), None),
            P("dp"),
            P("dp", "fsdp"),
            P(),
            P(None, "fsdp"),
            P(None, "fsdp"),
            P(None, "fsdp"),
            P(None, "fsdp"),
            P(None, "fsdp"),
            P(None, "fsdp"),
            P(None, "fsdp"),
            P("fsdp"),
            P("fsdp", None),
        ),
        out_specs=(
            P(("dp", "fsdp"), None),
            P(("dp", "fsdp"), None),
            P(None, "fsdp"),
            P(None, "fsdp"),
            P(None, "fsdp"),
            P(None, "fsdp"),
            P(None, "fsdp"),
            P(None, "fsdp"),
            P(None, "fsdp"),
            P("fsdp"),
            P("fsdp", None),
        ),
        check_vma=False,
    )
```

profile of v0, /device:TPU:0, one launch (start us, length us, event | category | flops | bytes accessed | tf_op | source)
XLA Modules:
  0.0 1026.2 jit_solution(14400516592101816151)
XLA Ops:
  12.3 6.0 all_gather.31
  18.3 5.3 all_gather.32
  23.7 5.1 all_gather.34
  28.7 5.1 all_gather.36
  34.5 5.2 all_gather.38
  39.9 19.0 %all-gather.5.cloned.1.call-done = bf16[1024,3072]{1,0:T(8,128)(2,1)} async-done(((bf16[1024,768]{1,0:T(8,128)(2,1)}), bf16[1024,3072]{1,0:T(8,128)(2,1)}) %all-gather.5.cloned.1.call-update) | async-done | bytes 6291472 | tf_op jit(solution)/shard_map/all_gather | solution.py:135
  58.8 5.7 fusion.42
  67.9 1.9 copy.47
  69.8 2.7 copy.45
  72.5 7.5 fusion.59
  80.0 8.4 fusion
  88.4 10.0 fusion.27
  98.4 3.3 fusion.60
  103.1 40.1 %all-gather.9.cloned.1.call-done = bf16[1024,4096]{1,0:T(8,128)(2,1)} async-done(((bf16[1024,1024]{1,0:T(8,128)(2,1)}), bf16[1024,4096]{1,0:T(8,128)(2,1)}) %all-gather.9.cloned.1.call-update) | async-done | bytes 8388624 | tf_op jit(solution)/shard_map/all_gather | solution.py:156
  143.2 27.8 %multiply_convert_fusion.1 = (bf16[512,4096]{1,0:T(8,128)(2,1)}, f32[512,4096]{1,0:T(8,128)}, f32[512,4096]{1,0:T(8,128)}) fusion(f32[4096]{0:T(1024)S(1)} %convert_element_type.155, bf16[1024,4096]{1,0:T(8,128)(2,1)} %all-gather.9.cloned.1.call-done, f32[512,1024]{1,0:T(8,128)S(1)} %get-tuple-element.104, f32[1024]{0:T(1024)S(1)} %bitcast.107, ...), kind=kOutput, calls=%fused_computation.13 | convolution fusion | flops 4436000768 | bytes 31485952 | tf_op jit(solution)/shard_map/dot_general | solution.py:25
  170.9 32.0 %all-gather.11.cloned.1.call-done = bf16[4096,1024]{1,0:T(8,128)(2,1)} async-done(((bf16[1024,1024]{1,0:T(8,128)(2,1)}), bf16[4096,1024]{1,0:T(8,128)(2,1)}) %all-gather.11.cloned.1.call-update) | async-done | bytes 8388624 | tf_op jit(solution)/shard_map/all_gather | solution.py:158
  202.9 14.2 %fusion.61 = (bf16[4096]{0:T(1024)(128)(2,1)}, bf16[512,4096]{1,0:T(8,128)(2,1)S(1)}) fusion(f32[512,4096]{1,0:T(8,128)} %get-tuple-element.85, bf16[4096,1024]{1,0:T(8,128)(2,1)} %all-gather.11.cloned.1.call-done, bf16[512,1024]{1,0:T(8,128)(2,1)} %param.15, f32[512]{0:T(512)S(1)} %compare_convert_fusion, f32[512,4096]{1,0:T(8,128)} %get-tuple-element.105, ...), kind=kOutput, calls=%fused_computation.122 | convolution fusion | flops 4330090496 | bytes 30435328 | tf_op jit(solution)/shard_map/dot_general | solution.py:29
  217.1 19.4 %multiply_reduce_fusion.1 = (bf16[1024]{0:T(1024)(128)(2,1)}, f32[512]{0:T(512)S(1)}, bf16[1024]{0:T(1024)(128)(2,1)}, f32[512,1024]{1,0:T(8,128)S(1)}) fusion(f32[512,1024]{1,0:T(8,128)S(1)} %get-tuple-element.104, f32[512]{0:T(512)S(1)} %fusion.34, f32[512]{0:T(512)S(1)} %broadcast_multiply_fusion, f32[1024]{0:T(1024)S(1)} %bitcast.103, ...), kind=kOutput, calls=%fused_computation.59 | convolution fusion | flops 4299159040 | bytes 16791552 | tf_op jit(solution)/shard_map/dot_general | solution.py:29
  240.7 2.6 convolution_convert_fusion.3
  243.2 3.5 convolution_convert_fusion.4
  246.7 2.3 copy.49
  249.1 17.3 %multiply_reduce_fusion = (f32[16,512]{1,0:T(8,128)}, f32[16,512,512]{1,2,0:T(8,128)}) fusion(f32[16,512,512]{1,2,0:T(8,128)} %get-tuple-element.102, f32[16,512]{1,0:T(8,128)} %log_add_fusion, bf16[512,16,64]{0,2,1:T(8,128)(2,1)} %bitcast.71, bf16[512,16,64]{0,2,1:T(8,128)(2,1)} %bitcast.82), kind=kOutput, calls=%fused_computation.1 | convolution fusion | flops 549445632 | bytes 35717120 | tf_op jit(solution)/shard_map/while/body/eval_jaxpr/qhd,khd->hqk/dot_general | solution.py:84
  267.2 10.6 %multiply_convert_fusion = bf16[16,512,512]{1,2,0:T(8,128)(2,1)} fusion(f32[16,512,512]{1,2,0:T(8,128)} %get-tuple-element.108, f32[16,512,512]{1,2,0:T(8,128)S(1)} %bitcast.66, f32[16,512]{1,0:T(8,128)} %get-tuple-element.107, f32[16,512]{1,0:T(8,128)} %log_add_fusion), kind=kLoop, calls=%fused_computation | loop fusion | flops 16777216 | bytes 42008576 | tf_op jit(solution)/shard_map/while/body/eval_jaxpr/convert_element_type | solution.py:88
  277.9 7.1 multiply_convert_fusion.2
  285.0 5.8 multiply_convert_fusion.3
  290.9 5.0 fusion.28
  295.8 8.4 convolution_convert_fusion.2
  305.8 9.7 convolution_convert_fusion.1
  316.8 9.7 convolution_convert_fusion
  332.0 7.0 fusion.48
  344.9 2.1 convert_multiply_fusion.4
  347.0 15.8 %reduce-scatter.17.cloned.1.call-done = bf16[1024,768]{1,0:T(8,128)(2,1)} async-done(((bf16[1024,3072]{1,0:T(8,128)(2,1)}), bf16[1024,768]{1,0:T(8,128)(2,1)}) %reduce-scatter.17.cloned.1.call-update) | async-done | bytes 1572880 | tf_op jit(solution)/shard_map/reduce_scatter | solution.py:213
  362.8 3.3 convert_multiply_fusion.2
  366.1 71.1 %reduce-scatter.21.cloned.1.call-done = bf16[1024,1024]{1,0:T(8,128)(2,1)} async-done(((bf16[1024,4096]{1,0:T(8,128)(2,1)}), bf16[1024,1024]{1,0:T(8,128)(2,1)}) %reduce-scatter.21.cloned.1.call-update) | async-done | bytes 2097168 | tf_op jit(solution)/shard_map/reduce_scatter | solution.py:231
  437.1 4.2 convert_multiply_fusion.1
  441.3 70.3 %reduce-scatter.23.cloned.1.call-done = bf16[1024,1024]{1,0:T(8,128)(2,1)} async-done(((bf16[4096,1024]{1,0:T(8,128)(2,1)}), bf16[1024,1024]{1,0:T(8,128)(2,1)}) %reduce-scatter.23.cloned.1.call-update) | async-done | bytes 2097168 | tf_op jit(solution)/shard_map/reduce_scatter | solution.py:240
  511.6 4.1 convert_multiply_fusion
  517.7 5.9 all-reduce
  523.6 3.5 add_convert_fusion.1
  527.7 9.0 add_convert_fusion.2
  537.6 19.1 %reduce-scatter.25.cloned.1.call-done = bf16[256,2]{1,0:T(8,128)(2,1)} async-done(((bf16[1024,2]{1,0:T(8,128)(2,1)}), bf16[256,2]{1,0:T(8,128)(2,1)}) %reduce-scatter.25.cloned.1.call-update) | async-done | bytes 1040
  557.6 21.6 %reduce-scatter.27.cloned.1.call-done = bf16[256,2]{1,0:T(8,128)(2,1)} async-done(((bf16[1024,2]{1,0:T(8,128)(2,1)}), bf16[256,2]{1,0:T(8,128)(2,1)}) %reduce-scatter.27.cloned.1.call-update) | async-done | bytes 1040
  580.1 21.6 %reduce-scatter.29.cloned.1.call-done = bf16[256,2]{1,0:T(8,128)(2,1)} async-done(((bf16[1024,2]{1,0:T(8,128)(2,1)}), bf16[256,2]{1,0:T(8,128)(2,1)}) %reduce-scatter.29.cloned.1.call-update) | async-done | bytes 1040
  602.7 38.5 %all-reduce.1 = (f32[2,256]{1,0:T(2,128)}, f32[2,256]{1,0:T(2,128)}, f32[2,256]{1,0:T(2,128)}, f32[2,256]{1,0:T(2,128)}, f32[1024]{0:T(1024)}) all-reduce(f32[2,256]{1,0:T(2,128)S(1)} %get-tuple-element.115, f32[2,256]{1,0:T(2,128)S(1)} %get-tuple-element.114, ...), channel_id=1, replica_groups=mesh['dp'=8,'fsdp'=4] {'dp'}, use_global_device_ids=true, to_apply=%region_14.15 | all-reduce | flops 3072 | bytes 24576 | tf_op jit(solution)/shard_map/psum | solution.py:254
  641.3 367.3 %all-reduce.5.cloned.1.call-done = (f32[1024,768]{1,0:T(8,128)}, f32[1024,256]{1,0:T(8,128)}, f32[1024,1024]{1,0:T(8,128)}, f32[1024,1024]{1,0:T(8,128)}) async-done(((f32[1024,768]{1,0:T(8,128)}, f32[1024,256]{1,0:T(8,128)}, f32[1024,1024]{1,0:T(8,128)}, f32[1024,1024]{1,0:T(8,128)}), (f32[1024,768]{1,0:T(8,128)}, f32[1024,256]{1,0:T(8,128)}, f32[1024,1024]{1,0:T(8,128)}, ...) | async-done | bytes 12582928 | tf_op jit(solution)/shard_map/psum | solution.py:254
  1008.6 3.9 copy.71
  1013.5 2.1 copy.73
  1017.2 2.0 copy.74
  (209 shorter events, 33.6 us)
Async XLA Ops:
  7.2 5.1 copy-start.49
  7.2 11.1 %copy-start.50 = (bf16[2,256]{1,0:T(2,128)(2,1)S(1)}, bf16[2,256]{1,0:T(2,128)(2,1)}, u32[]{:S(2)}) copy-start(bf16[2,256]{1,0:T(2,128)(2,1)} %param.20) | copy-start | bytes 3076
  7.2 16.4 %copy-start.51 = (bf16[2,256]{1,0:T(2,128)(2,1)S(1)}, bf16[2,256]{1,0:T(2,128)(2,1)}, u32[]{:S(2)}) copy-start(bf16[2,256]{1,0:T(2,128)(2,1)} %param.22) | copy-start | bytes 3076
  7.2 21.5 %copy-start.52 = (bf16[2,256]{1,0:T(2,128)(2,1)S(1)}, bf16[2,256]{1,0:T(2,128)(2,1)}, u32[]{:S(2)}) copy-start(bf16[2,256]{1,0:T(2,128)(2,1)} %param.24) | copy-start | bytes 3076
  7.2 27.2 %copy-start.46 = (bf16[1024]{0:T(1024)(128)(2,1)S(1)}, bf16[1024]{0:T(1024)(128)(2,1)}, u32[]{:S(2)}) copy-start(bf16[1024]{0:T(1024)(128)(2,1)} %param.26) | copy-start | bytes 6148
  7.2 51.6 %all-gather.5.cloned.1.call-start = ((), (), s32[]{:S(2)}) async-start(), calls=%async_computation.8 | async-start | bytes 7864320 | tf_op jit(solution)/shard_map/all_gather | solution.py:135
  8.0 90.5 %all-gather.7.cloned.1.call-start = ((), (), s32[]{:S(2)}) async-start(), calls=%async_computation.9 | async-start | bytes 2621440 | tf_op jit(solution)/shard_map/all_gather | solution.py:137
  8.7 134.4 %all-gather.9.cloned.1.call-start = ((), (), s32[]{:S(2)}) async-start(), calls=%async_computation.10 | async-start | bytes 10485760 | tf_op jit(solution)/shard_map/all_gather | solution.py:156
  9.5 193.4 %all-gather.11.cloned.1.call-start = ((), (), s32[]{:S(2)}) async-start(), calls=%async_computation.11 | async-start | bytes 10485760 | tf_op jit(solution)/shard_map/all_gather | solution.py:158
  10.0 334.9 %reduce-scatter.19.cloned.1.call-start = ((), (), s32[]{:S(2)}) async-start(), calls=%async_computation.13 | async-start | bytes 2621440 | tf_op jit(solution)/shard_map/reduce_scatter | solution.py:222
  11.9 52.7 %copy-start.25 = (f32[512]{0:T(512)}, f32[512]{0:T(512)S(1)}, u32[]{:S(2)}) copy-start(f32[512]{0:T(512)S(1)} %broadcast_multiply_fusion.1) | copy-start | bytes 6148
  12.3 52.3 %copy-start.29 = (f32[512]{0:T(512)}, f32[512]{0:T(512)S(1)}, u32[]{:S(2)}) copy-start(f32[512]{0:T(512)S(1)} %fusion.21) | copy-start | bytes 6148
  12.3 52.3 %copy-start.31 = (f32[512]{0:T(512)}, f32[512]{0:T(512)S(1)}, u32[]{:S(2)}) copy-start(f32[512]{0:T(512)S(1)} %fusion.33) | copy-start | bytes 6148
  34.4 30.2 %copy-start.45 = (f32[1,1024]{1,0:T(1,128)}, f32[1,1024]{1,0:T(1,128)S(1)}, u32[]{:S(2)}) copy-start(f32[1,1024]{1,0:T(1,128)S(1)} %get-tuple-element.94) | copy-start | bytes 12292
  34.4 108.8 %copy-start.43 = (f32[1,1024]{1,0:T(1,128)}, f32[1,1024]{1,0:T(1,128)S(1)}, u32[]{:S(2)}) copy-start(f32[1,1024]{1,0:T(1,128)S(1)} %get-tuple-element.93) | copy-start | bytes 12292
  34.5 30.2 %copy-start.23 = (f32[1,1024]{1,0:T(1,128)}, f32[1,1024]{1,0:T(1,128)S(1)}, u32[]{:S(2)}) copy-start(f32[1,1024]{1,0:T(1,128)S(1)} %get-tuple-element.92) | copy-start | bytes 12292
  34.5 202.0 %copy-start.35 = (f32[1,1024]{1,0:T(1,128)}, f32[1,1024]{1,0:T(1,128)S(1)}, u32[]{:S(2)}) copy-start(f32[1,1024]{1,0:T(1,128)S(1)} %get-tuple-element.91) | copy-start | bytes 12292
  67.9 12.1 %copy-start.8 = (bf16[512,1024]{0,1:T(8,128)(2,1)}, bf16[512,1024]{0,1:T(8,128)(2,1)S(1)}, u32[]{:S(2)}) copy-start(bf16[512,1024]{0,1:T(8,128)(2,1)S(1)} %copy.46) | copy-start | bytes 3145732
  69.8 10.2 copy-start.6
  80.0 8.5 copy-start.14
  101.7 134.8 %copy-start.3 = (f32[512,1024]{1,0:T(8,128)}, f32[512,1024]{1,0:T(8,128)S(1)}, u32[]{:S(2)}) copy-start(f32[512,1024]{1,0:T(8,128)S(1)} %get-tuple-element.104) | copy-start | bytes 6291460
  101.7 134.8 %copy-start.33 = (f32[512]{0:T(512)}, f32[512]{0:T(512)S(1)}, u32[]{:S(2)}) copy-start(f32[512]{0:T(512)S(1)} %broadcast_multiply_fusion) | copy-start | bytes 6148
  102.1 134.4 %copy-start.39 = (f32[512]{0:T(512)}, f32[512]{0:T(512)S(1)}, u32[]{:S(2)}) copy-start(f32[512]{0:T(512)S(1)} %fusion.34) | copy-start | bytes 6148
  217.1 19.4 %copy-start.56 = (bf16[512,4096]{1,0:T(8,128)(2,1)}, bf16[512,4096]{1,0:T(8,128)(2,1)S(1)}, u32[]{:S(2)}) copy-start(bf16[512,4096]{1,0:T(8,128)(2,1)S(1)} %get-tuple-element.111) | copy-start | bytes 12582916
  249.0 113.8 %reduce-scatter.17.cloned.1.call-start = ((), (), s32[]{:S(2)}) async-start(), calls=%async_computation.12 | async-start | bytes 7864320 | tf_op jit(solution)/shard_map/reduce_scatter | solution.py:213
  249.1 17.4 %slice-start = ((s8[16777216]{0:T(1024)(128)(4,1)}), s8[4194304]{0:T(1024)(128)(4,1)S(1)}, s32[]{:S(2)}) async-start(s8[16777216]{0:T(1024)(128)(4,1)} %bitcast.65), calls=%async_computation.21 | async-start | bytes 8388608
  249.1 17.3 %slice-start.1 = ((s8[16777216]{0:T(1024)(128)(4,1)}), s8[4194304]{0:T(1024)(128)(4,1)S(1)}, s32[]{:S(2)}) async-start(s8[16777216]{0:T(1024)(128)(4,1)} %bitcast.65), calls=%async_computation.22 | async-start | bytes 8388608
  249.1 17.3 %slice-start.2 = ((s8[16777216]{0:T(1024)(128)(4,1)}), s8[4194304]{0:T(1024)(128)(4,1)S(1)}, s32[]{:S(2)}) async-start(s8[16777216]{0:T(1024)(128)(4,1)} %bitcast.65), calls=%async_computation.23 | async-start | bytes 8388608
  249.1 18.2 %slice-start.3 = ((s8[16777216]{0:T(1024)(128)(4,1)}), s8[4194304]{0:T(1024)(128)(4,1)S(1)}, s32[]{:S(2)}) async-start(s8[16777216]{0:T(1024)(128)(4,1)} %bitcast.65), calls=%async_computation.24 | async-start | bytes 8388608
  267.2 10.6 %copy-start.9 = (bf16[512,1024]{0,1:T(8,128)(2,1)S(1)}, bf16[512,1024]{0,1:T(8,128)(2,1)}, u32[]{:S(2)}) copy-start(bf16[512,1024]{0,1:T(8,128)(2,1)} %copy-done.8) | copy-start | bytes 3145732
  277.9 7.1 copy-start.7
  290.9 5.0 copy-start.24
  290.9 5.0 copy-start.26
  304.3 132.9 %reduce-scatter.21.cloned.1.call-start = ((), (), s32[]{:S(2)}) async-start(), calls=%async_computation.14 | async-start | bytes 10485760 | tf_op jit(solution)/shard_map/reduce_scatter | solution.py:231
  315.5 196.1 %reduce-scatter.23.cloned.1.call-start = ((), (), s32[]{:S(2)}) async-start(), calls=%async_computation.15 | async-start | bytes 10485760 | tf_op jit(solution)/shard_map/reduce_scatter | solution.py:240
  326.6 5.4 copy-start.11
  326.6 5.4 copy-start.12
  326.6 210.1 %reduce-scatter.31.cloned.1.call-start = ((), (), s32[]{:S(2)}) async-start(), calls=%async_computation.19 | async-start | bytes 327680
  332.0 7.0 copy-start.30
  332.0 7.1 copy-start.32
  332.0 8.1 copy-start.13
  341.4 215.3 %reduce-scatter.25.cloned.1.call-start = ((), (), s32[]{:S(2)}) async-start(), calls=%async_computation.16 | async-start | bytes 327680
  342.6 236.6 %reduce-scatter.27.cloned.1.call-start = ((), (), s32[]{:S(2)}) async-start(), calls=%async_computation.17 | async-start | bytes 327680
  343.6 258.2 %reduce-scatter.29.cloned.1.call-start = ((), (), s32[]{:S(2)}) async-start(), calls=%async_computation.18 | async-start | bytes 327680
  344.6 664.0 %all-reduce.5.cloned.1.call-start = ((), (), s32[]{:S(2)}) async-start(), calls=%async_computation.20 | async-start | bytes 25165824 | tf_op jit(solution)/shard_map/psum | solution.py:254
  515.8 7.8 copy-start.2
  515.8 7.8 copy-start.28
  515.8 11.3 %copy-start.42 = (f32[1,1024]{1,0:T(1,128)S(1)}, f32[1,1024]{1,0:T(1,128)}, u32[]{:S(2)}) copy-start(f32[1,1024]{1,0:T(1,128)} %get-tuple-element.89) | copy-start | bytes 12292
  (26 other events, 66.8 us)
Sparse Core Ops, SparseCore 0:
  9.6 49.1 all-gather.4
  60.4 22.8 all-gather.6
  84.8 58.2 all-gather.8
  144.6 58.2 all-gather.10
  249.1 31.4 reduce-scatter.18
  304.4 58.3 reduce-scatter.16
  365.4 71.7 reduce-scatter.20
  439.9 71.6 reduce-scatter.22
  514.1 20.0 reduce-scatter.30
  536.6 20.0 reduce-scatter.24
  559.2 20.0 reduce-scatter.26
  581.7 20.0 reduce-scatter.28
  607.7 400.8 all-reduce.4
where the time goes:
time: 1040 us; the launch traced here: 1030 us
  waiting for transfers between devices  681 us (65%)
  matrix products  173 us (17%)
  blocking collectives  71 us (7%)
  other arithmetic  44.5 us (4%)
  local copies, waits for them, and re-layouts  36.7 us (4%)
  between operations  19.6 us (2%)
    psum x1, waiting for transfers between devices, local(): lax.psum((shards[0] * factor, shards[1] * factor, shards[2] * factor, sha...  367 us
    reduce_scatter x1, waiting for transfers between devices, local(): lax.psum_scatter(dot_left_t(normed_mlp, grad_pre).astype(jnp.bfloat16), '...  71.1 us
    reduce_scatter x1, waiting for transfers between devices, local(): lax.psum_scatter(dot_left_t(hidden, grad_low).astype(jnp.bfloat16), 'fsdp...  70.3 us
    unnamed x17, waiting for transfers between devices  65.1 us
    dot_general x4, matrix products, dot_plain(): return jnp.dot(first_op, second_op, preferred_element_type=jnp.float32)  45.8 us
    dot_general x4, matrix products, dot_right_t(): lax.dot_general(first_op, second_op, (((1,), (1,)), ((), ())), preferred_...  44 us
    all_gather x1, waiting for transfers between devices, local(): lax.all_gather(w_up, 'fsdp', axis=1, tiled=True)  40.1 us
    psum x1, blocking collectives, local(): lax.psum((shards[0] * factor, shards[1] * factor, shards[2] * factor, sha...  38.5 us
  transfers between devices with their start and end apart: 13, of which 10 were waited for; matrix products, arithmetic and copies ran while one was open for 19% of the time, Pallas kernels for 0%

commit v1 on v0

v1 whole, which is shorter than its diff:
```python
import functools

import jax
import jax.numpy as jnp
from jax import lax
from jax.experimental import pallas as pl
from jax.experimental.pallas import tpu as pltpu
from jax.sharding import PartitionSpec as P

D = 1024
HEADS = 16
HDIM = 64
LEN0 = 50
LEN1 = 145
EPSILON = 1e-06
WIDE = 1024
F32 = jnp.float32
BF16 = jnp.bfloat16
MESH = pl.DeviceIdType.MESH


def layer_norm(inputs, gain_row, shift_row):
    center = inputs - jnp.mean(inputs, axis=-1, keepdims=True)
    spread = jnp.mean(center * center, axis=-1, keepdims=True)
    return center * lax.rsqrt(spread + EPSILON) * gain_row + shift_row


def dot_plain(first_op, second_op):
    return jnp.dot(first_op, second_op, preferred_element_type=jnp.float32)


def segment_ids(group_id, image_count, row_count):
    length = jnp.where(group_id == 0, LEN0, LEN1).astype(jnp.int32)
    position = jnp.arange(row_count, dtype=jnp.int32)
    image_index = position // length
    in_image = image_index < image_count
    return (jnp.where(in_image, image_index, row_count), in_image)


def block_scores(query_part, key_rows, segment_part, segment):
    scores = jnp.einsum(
        "qhd,khd->hqk", query_part, key_rows, preferred_element_type=jnp.float32
    ) * HDIM ** (-0.5)
    allowed = segment_part[:, None] == segment[None, :]
    return jnp.where(allowed[None], scores, -1e30)


def split_plan(chunk_rows, bit_count):
    rows, cols, plan = chunk_rows, WIDE, []
    for _ in range(bit_count):
        if rows >= 32:
            rows //= 2
            plan.append(("rows", rows, cols))
        else:
            cols //= 2
            plan.append(("cols", rows, cols))
    return plan


def reduce_scratch(chunk_rows, bit_count):
    plan = split_plan(chunk_rows, bit_count)
    return [
        pltpu.VMEM((2, 2, chunk_rows, WIDE), BF16),
        pltpu.VMEM((2, 2, chunk_rows, WIDE), BF16),
        pltpu.VMEM((4, chunk_rows, WIDE), BF16),
        pltpu.VMEM((4, chunk_rows, WIDE), BF16),
        pltpu.VMEM((16, chunk_rows, WIDE), BF16),
        [pltpu.VMEM((4, r, c), BF16) for _, r, c in plan],
        pltpu.SemaphoreType.DMA((2, 2)),
        pltpu.SemaphoreType.DMA((2, 2)),
        pltpu.SemaphoreType.DMA((2, 4)),
        pltpu.SemaphoreType.DMA((bit_count, 2, 4)),
        pltpu.SemaphoreType.DMA((bit_count, 2, 4)),
    ]


def greet(peers):
    barrier = pltpu.get_barrier_semaphore()
    for peer in peers:
        pl.semaphore_signal(barrier, inc=1, device_id=peer, device_id_type=MESH)
    pl.semaphore_wait(barrier, len(peers))


def reduction(chunk_rows, chunk_count, bit_count, g_ref, out_ref, load, core_in, x_out, x_in, acc, bit_in,
              local_sem, core_sem, x_sem, bit_sem, ag_sem):
    dp, f = lax.axis_index("dp"), lax.axis_index("fsdp")
    core, across = lax.rem(f, 2), f // 2
    plan = split_plan(chunk_rows, bit_count)
    bits = [lax.rem(dp // (1 << b), 2) for b in range(bit_count)]
    flips = [dp + (1 - 2 * bits[b]) * (1 << b) for b in range(bit_count)]
    core_peer = (dp, f + 1 - 2 * core)
    x_peer = (dp, f + 2 - 4 * across)
    peers = [core_peer, x_peer] + [(p, f) for p in flips]

    def region(level, other):
        row, col, rows, cols = 0, 0, chunk_rows, WIDE
        for b in range(level):
            kind, rows, cols = plan[b]
            bit = 1 - bits[b] if other and b == level - 1 else bits[b]
            if kind == "rows":
                row = row + bit * rows
            else:
                col = col + bit * cols
        return row, rows, col, cols

    def cut(ref, lead, base, level, other):
        row, rows, col, cols = region(level, other)
        row_slice = pl.ds(pl.multiple_of(base + row, 16), rows)
        col_slice = slice(None) if cols == WIDE else pl.ds(pl.multiple_of(col, 128), cols)
        return ref.at[lead + (row_slice, col_slice)]

    def rows_of(j):
        return pl.ds(pl.multiple_of(j * chunk_rows, chunk_rows), chunk_rows)

    def remote(src, dst, sems, slot, peer):
        return pltpu.make_async_remote_copy(src, dst, sems.at[0, slot], sems.at[1, slot], device_id=peer,
                                            device_id_type=MESH)

    def load_copy(j):
        return pltpu.make_async_copy(g_ref.at[core, :, rows_of(j), :], load.at[lax.rem(j, 2)],
                                     local_sem.at[0, lax.rem(j, 2)])

    def core_copy(j):
        s = lax.rem(j, 2)
        return remote(g_ref.at[1 - core, :, rows_of(j), :], core_in.at[s], core_sem, s, core_peer)

    def x_copy(j):
        s = lax.rem(j, 4)
        return remote(x_out.at[s], x_in.at[s], x_sem, s, x_peer)

    def bit_copy(b, j):
        s = lax.rem(j, 4)
        return remote(cut(acc, (lax.rem(j, 16),), 0, b + 1, True), bit_in[b].at[s], bit_sem.at[b], s, (flips[b], f))

    def own_copy(j):
        return pltpu.make_async_copy(cut(acc, (lax.rem(j, 16),), 0, bit_count, False),
                                     cut(out_ref, (), j * chunk_rows, bit_count, False),
                                     local_sem.at[1, lax.rem(j, 2)])

    def ag_copy(b, j):
        mine = cut(out_ref, (), j * chunk_rows, b + 1, False)
        src = cut(acc, (lax.rem(j, 16),), 0, bit_count, False) if b == bit_count - 1 else mine
        return remote(src, mine, ag_sem.at[b], lax.rem(j, 4), (flips[b], f))

    skews = [2 if b < 1 else 1 for b in range(bit_count)]
    when_core, when_x = 1, 3
    when_bits, now = [], when_x
    for b in range(bit_count):
        now += skews[b]
        when_bits.append(now)
    when_ag = [0] * bit_count
    for b in reversed(range(bit_count)):
        now += skews[b]
        when_ag[b] = now

    def guarded(t, delay, action):
        j = t - delay

        @pl.when(jnp.logical_and(j >= 0, j < chunk_count))
        def _():
            action(j)

    def on_ag(b):
        def action(j):
            if b == bit_count - 1:
                own_copy(j).wait()
            ag_copy(b, j).wait()
            if b > 0:
                ag_copy(b - 1, j).start()
        return action

    def on_bit(b):
        def action(j):
            bit_copy(b, j).wait()
            mine = cut(acc, (lax.rem(j, 16),), 0, b + 1, False)
            mine[...] = (mine[...].astype(F32) + bit_in[b][lax.rem(j, 4)].astype(F32)).astype(BF16)
            if b + 1 < bit_count:
                bit_copy(b + 1, j).start()
            else:
                ag_copy(b, j).start()
                own_copy(j).start()
        return action

    def on_x(j):
        x_copy(j).wait()
        s = lax.rem(j, 16)
        acc[s] = (acc[s].astype(F32) + x_in[lax.rem(j, 4)].astype(F32)).astype(BF16)
        bit_copy(0, j).start()

    def on_core(j):
        load_copy(j).wait()
        core_copy(j).wait()
        s = lax.rem(j, 2)
        for piece, target in ((1 - across, x_out.at[lax.rem(j, 4)]), (across, acc.at[lax.rem(j, 16)])):
            target[...] = (load[s, piece].astype(F32) + core_in[s, piece].astype(F32)).astype(BF16)
        x_copy(j).start()

    def on_start(j):
        load_copy(j).start()
        core_copy(j).start()

    def tick(t):
        for b in range(bit_count):
            guarded(t, when_ag[b], on_ag(b))
        for b in reversed(range(bit_count)):
            guarded(t, when_bits[b], on_bit(b))
        guarded(t, when_x, on_x)
        guarded(t, when_core, on_core)
        guarded(t, 0, on_start)

    return tick, chunk_count + now, peers


def dot_nn(a, b):
    return lax.dot_general(a, b, (((1,), (0,)), ((), ())), preferred_element_type=F32)


def dot_nt(a, b):
    return lax.dot_general(a, b, (((1,), (1,)), ((), ())), preferred_element_type=F32)


def dot_tn(a, b):
    return lax.dot_general(a, b, (((0,), (0,)), ((), ())), preferred_element_type=F32)


def lanes(index, width):
    return pl.ds(pl.multiple_of(index * width, width), width)


def half_mask(shape, dim, half):
    spot = lax.broadcasted_iota(jnp.int32, shape, dim)
    return spot < HDIM if half == 0 else spot >= HDIM


def backward_kernel(rows, chunk_rows, chunk_count, bit_count, factor_ref, cot_hbm, live_hbm, bias_hbm, z_hbm, slope_hbm, h2_hbm,
                    x1_hbm, o_hbm, qkv_hbm, lse_hbm, h1_hbm, x_hbm, gains_hbm, wd_hbm, wu_hbm, wqkv_hbm, wo_hbm,
                    out_ref, gtok_ref, g_ref,
                    dy, live, bias, h2, x1, o, qkv, lse, h1, x, gains, wqkv, wo,
                    z_tile, slope_tile, wd_tile, wu_tile, stage, du_low,
                    dh, dx1, da, do, dp_all, vecs, upb, tail, load_sem, tile_sem, stage_sem, gtok_sem, comm):
    tick, tick_count, peers = reduction(chunk_rows, chunk_count, bit_count, g_ref, out_ref, *comm)
    proj_tick = min(29, 2048 // chunk_rows - 1)

    def tile_copies(n):
        s, q, f = lax.rem(n, 2), n // 4, lax.rem(n, 4)
        return [
            pltpu.make_async_copy(z_hbm.at[n], z_tile.at[s], tile_sem.at[0, s]),
            pltpu.make_async_copy(slope_hbm.at[n], slope_tile.at[s], tile_sem.at[1, s]),
            pltpu.make_async_copy(wd_hbm.at[f, lanes(q, 256), :], wd_tile.at[s], tile_sem.at[2, s]),
            pltpu.make_async_copy(wu_hbm.at[f, :, lanes(q, 256)], wu_tile.at[s], tile_sem.at[3, s]),
        ]

    whole = [(cot_hbm, dy), (live_hbm, live), (h2_hbm, h2), (x1_hbm, x1), (gains_hbm, gains), (wo_hbm, wo), (bias_hbm, bias),
             (o_hbm, o), (qkv_hbm, qkv), (lse_hbm, lse), (h1_hbm, h1), (wqkv_hbm, wqkv), (x_hbm, x)]

    def whole_copy(i):
        return pltpu.make_async_copy(whole[i][0], whole[i][1], load_sem.at[i])

    for i in range(3):
        whole_copy(i).start()
    for copy in tile_copies(0):
        copy.start()
    for i in range(3, len(whole)):
        whole_copy(i).start()
    greet(peers)
    factor = factor_ref[0]
    for i in range(3):
        whole_copy(i).wait()
    dy[...] = (dy[...].astype(F32) * live[...]).astype(BF16)
    dh[...] = jnp.zeros_like(dh)

    def stage_copy(which, n):
        s, q, f = lax.rem(n, 2), n // 4, lax.rem(n, 4)
        if which == 2:
            row = pl.ds(pl.multiple_of(2048 + q * 256, 256), 256)
        else:
            row = pl.ds(pl.multiple_of(q * 512 + which * 256, 256), 256)
        return pltpu.make_async_copy(stage.at[which, s], g_ref.at[lax.rem(f, 2), f // 2, row, :], stage_sem.at[which, s])

    def ffn(n, carry):
        s = lax.rem(n, 2)

        @pl.when(n + 1 < 16)
        def _():
            for copy in tile_copies(n + 1):
                copy.start()

        for copy in tile_copies(n):
            copy.wait()

        @pl.when(n >= 2)
        def _():
            for which in (0, 1):
                stage_copy(which, n - 2).wait()

        @pl.when(n >= 6)
        def _():
            tick(n - 6)

        stage[0, s] = (dot_tn(z_tile[s], dy[...]) * factor).astype(BF16)
        stage_copy(0, n).start()
        du = dot_nt(dy[...], wd_tile[s]) * slope_tile[s].astype(F32)
        low = du.astype(BF16)
        du_low[...] = low
        upb[n] = jnp.sum(low.astype(F32), axis=0, keepdims=True)
        stage[1, s] = (dot_tn(low, h2[...]) * factor).astype(BF16)
        stage_copy(1, n).start()
        dh[...] += dot_nt(du_low[...], wu_tile[s])
        return carry

    lax.fori_loop(0, 16, ffn, 0)
    for n in (14, 15):
        for which in (0, 1):
            stage_copy(which, n).wait()
    tick(10)

    for i in (3, 4):
        whole_copy(i).wait()
    vecs[...] = jnp.zeros_like(vecs)
    step = 64

    def norm_back(base_ref, which, finish):
        def body(i, carry):
            part = pl.ds(pl.multiple_of(i * step, step), step)
            v = base_ref[part, :].astype(F32)
            center = v - jnp.mean(v, axis=-1, keepdims=True)
            rstd = lax.rsqrt(jnp.mean(center * center, axis=-1, keepdims=True) + EPSILON)
            hat = center * rstd
            grad = dh[part, :]
            vecs[which] += jnp.sum(grad * hat, axis=0, keepdims=True)
            vecs[2 + which] += jnp.sum(grad, axis=0, keepdims=True)
            scaled = grad * gains[which]
            finish(part, rstd * (scaled - jnp.mean(scaled, axis=-1, keepdims=True)
                                 - hat * jnp.mean(scaled * hat, axis=-1, keepdims=True)))
            return carry

        lax.fori_loop(0, rows // step, body, 0)

    def finish_mlp(part, dx):
        dy_part = dy[part, :].astype(F32)
        full = dy_part + dx
        low = full.astype(BF16)
        dx1[part, :] = full
        da[part, :] = low
        vecs[6] += jnp.sum(low.astype(F32), axis=0, keepdims=True)
        vecs[7] += jnp.sum(dy_part, axis=0, keepdims=True)

    norm_back(x1, 1, finish_mlp)
    tick(11)

    whole_copy(5).wait()
    for c in range(4):
        total = jnp.zeros((rows, 256), F32)
        for f in range(4):
            total += dot_nt(da[:, 256 * f : 256 * f + 256], wo[f, 256 * c : 256 * c + 256, :])
        low = total.astype(BF16)
        do[2 * c] = low[:, :128]
        do[2 * c + 1] = low[:, 128:]
    tick(12)
    for i in range(6, 10):
        whole_copy(i).wait()

    def heads(p, carry):
        q_pair, k_pair, v_pair, do_pair = qkv[p], qkv[8 + p], qkv[16 + p], do[p]
        k_turned = k_pair.T
        dk = jnp.zeros((rows, 128), F32)
        dv = jnp.zeros((rows, 128), F32)
        dq = jnp.zeros((128, rows), F32)
        for half in range(2):
            @pl.when(13 + 2 * p + half < proj_tick)
            def _():
                tick(13 + 2 * p + half)

            mask = half_mask((rows, 128), 1, half)
            q_half = jnp.where(mask, q_pair, jnp.zeros_like(q_pair))
            do_half = jnp.where(mask, do_pair, jnp.zeros_like(do_pair))
            k_half = jnp.where(half_mask((128, rows), 0, half), k_turned, jnp.zeros_like(k_turned))
            scores = dot_nt(k_pair, q_half) + bias[...]
            weights = jnp.exp(scores - lse[p, half])
            grad = dot_nt(v_pair, do_half)
            inner = jnp.sum(weights * grad, axis=0, keepdims=True)
            low = weights.astype(BF16)
            ds = (weights * (grad - inner)).astype(BF16)
            dv += dot_nn(low, do_half)
            dk += dot_nn(ds, q_half)
            dq += dot_nn(k_half, ds)
        for i, value in ((0, dq.T * HDIM ** (-0.5)), (1, dk), (2, dv)):
            low = value.astype(BF16)
            dp_all[:, lanes(8 * i + p, 128)] = low
            if i != 1:
                vecs[4 + i // 2, :, lanes(p, 128)] = jnp.sum(low.astype(F32), axis=0, keepdims=True)
        return carry

    lax.fori_loop(0, 8, heads, 0)

    whole_copy(10).wait()

    def proj(n, carry):
        s, q, f = lax.rem(n, 2), n // 4, lax.rem(n, 4)

        @pl.when(n >= 2)
        def _():
            stage_copy(2, n - 2).wait()

        stage[2, s, :, 0:768] = (dot_tn(h1[:, lanes(q, 256)], dp_all[:, lanes(f, 768)]) * factor).astype(BF16)
        stage[2, s, :, 768:1024] = (dot_tn(o[:, lanes(q, 256)], da[:, lanes(f, 256)]) * factor).astype(BF16)
        stage_copy(2, n).start()

        @pl.when(lax.rem(n, 4) == 3)
        def _():
            tick(proj_tick + n // 4)

        return carry

    lax.fori_loop(0, 16, proj, 0)
    for n in (14, 15):
        stage_copy(2, n).wait()

    whole_copy(11).wait()
    whole_copy(12).wait()
    for c in range(4):
        total = jnp.zeros((rows, 256), F32)
        for f in range(4):
            total += dot_nt(dp_all[:, 768 * f : 768 * f + 768], wqkv[f, 256 * c : 256 * c + 256, :])
        dh[:, 256 * c : 256 * c + 256] = total
        tick(proj_tick + 4 + c)

    def finish_attn(part, dx):
        x[part, :] = (dx1[part, :] + dx).astype(BF16)

    norm_back(x, 0, finish_attn)
    gtok_copy = pltpu.make_async_copy(x, gtok_ref, gtok_sem.at[0])
    gtok_copy.start()
    for f in range(4):
        tail[f] = jnp.zeros((chunk_rows, WIDE), BF16)
        for i in range(8):
            tail[f, 2 * i : 2 * i + 1, 0:256] = (vecs[i, :, 256 * f : 256 * f + 256] * factor).astype(BF16)
        for q in range(4):
            tail[f, 16:17, 256 * q : 256 * q + 256] = (upb[4 * q + f] * factor).astype(BF16)
    tail_copies = [pltpu.make_async_copy(tail.at[f], g_ref.at[f % 2, f // 2, pl.ds(3072, chunk_rows), :], gtok_sem.at[1 + f])
                   for f in range(4)]
    for copy in tail_copies:
        copy.start()
    for copy in tail_copies:
        copy.wait()

    def rest(t, carry):
        tick(t)
        return carry

    lax.fori_loop(proj_tick + 8, tick_count, rest, 0)
    gtok_copy.wait()


def backward(factor, cot, live, bias, z, slope, h2, x1, o, qkv, lse, h1, x, gains, wd, wu, wqkv, wo, dp_size):
    rows = cot.shape[0]
    chunk_rows = 64 if dp_size <= 32 else 128
    chunk_count = 3072 // chunk_rows + 1
    bit_count = dp_size.bit_length() - 1
    any_space = pl.BlockSpec(memory_space=pl.ANY)
    like = lambda a: pltpu.VMEM(a.shape, a.dtype)
    scratch = [like(a) for a in (cot, live, bias, h2, x1, o, qkv, lse, h1, x, gains, wqkv, wo)] + [
        pltpu.VMEM((2, rows, 256), BF16),
        pltpu.VMEM((2, rows, 256), BF16),
        pltpu.VMEM((2, 256, D), BF16),
        pltpu.VMEM((2, D, 256), BF16),
        pltpu.VMEM((3, 2, 256, WIDE), BF16),
        pltpu.VMEM((rows, 256), BF16),
        pltpu.VMEM((rows, D), F32),
        pltpu.VMEM((rows, D), F32),
        pltpu.VMEM((rows, D), BF16),
        pltpu.VMEM((8, rows, 128), BF16),
        pltpu.VMEM((rows, 3 * D), BF16),
        pltpu.VMEM((8, 1, D), F32),
        pltpu.VMEM((16, 1, 256), F32),
        pltpu.VMEM((4, chunk_rows, WIDE), BF16),
        pltpu.SemaphoreType.DMA((13,)),
        pltpu.SemaphoreType.DMA((4, 2)),
        pltpu.SemaphoreType.DMA((3, 2)),
        pltpu.SemaphoreType.DMA((5,)),
        reduce_scratch(chunk_rows, bit_count),
    ]
    g_rows = 3072 + chunk_rows
    return pl.pallas_call(
        functools.partial(backward_kernel, rows, chunk_rows, chunk_count, bit_count),
        out_shape=(
            jax.ShapeDtypeStruct((g_rows, WIDE), BF16),
            jax.ShapeDtypeStruct((rows, D), BF16),
            jax.ShapeDtypeStruct((2, 2, g_rows, WIDE), BF16),
        ),
        in_specs=[pl.BlockSpec(memory_space=pltpu.SMEM)] + [any_space] * 17,
        out_specs=(any_space, any_space, any_space),
        scratch_shapes=scratch,
        compiler_params=pltpu.CompilerParams(collective_id=1, has_side_effects=True, vmem_limit_bytes=60 * 2**20),
        name="backward",
    )(factor, cot, live, bias, z, slope, h2, x1, o, qkv, lse, h1, x, gains, wd, wu, wqkv, wo)


def local(
    tokens,
    cotangent,
    group,
    images,
    counts,
    ln_gain,
    ln_bias,
    w_qkv,
    qv_bias,
    w_out,
    out_bias,
    w_up,
    up_bias,
    w_down,
):
    rows = tokens.shape[0]
    group_id = group[0]
    segment, in_image = segment_ids(group_id, images[0, 0], rows)
    gather = lambda a: lax.all_gather(a, "fsdp", axis=0)
    vec = gather(jnp.concatenate([ln_gain, ln_bias, qv_bias, out_bias, up_bias.reshape(4, 256)], axis=0)).astype(F32)
    pick = lambda i: vec[:, i].reshape(D)
    wqkv, wo, wu, wd = gather(w_qkv), gather(w_out), gather(w_up), gather(w_down)
    flat = lambda w: w.transpose(1, 0, 2).reshape(D, -1)
    x = tokens.astype(F32)
    h1 = layer_norm(x, pick(0), pick(2)).astype(BF16)
    projected = dot_plain(h1, flat(wqkv))
    q = (projected[:, :D] + pick(4)).astype(BF16)
    k = projected[:, D : 2 * D].astype(BF16)
    v = (projected[:, 2 * D :] + pick(5)).astype(BF16)
    split = lambda a: a.reshape(rows, HEADS, HDIM)
    scores = block_scores(split(q), split(k), segment, segment)
    highest = jnp.max(scores, axis=-1, keepdims=True)
    weights = jnp.exp(scores - highest)
    totals = jnp.sum(weights, axis=-1, keepdims=True)
    o = jnp.einsum("hqk,khd->qhd", (weights / totals).astype(BF16), split(v), preferred_element_type=F32)
    o = o.reshape(rows, D).astype(BF16)
    lse = (highest + jnp.log(totals))[..., 0]
    x1 = x + dot_plain(o, flat(wo)) + pick(6)
    h2 = layer_norm(x1, pick(1), pick(3)).astype(BF16)
    u = dot_plain(h2, flat(wu)) + vec[:, 8:].reshape(-1)
    gelu, pull = jax.vjp(functools.partial(jax.nn.gelu, approximate=False), u)
    z = gelu.astype(BF16)
    slope = pull(jnp.ones_like(u))[0].astype(BF16)
    output = (x1 + dot_plain(z, wd.reshape(-1, D)) + pick(7)).astype(BF16)
    tile = lambda a: a.reshape(rows, 4, 4, 256).transpose(2, 1, 0, 3).reshape(16, rows, 256)
    qkv = jnp.concatenate([q * HDIM ** (-0.5), k, v], axis=1).astype(BF16).reshape(rows, 24, 128).transpose(1, 0, 2)
    bias = jnp.where(segment[:, None] == segment[None, :], 0.0, -1e30).astype(F32)
    weights_raw = counts.astype(F32)
    shares = weights_raw / (weights_raw[0] + weights_raw[1]) / (lax.axis_size("dp") * lax.axis_size("fsdp") // 2)
    factor = jnp.where(group_id == 0, shares[0], shares[1])
    total, grad_tokens, _ = backward(
        factor.reshape(1), cotangent, in_image[:, None].astype(F32), bias, tile(z), tile(slope), h2, x1, o, qkv,
        lse.reshape(8, 2, 1, rows), h1, tokens, jnp.stack([pick(0), pick(1)])[:, None, :], wd, wu, wqkv, wo,
        lax.axis_size("dp"))
    total = total.astype(F32)
    blocks = total[:2048].reshape(4, 2, 256, D)
    small = total[3072:3089]
    return (
        output, grad_tokens, small[0:4:2, :256], small[4:8:2, :256], total[2048:3072, :768], small[8:12:2, :256],
        total[2048:3072, 768:], small[12:16:2, :256], blocks[:, 1].reshape(D, D).T, small[16], blocks[:, 0].reshape(D, D),
    )


def solution(mesh):
    return jax.shard_map(
        local,
        mesh=mesh,
        in_specs=(
            P(("dp", "fsdp"), None),
            P(("dp", "fsdp"), None),
            P("dp"),
            P("dp", "fsdp"),
            P(),
            P(None, "fsdp"),
            P(None, "fsdp"),
            P(None, "fsdp"),
            P(None, "fsdp"),
            P(None, "fsdp"),
            P(None, "fsdp"),
            P(None, "fsdp"),
            P("fsdp"),
            P("fsdp", None),
        ),
        out_specs=(
            P(("dp", "fsdp"), None),
            P(("dp", "fsdp"), None),
            P(None, "fsdp"),
            P(None, "fsdp"),
            P(None, "fsdp"),
            P(None, "fsdp"),
            P(None, "fsdp"),
            P(None, "fsdp"),
            P(None, "fsdp"),
            P("fsdp"),
            P("fsdp", None),
        ),
        check_vma=False,
    )
```

time: 1040 us -> 510 us (0.49)
  waiting for transfers between devices: 681 us -> 49.6 us
  Pallas kernels: 0 us -> 238 us
  matrix products: 173 us -> 65.8 us
  blocking collectives: 71 us -> 6.16 us
  local copies, waits for them, and re-layouts: 36.7 us -> 95.4 us
  other arithmetic: 44.5 us -> 31.1 us
    psum x1 -> x0, waiting for transfers between devices: 367 us -> none  [local(): lax.psum((shards[0] * factor, shards[1] * factor, shards[2] * factor, sha...]
    pallas_call x0 -> x1, Pallas kernels: none -> 238 us  [backward(): pl.pallas_call(functools.partial(backward_kernel, rows, chunk_rows, chunk...]
    reduce_scatter x4 -> x0, waiting for transfers between devices: 157 us -> none  [the longest x1 71.1 us: local(): lax.psum_scatter(dot_left_t(normed_mlp, grad_pre).astype(jnp.bfloat16), '...]
    dot_general x13 -> x1, matrix products: 120 us -> 9.34 us  [local(): jnp.einsum('hqk,khd->qhd', (weights / totals).astype(BF16), split(v), pre...]
    unnamed x17 -> x4, waiting for transfers between devices: 65.1 us -> 2.58 us
    all_gather x4, waiting for transfers between devices: 91 us -> 47 us  [local(): gather = lambda a: lax.all_gather(a, 'fsdp', axis=0)]
    psum x1 -> x0, blocking collectives: 38.5 us -> none  [local(): lax.psum((shards[0] * factor, shards[1] * factor, shards[2] * factor, sha...]
    reshape x4 -> x6, local copies, waits for them, and re-layouts: 0.02 us -> 32.6 us  [the longest x4 27.3 us: local(): a.reshape(rows, 4, 4, 256).transpose(2, 1, 0, 3).reshape(16, rows, 256)]
  transfers between devices with their start and end apart: 13 -> 4, of which waited for: 10 -> 2; matrix products, arithmetic and copies ran while one was open for 19% -> 32% of each run, Pallas kernels for 0% -> 0%
where the time goes in v1:
time: 510 us; the launch traced here: 504 us
  Pallas kernels  238 us (47%)
  local copies, waits for them, and re-layouts  95.4 us (19%)
  matrix products  65.8 us (13%)
  waiting for transfers between devices  49.6 us (10%)
  other arithmetic  31.1 us (6%)
  between operations  18.3 us (4%)
  blocking collectives  6.16 us (1%)
    pallas_call x1, Pallas kernels, backward(): pl.pallas_call(functools.partial(backward_kernel, rows, chunk_rows, chunk...  238 us
    all_gather x4, waiting for transfers between devices, local(): gather = lambda a: lax.all_gather(a, 'fsdp', axis=0)  47 us
    dot_general x4, matrix products, dot_plain(): return jnp.dot(first_op, second_op, preferred_element_type=jnp.float32)  46.6 us
    reshape x4, local copies, waits for them, and re-layouts, local(): a.reshape(rows, 4, 4, 256).transpose(2, 1, 0, 3).reshape(16, rows, 256)  27.3 us
    transpose x3, local copies, waits for them, and re-layouts, local(): flat = lambda w: w.transpose(1, 0, 2).reshape(D, -1)  25.7 us
  transfers between devices with their start and end apart: 4, of which 2 were waited for; matrix products, arithmetic and copies ran while one was open for 32% of the time, Pallas kernels for 0%

profile of v1, /device:TPU:0, one launch (start us, length us, event | category | flops | bytes accessed | tf_op | source)
XLA Modules:
  0.0 504.3 jit_solution(7041625917458229017)
XLA Ops:
  7.2 0.7 all-gather.13.cloned.1.call-update
  8.0 0.7 all-gather.11.cloned.1.call-update
  8.7 0.7 all-gather.15.cloned.1.call-update
  10.0 0.7 reshape.223
  10.7 0.8 concatenate.6
  11.4 6.2 %all-gather.5 = bf16[4,12,256]{2,1,0:T(8,128)(2,1)S(1)} all-gather(bf16[1,12,256]{2,1,0:T(8,128)(2,1)S(1)} %bitcast.91), channel_id=2, replica_groups=mesh['dp'=8,'fsdp'=4] {'fsdp'}, dimensions={0}, use_global_device_ids=true | all-gather | bytes 30720 | tf_op jit(solution)/shard_map/all_gather | solution.py:518
  17.6 0.6 fusion.28
  19.9 1.1 broadcast_select_fusion.bias_hbm
  21.0 0.7 convert_element_type.59
  23.6 0.7 divide_multiply_fusion
  25.5 0.6 broadcast_in_dim.44.gains_hbm
  26.1 3.3 fusion.20.live_hbm
  31.5 3.4 all-gather.13.cloned.1.call-done
  34.9 4.4 copy.54
  39.3 43.6 %all-gather.11.cloned.1.call-done = bf16[4096,768]{1,0:T(8,128)(2,1)} async-done(((bf16[1024,768]{1,0:T(8,128)(2,1)}), bf16[4096,768]{1,0:T(8,128)(2,1)}) %all-gather.11.cloned.1.call-update) | async-done | bytes 6291472 | tf_op jit(solution)/shard_map/all_gather | solution.py:518
  82.9 8.7 %copy.48 = bf16[1024,4,768]{0,2,1:T(8,128)(2,1)} copy(bf16[1024,4,768]{2,0,1:T(8,128)(2,1)} %bitcast.65) | data formatting | bytes 12582912 | tf_op jit(solution)/shard_map/transpose | solution.py:522
  91.6 6.1 %fusion.32 = f32[512,3072]{1,0:T(8,128)S(1)} fusion(bf16[512,1024]{1,0:T(8,128)(2,1)S(1)} %fusion.14.h1_hbm, bf16[1024,3072]{0,1:T(8,128)(2,1)} %bitcast.76), kind=kOutput, calls=%fused_computation.72 | convolution fusion | flops 3221225472 | bytes 13631488 | tf_op jit(solution)/shard_map/dot_general | solution.py:29
  97.9 1.9 broadcast_multiply_fusion
  99.8 2.3 copy.51
  102.1 1.3 copy.52
  103.4 1.3 copy.49
  104.7 9.9 %fusion = (f32[16,512]{1,0:T(8,128)S(1)}, f32[16,512,512]{1,2,0:T(8,128)}) fusion(pred[512,512]{0,1:T(8,128)(4,1)S(1)} %copy.50, bf16[512,16,64]{0,2,1:T(8,128)(2,1)} %bitcast.77, bf16[512,16,64]{0,2,1:T(8,128)(2,1)} %bitcast.78), kind=kOutput, calls=%fused_computation.3 | convolution fusion | flops 549445632 | bytes 19169280 | tf_op jit(solution)/shard_map/qhd,khd->hqk/dot_general | solution.py:41
  114.6 9.3 %fusion.1 = f32[16,512]{1,0:T(8,128)S(1)} fusion(f32[16,512,512]{1,2,0:T(8,128)} %get-tuple-element.35, f32[16,512]{1,0:T(8,128)S(1)} %get-tuple-element.34, pred[512,512]{0,1:T(8,128)(4,1)S(1)} %copy.50), kind=kLoop, calls=%fused_computation.4 | loop fusion | flops 16769024 | bytes 17104896 | tf_op jit(solution)/shard_map/reduce_sum | solution.py:533
  123.9 9.3 %fusion.18 = bf16[16,64,512]{2,1,0:T(8,128)(2,1)} fusion(bf16[512,16,64]{0,2,1:T(8,128)(2,1)} %bitcast.84, f32[16,512,512]{1,2,0:T(8,128)} %get-tuple-element.35, f32[16,512]{1,0:T(8,128)S(1)} %fusion.1, f32[16,512]{1,0:T(8,128)S(1)} %get-tuple-element.34, pred[512,512]{0,1:T(8,128)(4,1)S(1)} %copy.50), kind=kOutput, calls=%fused_computation.42 | convolution fusion | flops 558366720 | bytes 19202048 | tf_op jit(solution)/shard_map/hqk,khd->qhd/dot_general | solution.py:534
  133.2 1.9 pad_maximum_fusion
  135.2 4.7 copy.58
  139.9 4.6 copy.59
  144.5 1.3 copy.60.o_hbm
  145.8 0.6 add.156.lse_hbm
  146.5 3.3 fusion.31
  150.7 12.6 %copy.55 = bf16[1024,4,1024]{0,2,1:T(8,128)(2,1)} copy(bf16[1024,4,1024]{2,0,1:T(8,128)(2,1)} %bitcast.63) | data formatting | bytes 16777216 | tf_op jit(solution)/shard_map/transpose | solution.py:522
  163.2 27.0 %add_convert_fusion = (bf16[512,4096]{1,0:T(8,128)(2,1)}, f32[512,4096]{1,0:T(8,128)}, f32[512,4096]{1,0:T(8,128)}) fusion(f32[4096]{0:T(1024)S(1)} %bitcast.85, bf16[512,1024]{1,0:T(8,128)(2,1)S(1)} %add_convert_fusion.2.h2_hbm, bf16[1024,4096]{0,1:T(8,128)(2,1)} %bitcast.74), kind=kOutput, calls=%fused_computation.7 | convolution fusion | flops 4441767936 | bytes 30425088 | tf_op jit(solution)/shard_map/dot_general | solution.py:29
  190.2 8.1 %reshape.233 = bf16[512,4,4,256]{3,2,1,0:T(4,128)(2,1)} reshape(bf16[512,4096]{1,0:T(8,128)(2,1)} %get-tuple-element.17) | data formatting | bytes 8388608 | tf_op jit(solution)/shard_map/reshape | solution.py:544
  198.4 5.7 %copy.57 = bf16[512,4,4,256]{3,0,1,2:T(8,128)(2,1)} copy(bf16[512,4,4,256]{3,2,1,0:T(4,128)(2,1)} %reshape.233) | data formatting | bytes 8388608 | tf_op jit(solution)/shard_map/reshape | solution.py:544
  204.0 9.8 %multiply_convert_fusion = bf16[512,4096]{1,0:T(8,128)(2,1)} fusion(f32[512,4096]{1,0:T(8,128)} %get-tuple-element.18, f32[512,4096]{1,0:T(8,128)} %get-tuple-element.38, f32[4096]{0:T(1024)S(1)} %bitcast.86), kind=kLoop, calls=%fused_computation.8 | loop fusion | flops 8388608 | bytes 20987904 | tf_op jit(solution)/shard_map/convert_element_type | solution.py:541
  213.8 7.8 %reshape.231 = bf16[512,4,4,256]{3,2,1,0:T(4,128)(2,1)} reshape(bf16[512,4096]{1,0:T(8,128)(2,1)} %multiply_convert_fusion) | data formatting | bytes 8388608 | tf_op jit(solution)/shard_map/reshape | solution.py:544
  221.6 5.7 %copy.56 = bf16[512,4,4,256]{3,0,1,2:T(8,128)(2,1)} copy(bf16[512,4,4,256]{3,2,1,0:T(4,128)(2,1)} %reshape.231) | data formatting | bytes 8388608 | tf_op jit(solution)/shard_map/reshape | solution.py:544
  227.3 237.8 %backward.1 = (bf16[3136,1024]{1,0:T(8,128)(2,1)}, bf16[512,1024]{1,0:T(8,128)(2,1)}, bf16[2,2,3136,1024]{3,2,1,0:T(8,128)(2,1)}) custom-call(f32[1]{0:T(128)S(6)} %select_n.58.factor_ref, bf16[512,1024]{1,0:T(8,128)(2,1)} %cot_hbm.1, f32[512,1]{1,0:T(8,128)} %fusion.20.live_hbm, f32[512,512]{1,0:T(8,128)} %broadcast_select_fusion.bias_hbm, ...), custom_call_target="tpu_custom_call" | custom-call | tf_op jit(solution)/shard_map/backward/pallas_call | solution.py:484
  465.2 1.3 slice.129
  466.5 0.8 slice.124
  467.9 0.6 slice.105
  469.7 2.2 slice.126
  471.9 3.5 slice.125
  475.4 1.0 slice.127
  476.4 4.3 fusion.27
  480.7 5.5 %copy.63 = f32[1024,1024]{0,1:T(8,128)} copy(f32[1024,1024]{1,0:T(8,128)} %bitcast.69) | data formatting | bytes 8388608 | tf_op jit(solution)/shard_map/reshape;squeeze | solution.py:559
  486.2 10.2 %add_convert_fusion.1 = bf16[512,1024]{1,0:T(8,128)(2,1)} fusion(f32[512,1024]{1,0:T(8,128)S(1)} %copy-done.2, bf16[512,4096]{1,0:T(8,128)(2,1)} %multiply_convert_fusion, bf16[4096,1024]{1,0:T(8,128)(2,1)} %all-gather.17.cloned.1.call-done, f32[1024]{0:T(1024)S(1)} %bitcast.96), kind=kOutput, calls=%fused_computation.39 | convolution fusion | flops 4296540160 | bytes 15732736 | tf_op jit(solution)/shard_map/dot_general | solution.py:29
  496.4 1.0 copy.68
  (50 shorter events, 6.6 us)
Async XLA Ops:
  7.2 17.6 %copy-start.3 = (bf16[512,1024]{1,0:T(8,128)(2,1)S(1)}, bf16[512,1024]{1,0:T(8,128)(2,1)}, u32[]{:S(2)}) copy-start(bf16[512,1024]{1,0:T(8,128)(2,1)} %x_hbm.1) | copy-start | bytes 3145732
  7.2 27.7 %all-gather.13.cloned.1.call-start = ((), (), s32[]{:S(2)}) async-start(), calls=%async_computation.1 | async-start | bytes 2621440 | tf_op jit(solution)/shard_map/all_gather | solution.py:518
  7.9 75.0 %all-gather.11.cloned.1.call-start = ((), (), s32[]{:S(2)}) async-start(), calls=%async_computation | async-start | bytes 7864320 | tf_op jit(solution)/shard_map/all_gather | solution.py:518
  8.7 142.0 %all-gather.15.cloned.1.call-start = ((), (), s32[]{:S(2)}) async-start(), calls=%async_computation.2 | async-start | bytes 10485760 | tf_op jit(solution)/shard_map/all_gather | solution.py:518
  9.4 217.9 %all-gather.17.cloned.1.call-start = ((), (), s32[]{:S(2)}) async-start(), calls=%async_computation.3 | async-start | bytes 10485760 | tf_op jit(solution)/shard_map/all_gather | solution.py:518
  31.5 60.1 %copy-start.4 = (bf16[512,1024]{1,0:T(8,128)(2,1)}, bf16[512,1024]{1,0:T(8,128)(2,1)S(1)}, u32[]{:S(2)}) copy-start(bf16[512,1024]{1,0:T(8,128)(2,1)S(1)} %fusion.14.h1_hbm) | copy-start | bytes 3145732
  123.9 9.4 %copy-start.6 = (bf16[512,1024]{1,0:T(8,128)(2,1)S(1)}, bf16[512,1024]{1,0:T(8,128)(2,1)}, u32[]{:S(2)}) copy-start(bf16[512,1024]{1,0:T(8,128)(2,1)} %get-tuple-element.15) | copy-start | bytes 3145732
  135.2 9.4 %copy-start.8 = (bf16[16,64,512]{2,1,0:T(8,128)(2,1)S(1)}, bf16[16,64,512]{2,1,0:T(8,128)(2,1)}, u32[]{:S(2)}) copy-start(bf16[16,64,512]{2,1,0:T(8,128)(2,1)} %fusion.18) | copy-start | bytes 3145732
  149.8 13.4 %copy-start.1 = (f32[512,1024]{1,0:T(8,128)}, f32[512,1024]{1,0:T(8,128)S(1)}, u32[]{:S(2)}) copy-start(f32[512,1024]{1,0:T(8,128)S(1)} %get-tuple-element.37.x1_hbm) | copy-start | bytes 6291460
  150.6 12.6 %copy-start.5 = (bf16[512,1024]{1,0:T(8,128)(2,1)}, bf16[512,1024]{1,0:T(8,128)(2,1)S(1)}, u32[]{:S(2)}) copy-start(bf16[512,1024]{1,0:T(8,128)(2,1)S(1)} %add_convert_fusion.2.h2_hbm) | copy-start | bytes 3145732
  469.7 5.7 %copy-start = (bf16[3136,1024]{1,0:T(8,128)(2,1)S(1)}, bf16[3136,1024]{1,0:T(8,128)(2,1)}, u32[]{:S(2)}) copy-start(bf16[3136,1024]{1,0:T(8,128)(2,1)} %get-tuple-element.14) | copy-start | bytes 19267588
  480.7 5.5 %copy-start.2 = (f32[512,1024]{1,0:T(8,128)S(1)}, f32[512,1024]{1,0:T(8,128)}, u32[]{:S(2)}) copy-start(f32[512,1024]{1,0:T(8,128)} %copy-done.1) | copy-start | bytes 6291460
  480.7 5.5 %copy-start.9 = (f32[4,1,256]{2,1,0:T(1,128)S(1)}, f32[4,1,256]{2,1,0:T(1,128)}, u32[]{:S(2)}) copy-start(f32[4,1,256]{2,1,0:T(1,128)} %get-tuple-element.22) | copy-start | bytes 12292
  486.2 10.2 %copy-start.7 = (bf16[512,1024]{1,0:T(8,128)(2,1)S(1)}, bf16[512,1024]{1,0:T(8,128)(2,1)}, u32[]{:S(2)}) copy-start(bf16[512,1024]{1,0:T(8,128)(2,1)} %get-tuple-element.51) | copy-start | bytes 3145732
Sparse Core Ops, SparseCore 0:
  9.6 25.2 all-gather.12
  36.5 46.3 all-gather.10
  84.4 58.2 all-gather.14
  144.2 58.2 all-gather.16

commit v2 on v1

--- a/solution.py
+++ b/solution.py
@@ -17,32 +17,6 @@
 F32 = jnp.float32
 BF16 = jnp.bfloat16
 MESH = pl.DeviceIdType.MESH
-
-
-def layer_norm(inputs, gain_row, shift_row):
-    center = inputs - jnp.mean(inputs, axis=-1, keepdims=True)
-    spread = jnp.mean(center * center, axis=-1, keepdims=True)
-    return center * lax.rsqrt(spread + EPSILON) * gain_row + shift_row
-
-
-def dot_plain(first_op, second_op):
-    return jnp.dot(first_op, second_op, preferred_element_type=jnp.float32)
-
-
-def segment_ids(group_id, image_count, row_count):
-    length = jnp.where(group_id == 0, LEN0, LEN1).astype(jnp.int32)
-    position = jnp.arange(row_count, dtype=jnp.int32)
-    image_index = position // length
-    in_image = image_index < image_count
-    return (jnp.where(in_image, image_index, row_count), in_image)
-
-
-def block_scores(query_part, key_rows, segment_part, segment):
-    scores = jnp.einsum(
-        "qhd,khd->hqk", query_part, key_rows, preferred_element_type=jnp.float32
-    ) * HDIM ** (-0.5)
-    allowed = segment_part[:, None] == segment[None, :]
-    return jnp.where(allowed[None], scores, -1e30)
 
 
 def split_plan(chunk_rows, bit_count):
@@ -232,10 +206,10 @@
     return spot < HDIM if half == 0 else spot >= HDIM
 
 
-def backward_kernel(rows, chunk_rows, chunk_count, bit_count, factor_ref, cot_hbm, live_hbm, bias_hbm, z_hbm, slope_hbm, h2_hbm,
-                    x1_hbm, o_hbm, qkv_hbm, lse_hbm, h1_hbm, x_hbm, gains_hbm, wd_hbm, wu_hbm, wqkv_hbm, wo_hbm,
+def backward_kernel(rows, chunk_rows, chunk_count, bit_count, info_ref, cot_hbm, z_hbm, slope_hbm, h2_hbm,
+                    x1_hbm, o_hbm, qkv_hbm, lse_hbm, h1_hbm, x_hbm, vecs_hbm, wd_hbm, wu_hbm, wqkv_hbm, wo_hbm,
                     out_ref, gtok_ref, g_ref,
-                    dy, live, bias, h2, x1, o, qkv, lse, h1, x, gains, wqkv, wo,
+                    dy, h2, x1, o, qkv, lse, h1, x, gains, wqkv, wo, bias,
                     z_tile, slope_tile, wd_tile, wu_tile, stage, du_low,
                     dh, dx1, da, do, dp_all, vecs, upb, tail, load_sem, tile_sem, stage_sem, gtok_sem, comm):
     tick, tick_count, peers = reduction(chunk_rows, chunk_count, bit_count, g_ref, out_ref, *comm)
@@ -250,23 +224,24 @@
             pltpu.make_async_copy(wu_hbm.at[f, :, lanes(q, 256)], wu_tile.at[s], tile_sem.at[3, s]),
         ]
 
-    whole = [(cot_hbm, dy), (live_hbm, live), (h2_hbm, h2), (x1_hbm, x1), (gains_hbm, gains), (wo_hbm, wo), (bias_hbm, bias),
-             (o_hbm, o), (qkv_hbm, qkv), (lse_hbm, lse), (h1_hbm, h1), (wqkv_hbm, wqkv), (x_hbm, x)]
+    whole = [(cot_hbm, dy), (h2_hbm, h2), (x1_hbm, x1), (vecs_hbm, gains), (wo_hbm, wo), (o_hbm, o), (qkv_hbm, qkv),
+             (lse_hbm, lse), (h1_hbm, h1), (wqkv_hbm, wqkv), (x_hbm, x)]
 
     def whole_copy(i):
         return pltpu.make_async_copy(whole[i][0], whole[i][1], load_sem.at[i])
 
-    for i in range(3):
+    for i in range(2):
         whole_copy(i).start()
     for copy in tile_copies(0):
         copy.start()
-    for i in range(3, len(whole)):
+    for i in range(2, len(whole)):
         whole_copy(i).start()
     greet(peers)
-    factor = factor_ref[0]
-    for i in range(3):
+    factor = info_ref[0]
+    for i in range(2):
         whole_copy(i).wait()
-    dy[...] = (dy[...].astype(F32) * live[...]).astype(BF16)
+    live = lax.broadcasted_iota(jnp.int32, (rows, D), 0).astype(F32) < info_ref[2]
+    dy[...] = jnp.where(live, dy[...].astype(F32), 0.0).astype(BF16)
     dh[...] = jnp.zeros_like(dh)
 
     def stage_copy(which, n):
@@ -314,7 +289,7 @@
             stage_copy(which, n).wait()
     tick(10)
 
-    for i in (3, 4):
+    for i in (2, 3):
         whole_copy(i).wait()
     vecs[...] = jnp.zeros_like(vecs)
     step = 64
@@ -348,7 +323,7 @@
     norm_back(x1, 1, finish_mlp)
     tick(11)
 
-    whole_copy(5).wait()
+    whole_copy(4).wait()
     for c in range(4):
         total = jnp.zeros((rows, 256), F32)
         for f in range(4):
@@ -357,8 +332,9 @@
         do[2 * c] = low[:, :128]
         do[2 * c + 1] = low[:, 128:]
     tick(12)
-    for i in range(6, 10):
+    for i in range(5, 8):
         whole_copy(i).wait()
+    fill_bias(bias, info_ref, rows)
 
     def heads(p, carry):
         q_pair, k_pair, v_pair, do_pair = qkv[p], qkv[8 + p], qkv[16 + p], do[p]
@@ -393,7 +369,7 @@
 
     lax.fori_loop(0, 8, heads, 0)
 
-    whole_copy(10).wait()
+    whole_copy(8).wait()
 
     def proj(n, carry):
         s, q, f = lax.rem(n, 2), n // 4, lax.rem(n, 4)
@@ -416,8 +392,8 @@
     for n in (14, 15):
         stage_copy(2, n).wait()
 
-    whole_copy(11).wait()
-    whole_copy(12).wait()
+    whole_copy(9).wait()
+    whole_copy(10).wait()
     for c in range(4):
         total = jnp.zeros((rows, 256), F32)
         for f in range(4):
@@ -452,14 +428,15 @@
     gtok_copy.wait()
 
 
-def backward(factor, cot, live, bias, z, slope, h2, x1, o, qkv, lse, h1, x, gains, wd, wu, wqkv, wo, dp_size):
+def backward(info, cot, z, slope, h2, x1, o, qkv, lse, h1, x, vecs, wd, wu, wqkv, wo, dp_size):
     rows = cot.shape[0]
     chunk_rows = 64 if dp_size <= 32 else 128
     chunk_count = 3072 // chunk_rows + 1
     bit_count = dp_size.bit_length() - 1
     any_space = pl.BlockSpec(memory_space=pl.ANY)
     like = lambda a: pltpu.VMEM(a.shape, a.dtype)
-    scratch = [like(a) for a in (cot, live, bias, h2, x1, o, qkv, lse, h1, x, gains, wqkv, wo)] + [
+    scratch = [like(a) for a in (cot, h2, x1, o, qkv, lse, h1, x, vecs, wqkv, wo)] + [
+        pltpu.VMEM((rows, rows), F32),
         pltpu.VMEM((2, rows, 256), BF16),
         pltpu.VMEM((2, rows, 256), BF16),
         pltpu.VMEM((2, 256, D), BF16),
@@ -474,7 +451,7 @@
         pltpu.VMEM((8, 1, D), F32),
         pltpu.VMEM((16, 1, 256), F32),
         pltpu.VMEM((4, chunk_rows, WIDE), BF16),
-        pltpu.SemaphoreType.DMA((13,)),
+        pltpu.SemaphoreType.DMA((11,)),
         pltpu.SemaphoreType.DMA((4, 2)),
         pltpu.SemaphoreType.DMA((3, 2)),
         pltpu.SemaphoreType.DMA((5,)),
@@ -488,12 +465,392 @@
             jax.ShapeDtypeStruct((rows, D), BF16),
             jax.ShapeDtypeStruct((2, 2, g_rows, WIDE), BF16),
         ),
-        in_specs=[pl.BlockSpec(memory_space=pltpu.SMEM)] + [any_space] * 17,
+        in_specs=[pl.BlockSpec(memory_space=pltpu.SMEM)] + [any_space] * 15,
         out_specs=(any_space, any_space, any_space),
         scratch_shapes=scratch,
         compiler_params=pltpu.CompilerParams(collective_id=1, has_side_effects=True, vmem_limit_bytes=60 * 2**20),
         name="backward",
-    )(factor, cot, live, bias, z, slope, h2, x1, o, qkv, lse, h1, x, gains, wd, wu, wqkv, wo)
+    )(info, cot, z, slope, h2, x1, o, qkv, lse, h1, x, vecs, wd, wu, wqkv, wo)
+
+
+def fill_bias(bias, info_ref, rows):
+    step = 128
+
+    def segments(dim, shape, start):
+        place = (lax.broadcasted_iota(jnp.int32, shape, dim) + start).astype(F32)
+        return jnp.where(place < info_ref[2], jnp.floor((place + 0.5) * info_ref[1]), float(rows))
+
+    for i in range(rows // step):
+        same = segments(0, (step, rows), i * step) == segments(1, (step, rows), 0)
+        bias[i * step : (i + 1) * step, :] = jnp.where(same, 0.0, -1e30)
+
+
+ERF_TOP = (-2.72614225801306e-10, 2.77068142495902e-08, -2.10102402082508e-06, -5.69250639462346e-05,
+           -7.34990630326855e-04, -2.95459980854025e-03, -1.60960333262415e-02)
+ERF_BOTTOM = (-1.45660718464996e-05, -2.13374055278905e-04, -1.68282697438203e-03, -7.37332916720468e-03,
+              -1.42647390514189e-02)
+
+
+def erf(v):
+    v = jnp.clip(v, -4.0, 4.0)
+    square = v * v
+    top, bottom = ERF_TOP[0], ERF_BOTTOM[0]
+    for c in ERF_TOP[1:]:
+        top = top * square + c
+    for c in ERF_BOTTOM[1:]:
+        bottom = bottom * square + c
+    return v * top / bottom
+
+
+PARTS = 3
+PART_ROWS = 336
+PIECE_ROWS = 112
+PIECES = PART_ROWS // PIECE_ROWS
+REST = PARTS * PART_ROWS
+
+
+def forward_kernel(rows, info_ref, tok_hbm, vec_hbm, sqkv, so, su, sd,
+                   wqkv, wo, wu, wd, out_hbm, qkv_hbm, lse_hbm, o_hbm, x1_hbm, h1_hbm, h2_hbm, z_hbm, slope_hbm, vecs_hbm,
+                   x, h1, qkv, o, x1, h2, y, bias, lse, vec, vecs, qv, upb, wqkv_v, wo_v, wu_t, wd_t, z_t, slope_t, own,
+                   own_sem, vec_sem, rest_sem, x_sem, y_sem, z_sem, fx_sem, fy_sem, fz_sem, frest_sem, core_sem,
+                   load_sem, tile_sem, save_sem, ztile_sem):
+    dp, f = lax.axis_index("dp"), lax.axis_index("fsdp")
+    core, across = lax.rem(f, 2), f // 2
+    yb, zb = lax.rem(dp, 2), lax.rem(dp // 2, 2)
+    core_f, x_f = f + 1 - 2 * core, f + 2 - 4 * across
+    diag_f = 3 - f
+    core_peer, x_peer, diag_peer = (dp, core_f), (dp, x_f), (dp, diag_f)
+    y_peer, z_peer = (dp + 1 - 2 * yb, f), (dp + 2 - 4 * zb, f)
+    part_x = yb + (1 - yb) * 2 * zb
+    part_y = (1 - yb) + yb * 2 * zb
+    part_z = 2 - 2 * zb
+    shards, full = (sqkv, so, su, sd), (wqkv, wo, wu, wd)
+
+    def order(i):
+        return 2 * lax.rem(across + i // 2, 2) + lax.rem(core + i, 2)
+
+    def remote(src, dst, sems, slot, peer):
+        return pltpu.make_async_remote_copy(src, dst, sems.at[0, slot], sems.at[1, slot], device_id=peer,
+                                            device_id_type=MESH)
+
+    def part(k, index):
+        return pl.ds(pl.multiple_of(index * PART_ROWS + (k % PIECES) * PIECE_ROWS, 16), PIECE_ROWS)
+
+    rest = pl.ds(REST, D - REST)
+
+    def x_copy(k):
+        w, at = k // PIECES, part(k, part_x)
+        return remote(shards[w].at[at, :], full[w].at[f, at, :], x_sem, k, x_peer)
+
+    def hop(k, index, sems, peer):
+        w, at = k // PIECES, part(k, index)
+        return remote(full[w].at[x_f, at, :], full[w].at[x_f, at, :], sems, k, peer)
+
+    y_copy = lambda k: hop(k, part_x, y_sem, y_peer)
+    z_copy = lambda k: hop(k, 2 * zb, z_sem, z_peer)
+    fx_copy = lambda k: hop(k, part_x, fx_sem, core_peer)
+    fy_copy = lambda k: hop(k, part_y, fy_sem, core_peer)
+    fz_copy = lambda k: hop(k, part_z, fz_sem, core_peer)
+
+    def rest_copy(w):
+        return remote(shards[w].at[rest, :], full[w].at[f, rest, :], rest_sem, w, x_peer)
+
+    def frest_copy(w):
+        return remote(full[w].at[x_f, rest, :], full[w].at[x_f, rest, :], frest_sem, w, core_peer)
+
+    def core_copy(w):
+        return remote(shards[w], full[w].at[f], core_sem, w, core_peer)
+
+    def own_load(w):
+        return pltpu.make_async_copy(shards[w], own[w], own_sem.at[0, w])
+
+    def own_copy(w):
+        return pltpu.make_async_copy(own[w], full[w].at[f], own_sem.at[1, w])
+
+    count = 4 * PIECES
+
+    def service(k):
+        if 0 <= k - 2 < count:
+            z_copy(k - 2).wait_recv()
+            fz_copy(k - 2).start()
+        if 0 <= k - 1 < count:
+            y_copy(k - 1).wait_recv()
+            fy_copy(k - 1).start()
+
+            @pl.when(yb == 1)
+            def _():
+                z_copy(k - 1).start()
+        if 0 <= k < count:
+            x_copy(k).wait_recv()
+            y_copy(k).start()
+
+            @pl.when(yb == 0)
+            def _():
+                z_copy(k).start()
+
+            fx_copy(k).start()
+            if k + 3 < count:
+                x_copy(k + 3).start()
+            if k % PIECES == 0:
+                w = k // PIECES
+                rest_copy(w).wait_recv()
+                frest_copy(w).start()
+
+    def arrived(w):
+        frest_copy(w).wait_recv()
+        for k in range(w * PIECES, (w + 1) * PIECES):
+            fx_copy(k).wait_recv()
+            fy_copy(k).wait_recv()
+            fz_copy(k).wait_recv()
+
+    load_x = pltpu.make_async_copy(tok_hbm, x, load_sem.at[0])
+    load_x.start()
+    load_vec = pltpu.make_async_copy(vec_hbm, vec.at[f], load_sem.at[1])
+    load_vec.start()
+    for w in range(4):
+        own_load(w).start()
+    greet([core_peer, x_peer, diag_peer, y_peer, z_peer])
+    load_vec.wait()
+    vec_copies = [remote(vec.at[f], vec.at[f], vec_sem, i, peer)
+                  for i, peer in enumerate((core_peer, x_peer, diag_peer))]
+    for copy in vec_copies:
+        copy.start()
+    for k in range(3):
+        x_copy(k).start()
+    core_copy(0).start()
+    for w in range(4):
+        rest_copy(w).start()
+    for w in range(1, 4):
+        core_copy(w).start()
+    for w in range(4):
+        own_load(w).wait()
+        own_copy(w).start()
+    fill_bias(bias, info_ref, rows)
+    for copy in vec_copies:
+        copy.wait()
+    qv[...] = jnp.zeros_like(qv)
+    for g in range(4):
+        wide = vec[g].astype(F32)
+        for i in range(8):
+            vecs[i, :, 256 * g : 256 * g + 256] = wide[i : i + 1, :]
+        for i in range(4):
+            upb[4 * g + i] = wide[8 + i : 9 + i, :]
+        for i in range(2):
+            qv[2 * g + i] = wide[4:5, 128 * i : 128 * i + 128]
+            qv[16 + 2 * g + i] = wide[5:6, 128 * i : 128 * i + 128]
+
+    step = 64
+
+    def normalize(value, which):
+        center = value - jnp.mean(value, axis=-1, keepdims=True)
+        spread = jnp.mean(center * center, axis=-1, keepdims=True)
+        return (center * lax.rsqrt(spread + EPSILON) * vecs[which] + vecs[2 + which]).astype(BF16)
+
+    load_x.wait()
+
+    def norm_in(i, carry):
+        at = pl.ds(pl.multiple_of(i * step, step), step)
+        h1[at, :] = normalize(x[at, :].astype(F32), 0)
+        return carry
+
+    lax.fori_loop(0, rows // step, norm_in, 0)
+    saves = []
+
+    def save(src, dst):
+        copy = pltpu.make_async_copy(src, dst, save_sem.at[len(saves)])
+        copy.start()
+        saves.append(copy)
+
+    save(h1, h1_hbm)
+    save(vecs, vecs_hbm)
+
+    def qkv_load(i):
+        return pltpu.make_async_copy(wqkv.at[order(i)], wqkv_v.at[i % 2], load_sem.at[2 + i % 2])
+
+    def project(i):
+        qkv_load(i).wait()
+        product = dot_nn(h1[...], wqkv_v[i % 2])
+        for b in range(6):
+            block = 6 * order(i) + b
+            scale = jnp.where(block < 8, HDIM ** (-0.5), 1.0).astype(F32)
+            qkv[block] = ((product[:, 128 * b : 128 * b + 128] + qv[block]) * scale).astype(BF16)
+
+    own_copy(0).wait()
+    qkv_load(0).start()
+    core_copy(0).wait_recv()
+    qkv_load(1).start()
+    project(0)
+    service(0)
+    project(1)
+    for k in range(1, 5):
+        service(k)
+    qkv_load(2).start()
+    arrived(0)
+    qkv_load(3).start()
+    project(2)
+    project(3)
+    service(5)
+    save(qkv, qkv_hbm)
+
+    def heads(p, carry):
+        for i, k in ((0, 6), (2, 7), (4, 8), (7, 9)):
+            @pl.when(p == i)
+            def _(k=k):
+                service(k)
+
+        q_pair, k_pair, v_turned = qkv[p], qkv[8 + p], qkv[16 + p].T
+        total = jnp.zeros((128, rows), F32)
+        for half in range(2):
+            q_half = jnp.where(half_mask((rows, 128), 1, half), q_pair, jnp.zeros_like(q_pair))
+            v_half = jnp.where(half_mask((128, rows), 0, half), v_turned, jnp.zeros_like(v_turned))
+            scores = dot_nt(k_pair, q_half) + bias[...]
+            highest = jnp.max(scores, axis=0, keepdims=True)
+            weights = jnp.exp(scores - highest)
+            sums = jnp.sum(weights, axis=0, keepdims=True)
+            total += dot_nn(v_half, (weights * (1.0 / sums)).astype(BF16))
+            lse[p, half] = highest + jnp.log(sums)
+        o[:, lanes(p, 128)] = total.T.astype(BF16)
+        return carry
+
+    lax.fori_loop(0, 8, heads, 0)
+    save(o, o_hbm)
+    save(lse, lse_hbm)
+
+    own_copy(1).wait()
+    core_copy(1).wait_recv()
+    arrived(1)
+    wo_load = pltpu.make_async_copy(wo, wo_v, load_sem.at[4])
+    wo_load.start()
+    own_copy(2).wait()
+    own_copy(3).wait()
+    for w in (2, 3):
+        core_copy(w).wait_recv()
+
+    def tile_of(n):
+        return 4 * lax.rem(n, 4) + order(n // 4)
+
+    def tile_loads(n):
+        s, q, g = lax.rem(n, 2), lax.rem(n, 4), order(n // 4)
+        return [pltpu.make_async_copy(wu.at[g, :, lanes(q, 256)], wu_t.at[s], tile_sem.at[0, s]),
+                pltpu.make_async_copy(wd.at[g, lanes(q, 256), :], wd_t.at[s], tile_sem.at[1, s])]
+
+    for copy in tile_loads(0):
+        copy.start()
+    wo_load.wait()
+    for g in range(4):
+        at = slice(256 * g, 256 * g + 256)
+        x1[:, at] = x[:, at].astype(F32) + dot_nn(o[...], wo_v[g]) + vecs[6, :, at]
+    save(x1, x1_hbm)
+
+    def norm_mid(i, carry):
+        at = pl.ds(pl.multiple_of(i * step, step), step)
+        value = x1[at, :]
+        h2[at, :] = normalize(value, 1)
+        y[at, :] = value + vecs[7]
+        return carry
+
+    lax.fori_loop(0, rows // step, norm_mid, 0)
+    save(h2, h2_hbm)
+
+    def tile_saves(n):
+        s = lax.rem(n, 2)
+        return [pltpu.make_async_copy(z_t.at[s], z_hbm.at[tile_of(n)], ztile_sem.at[0, s]),
+                pltpu.make_async_copy(slope_t.at[s], slope_hbm.at[tile_of(n)], ztile_sem.at[1, s])]
+
+    def ffn(n, carry):
+        s = lax.rem(n, 2)
+        for i, k in ((1, 10), (4, 11), (6, 12), (7, 13)):
+            @pl.when(n == i)
+            def _(k=k):
+                service(k)
+                if k == 13:
+                    arrived(2)
+                    arrived(3)
+
+        @pl.when(n + 1 < 16)
+        def _():
+            for copy in tile_loads(n + 1):
+                copy.start()
+
+        for copy in tile_loads(n):
+            copy.wait()
+
+        @pl.when(n >= 2)
+        def _():
+            for copy in tile_saves(n - 2):
+                copy.wait()
+
+        u = dot_nn(h2[...], wu_t[s]) + upb[4 * order(n // 4) + lax.rem(n, 4)]
+        bell = 0.5 + 0.5 * erf(u * (0.5 ** 0.5))
+        z = (u * bell).astype(BF16)
+        z_t[s] = z
+        slope_t[s] = (bell + u * (jnp.exp(-0.5 * u * u) * 0.3989422804014327)).astype(BF16)
+        for copy in tile_saves(n):
+            copy.start()
+        y[...] += dot_nn(z, wd_t[s])
+        return carry
+
+    lax.fori_loop(0, 16, ffn, 0)
+    x[...] = y[...].astype(BF16)
+    save(x, out_hbm)
+    for n in (14, 15):
+        for copy in tile_saves(n):
+            copy.wait()
+    for copy in saves:
+        copy.wait()
+    for k in range(count):
+        for copy in (x_copy(k), y_copy(k), z_copy(k), fx_copy(k), fy_copy(k), fz_copy(k)):
+            copy.wait_send()
+    for w in range(4):
+        for copy in (rest_copy(w), frest_copy(w), core_copy(w)):
+            copy.wait_send()
+
+
+def forward(info, tokens, vec, w_qkv, w_out, w_up, w_down):
+    rows = tokens.shape[0]
+    any_space = pl.BlockSpec(memory_space=pl.ANY)
+    full = lambda a: jax.ShapeDtypeStruct((4,) + a.shape, a.dtype)
+    shape = jax.ShapeDtypeStruct
+    count = 4 * PIECES
+    sems = lambda *dims: pltpu.SemaphoreType.DMA(dims)
+    return pl.pallas_call(
+        functools.partial(forward_kernel, rows),
+        out_shape=(
+            full(w_qkv), full(w_out), full(w_up), full(w_down),
+            shape((rows, D), BF16), shape((24, rows, 128), BF16), shape((8, 2, 1, rows), F32), shape((rows, D), BF16),
+            shape((rows, D), F32), shape((rows, D), BF16), shape((rows, D), BF16), shape((16, rows, 256), BF16),
+            shape((16, rows, 256), BF16), shape((8, 1, D), F32),
+        ),
+        in_specs=[pl.BlockSpec(memory_space=pltpu.SMEM)] + [any_space] * 6,
+        out_specs=(any_space,) * 14,
+        scratch_shapes=[
+            pltpu.VMEM((rows, D), BF16),
+            pltpu.VMEM((rows, D), BF16),
+            pltpu.VMEM((24, rows, 128), BF16),
+            pltpu.VMEM((rows, D), BF16),
+            pltpu.VMEM((rows, D), F32),
+            pltpu.VMEM((rows, D), BF16),
+            pltpu.VMEM((rows, D), F32),
+            pltpu.VMEM((rows, rows), F32),
+            pltpu.VMEM((8, 2, 1, rows), F32),
+            pltpu.VMEM((4, 16, 256), BF16),
+            pltpu.VMEM((8, 1, D), F32),
+            pltpu.VMEM((24, 1, 128), F32),
+            pltpu.VMEM((16, 1, 256), F32),
+            pltpu.VMEM((2,) + w_qkv.shape, BF16),
+            pltpu.VMEM((4,) + w_out.shape, BF16),
+            pltpu.VMEM((2, D, 256), BF16),
+            pltpu.VMEM((2, 256, D), BF16),
+            pltpu.VMEM((2, rows, 256), BF16),
+            pltpu.VMEM((2, rows, 256), BF16),
+            [pltpu.VMEM(a.shape, BF16) for a in (w_qkv, w_out, w_up, w_down)],
+            sems(2, 4), sems(2, 3), sems(2, 4),
+            sems(2, count), sems(2, count), sems(2, count), sems(2, count), sems(2, count), sems(2, count),
+            sems(2, 4), sems(2, 4), sems(5), sems(2, 2), sems(8), sems(2, 2),
+        ],
+        compiler_params=pltpu.CompilerParams(collective_id=2, has_side_effects=True, vmem_limit_bytes=60 * 2**20),
+        name="forward",
+    )(info, tokens, vec, w_qkv, w_out, w_up, w_down)
 
 
 def local(
@@ -514,49 +871,23 @@
 ):
     rows = tokens.shape[0]
     group_id = group[0]
-    segment, in_image = segment_ids(group_id, images[0, 0], rows)
-    gather = lambda a: lax.all_gather(a, "fsdp", axis=0)
-    vec = gather(jnp.concatenate([ln_gain, ln_bias, qv_bias, out_bias, up_bias.reshape(4, 256)], axis=0)).astype(F32)
-    pick = lambda i: vec[:, i].reshape(D)
-    wqkv, wo, wu, wd = gather(w_qkv), gather(w_out), gather(w_up), gather(w_down)
-    flat = lambda w: w.transpose(1, 0, 2).reshape(D, -1)
-    x = tokens.astype(F32)
-    h1 = layer_norm(x, pick(0), pick(2)).astype(BF16)
-    projected = dot_plain(h1, flat(wqkv))
-    q = (projected[:, :D] + pick(4)).astype(BF16)
-    k = projected[:, D : 2 * D].astype(BF16)
-    v = (projected[:, 2 * D :] + pick(5)).astype(BF16)
-    split = lambda a: a.reshape(rows, HEADS, HDIM)
-    scores = block_scores(split(q), split(k), segment, segment)
-    highest = jnp.max(scores, axis=-1, keepdims=True)
-    weights = jnp.exp(scores - highest)
-    totals = jnp.sum(weights, axis=-1, keepdims=True)
-    o = jnp.einsum("hqk,khd->qhd", (weights / totals).astype(BF16), split(v), preferred_element_type=F32)
-    o = o.reshape(rows, D).astype(BF16)
-    lse = (highest + jnp.log(totals))[..., 0]
-    x1 = x + dot_plain(o, flat(wo)) + pick(6)
-    h2 = layer_norm(x1, pick(1), pick(3)).astype(BF16)
-    u = dot_plain(h2, flat(wu)) + vec[:, 8:].reshape(-1)
-    gelu, pull = jax.vjp(functools.partial(jax.nn.gelu, approximate=False), u)
-    z = gelu.astype(BF16)
-    slope = pull(jnp.ones_like(u))[0].astype(BF16)
-    output = (x1 + dot_plain(z, wd.reshape(-1, D)) + pick(7)).astype(BF16)
-    tile = lambda a: a.reshape(rows, 4, 4, 256).transpose(2, 1, 0, 3).reshape(16, rows, 256)
-    qkv = jnp.concatenate([q * HDIM ** (-0.5), k, v], axis=1).astype(BF16).reshape(rows, 24, 128).transpose(1, 0, 2)
-    bias = jnp.where(segment[:, None] == segment[None, :], 0.0, -1e30).astype(F32)
     weights_raw = counts.astype(F32)
     shares = weights_raw / (weights_raw[0] + weights_raw[1]) / (lax.axis_size("dp") * lax.axis_size("fsdp") // 2)
     factor = jnp.where(group_id == 0, shares[0], shares[1])
+    length = jnp.where(group_id == 0, LEN0, LEN1)
+    info = jnp.stack([factor, 1.0 / length.astype(F32), (images[0, 0] * length).astype(F32)])
+    vec = jnp.concatenate(
+        [ln_gain, ln_bias, qv_bias, out_bias, up_bias.reshape(4, 256), jnp.zeros((4, 256), BF16)], axis=0)
+    wqkv, wo, wu, wd, output, qkv, lse, o, x1, h1, h2, z, slope, vecs = forward(
+        info, tokens, vec, w_qkv, w_out, w_up, w_down)
     total, grad_tokens, _ = backward(
-        factor.reshape(1), cotangent, in_image[:, None].astype(F32), bias, tile(z), tile(slope), h2, x1, o, qkv,
-        lse.reshape(8, 2, 1, rows), h1, tokens, jnp.stack([pick(0), pick(1)])[:, None, :], wd, wu, wqkv, wo,
-        lax.axis_size("dp"))
-    total = total.astype(F32)
+        info, cotangent, z, slope, h2, x1, o, qkv, lse, h1, tokens, vecs, wd, wu, wqkv, wo, lax.axis_size("dp"))
     blocks = total[:2048].reshape(4, 2, 256, D)
-    small = total[3072:3089]
+    small = total[3072:3089].astype(F32)
     return (
-        output, grad_tokens, small[0:4:2, :256], small[4:8:2, :256], total[2048:3072, :768], small[8:12:2, :256],
-        total[2048:3072, 768:], small[12:16:2, :256], blocks[:, 1].reshape(D, D).T, small[16], blocks[:, 0].reshape(D, D),
+        output, grad_tokens, small[0:4:2, :256], small[4:8:2, :256], total[2048:3072, :768].astype(F32), small[8:12:2, :256],
+        total[2048:3072, 768:].astype(F32), small[12:16:2, :256], blocks[:, 1].reshape(D, D).T.astype(F32), small[16],
+        blocks[:, 0].reshape(D, D).astype(F32),
     )
 
 

time: 510 us -> 383 us (0.75); the launches traced: 504 us -> 383 us
  Pallas kernels: 238 us -> 348 us
  local copies, waits for them, and re-layouts: 95.4 us -> 17.3 us
  matrix products: 65.8 us -> 0 us
  waiting for transfers between devices: 49.6 us -> 0 us
  other arithmetic: 31.1 us -> 12.7 us
  between operations: 18.3 us -> 4.62 us
  blocking collectives: 6.16 us -> 0 us
    pallas_call x0 -> x1, Pallas kernels: none -> 106 us  [forward(): pl.pallas_call(functools.partial(forward_kernel, rows), out_shape=(full(w...]
    dot_general x6 -> x0, matrix products: 65.8 us -> none  [the longest x4 46.6 us: dot_plain(): return jnp.dot(first_op, second_op, preferred_element_type=jnp.float32)]
    all_gather x4 -> x0, waiting for transfers between devices: 47 us -> none  [local(): gather = lambda a: lax.all_gather(a, 'fsdp', axis=0)]
    reshape x5 -> x0, local copies, waits for them, and re-layouts: 31.9 us -> none  [the longest x4 27.3 us: local(): a.reshape(rows, 4, 4, 256).transpose(2, 1, 0, 3).reshape(16, rows, 256)]
    transpose x3 -> x0, local copies, waits for them, and re-layouts: 25.7 us -> none  [local(): flat = lambda w: w.transpose(1, 0, 2).reshape(D, -1)]
    slice x6 -> x1, local copies, waits for them, and re-layouts: 12.7 us -> 0.44 us  [local(): blocks[:, 0].reshape(D, D).astype(F32)]
    reduce_sum x4 -> x0, other arithmetic: 10.2 us -> none  [the longest x1 9.25 us: local(): totals = jnp.sum(weights, axis=-1, keepdims=True)]
    all_gather x1 -> x0, blocking collectives: 6.16 us -> none  [local(): gather = lambda a: lax.all_gather(a, 'fsdp', axis=0)]
  transfers between devices with their start and end apart: 4 -> 0, of which waited for: 2 -> 0; matrix products, arithmetic and copies ran while one was open for 32% -> 0% of each run, Pallas kernels for 0% -> 0%
where the time goes in v2:
time: 383 us
  Pallas kernels  348 us (91%)
  local copies, waits for them, and re-layouts  17.3 us (5%)
  other arithmetic  12.7 us (3%)
  between operations  4.62 us (1%)
    pallas_call x1, Pallas kernels, backward(): pl.pallas_call(functools.partial(backward_kernel, rows, chunk_rows, chunk...  242 us
    pallas_call x1, Pallas kernels, forward(): pl.pallas_call(functools.partial(forward_kernel, rows), out_shape=(full(w...  106 us

profile of v2, /device:TPU:0, one launch (start us, length us, event | category | flops | bytes accessed | tf_op | source)
XLA Modules:
  0.0 382.5 jit_solution(15180446362519653653)
XLA Ops:
  2.0 0.7 convert_element_type.33
  2.6 0.6 fusion.2
  4.5 0.7 divide_multiply_fusion
  5.2 0.6 fusion.1
  7.1 0.6 pad_maximum_fusion.info_ref
  7.7 0.7 reshape.40
  8.4 1.9 concatenate.3.vec_hbm
  10.3 106.3 %forward.1 = (bf16[4,1024,768]{2,1,0:T(8,128)(2,1)}, bf16[4,1024,256]{2,1,0:T(8,128)(2,1)}, bf16[4,1024,1024]{2,1,0:T(8,128)(2,1)}, bf16[4,1024,1024]{2,1,0:T(8,...) custom-call(f32[3]{0:T(128)} %pad_maximum_fusion.info_ref, ...), custom_call_target="tpu_custom_call" | custom-call | tf_op jit(solution)/shard_map/forward/pallas_call | solution.py:816
  116.6 241.6 %backward.1 = (bf16[3136,1024]{1,0:T(8,128)(2,1)}, bf16[512,1024]{1,0:T(8,128)(2,1)}, bf16[2,2,3136,1024]{3,2,1,0:T(8,128)(2,1)}) custom-call(f32[3]{0:T(128)} %pad_maximum_fusion.info_ref, bf16[512,1024]{1,0:T(8,128)(2,1)} %cot_hbm.1, bf16[16,512,256]{2,1,0:T(8,128)(2,1)} %get-tuple-element.28.z_hbm, bf16[16,512,256]{2,1,0:T(8,128)(2,1)} %get-tuple-element.29.slope_hbm, ...), custom_call_target="tpu_custom_call" | custom-call | tf_op jit(solution)/shard_map/backward/pallas_call | solution.py:461
  358.2 0.8 slice_convert_fusion.2
  359.0 0.6 slice.55
  359.6 0.6 slice.53
  360.2 0.6 slice.51
  360.8 0.6 slice.50
  361.4 0.6 slice.61
  362.0 2.1 slice_convert_fusion.1
  364.1 3.3 slice_convert_fusion
  367.4 2.6 slice.56
  370.0 0.4 fusion
  370.4 4.6 %bitcast_convert_fusion = (f32[1024,1024]{1,0:T(8,128)}, f32[1024,1024]{1,0:T(8,128)}) fusion(bf16[4,1,256,1024]{3,2,1,0:T(8,128)(2,1)S(1)} %get-tuple-element.43, bf16[4,1,256,1024]{3,2,1,0:T(8,128)(2,1)S(1)} %get-tuple-element.44), kind=kLoop, calls=%fused_computation | loop fusion | flops 2097152 | bytes 12582912 | tf_op jit(solution)/shard_map/convert_element_type | solution.py:890
  375.1 0.0 copy-start
  375.1 0.0 copy-start.1
  375.1 5.5 %copy.26 = f32[1024,1024]{0,1:T(8,128)} copy(f32[1024,1024]{1,0:T(8,128)} %get-tuple-element.50) | data formatting | bytes 8388608 | tf_op jit(solution)/shard_map/convert_element_type | solution.py:889
  380.6 0.0 copy-done
  380.6 1.0 copy.31
  381.5 0.0 copy-done.1
  381.5 1.0 copy.32
  (1 shorter events, 0.0 us)
Async XLA Ops:
  375.1 5.5 %copy-start = (bf16[512,1024]{1,0:T(8,128)(2,1)S(1)}, bf16[512,1024]{1,0:T(8,128)(2,1)}, u32[]{:S(2)}) copy-start(bf16[512,1024]{1,0:T(8,128)(2,1)} %get-tuple-element.62) | copy-start | bytes 3145732
  375.1 6.5 %copy-start.1 = (bf16[512,1024]{1,0:T(8,128)(2,1)S(1)}, bf16[512,1024]{1,0:T(8,128)(2,1)}, u32[]{:S(2)}) copy-start(bf16[512,1024]{1,0:T(8,128)(2,1)} %get-tuple-element.63) | copy-start | bytes 3145732

commit v3 on v1

v3 whole, which is shorter than its diff:
```python
import functools

import jax
import jax.numpy as jnp
from jax import lax
from jax.experimental import pallas as pl
from jax.experimental.pallas import tpu as pltpu
from jax.sharding import PartitionSpec as P

D = 1024
HDIM = 64
LEN0 = 50
LEN1 = 145
EPSILON = 1e-06
WIDE = 1024
F32 = jnp.float32
BF16 = jnp.bfloat16
MESH = pl.DeviceIdType.MESH
VMEM_BYTES = 62 * 2**20


def split_plan(chunk_rows, bit_count):
    rows, cols, plan = chunk_rows, WIDE, []
    for _ in range(bit_count):
        if rows >= 32:
            rows //= 2
            plan.append(("rows", rows, cols))
        else:
            cols //= 2
            plan.append(("cols", rows, cols))
    return plan


def pipeline_plan(bit_count):
    lag = 2 if bit_count <= 3 else 1
    order = ["core", "x"] + [("bit", b) for b in range(bit_count)] + [("ag", b) for b in reversed(range(bit_count))]
    skews = {stage: 1 if stage == "core" else lag for stage in order}
    when, now = {}, 0
    for stage in order:
        now += skews[stage]
        when[stage] = now
    return skews, when, now


def reduce_scratch(chunk_rows, bit_count):
    plan = split_plan(chunk_rows, bit_count)
    skews, when, _ = pipeline_plan(bit_count)
    slots = {stage: 2 * skew for stage, skew in skews.items()}
    held = when["ag", bit_count - 1] - when["core"] + 1
    return [
        pltpu.VMEM((slots["core"], 2, chunk_rows, WIDE), BF16),
        pltpu.VMEM((slots["core"], 2, chunk_rows, WIDE), BF16),
        pltpu.VMEM((slots["x"], chunk_rows, WIDE), BF16),
        pltpu.VMEM((slots["x"], chunk_rows, WIDE), BF16),
        pltpu.VMEM((held, chunk_rows, WIDE), BF16),
        [pltpu.VMEM((slots["bit", b], r, c), BF16) for b, (_, r, c) in enumerate(plan)],
        pltpu.SemaphoreType.DMA((2, slots["core"])),
        pltpu.SemaphoreType.DMA((2, slots["core"])),
        pltpu.SemaphoreType.DMA((2, slots["x"])),
        [pltpu.SemaphoreType.DMA((2, slots["bit", b])) for b in range(bit_count)],
        [pltpu.SemaphoreType.DMA((2, slots["ag", b])) for b in range(bit_count)],
    ]


def greet(peers):
    barrier = pltpu.get_barrier_semaphore()
    for peer in peers:
        pl.semaphore_signal(barrier, inc=1, device_id=peer, device_id_type=MESH)
    pl.semaphore_wait(barrier, len(peers))


def reduction(chunk_rows, chunk_count, bit_count, g_ref, out_ref, load, core_in, x_out, x_in, acc, bit_in,
              local_sem, core_sem, x_sem, bit_sem, ag_sem):
    dp, f = lax.axis_index("dp"), lax.axis_index("fsdp")
    core, across = lax.rem(f, 2), f // 2
    plan = split_plan(chunk_rows, bit_count)
    skews, when, depth = pipeline_plan(bit_count)
    slot = lambda stage, j: lax.rem(j, 2 * skews[stage])
    held = lambda j: lax.rem(j, acc.shape[0])
    bits = [lax.rem(dp // (1 << b), 2) for b in range(bit_count)]
    flips = [dp + (1 - 2 * bits[b]) * (1 << b) for b in range(bit_count)]
    core_peer = (dp, f + 1 - 2 * core)
    x_peer = (dp, f + 2 - 4 * across)
    peers = [core_peer, x_peer] + [(p, f) for p in flips]

    def region(level, other):
        row, col, rows, cols = 0, 0, chunk_rows, WIDE
        for b in range(level):
            kind, rows, cols = plan[b]
            bit = 1 - bits[b] if other and b == level - 1 else bits[b]
            if kind == "rows":
                row = row + bit * rows
            else:
                col = col + bit * cols
        return row, rows, col, cols

    def cut(ref, lead, base, level, other):
        row, rows, col, cols = region(level, other)
        row_slice = pl.ds(pl.multiple_of(base + row, 16), rows)
        col_slice = slice(None) if cols == WIDE else pl.ds(pl.multiple_of(col, 128), cols)
        return ref.at[lead + (row_slice, col_slice)]

    def rows_of(j):
        return pl.ds(pl.multiple_of(j * chunk_rows, chunk_rows), chunk_rows)

    def remote(src, dst, sems, slot, peer):
        return pltpu.make_async_remote_copy(src, dst, sems.at[0, slot], sems.at[1, slot], device_id=peer,
                                            device_id_type=MESH)

    def load_copy(j):
        s = slot("core", j)
        return pltpu.make_async_copy(g_ref.at[core, :, rows_of(j), :], load.at[s], local_sem.at[0, s])

    def core_copy(j):
        s = slot("core", j)
        return remote(g_ref.at[1 - core, :, rows_of(j), :], core_in.at[s], core_sem, s, core_peer)

    def x_copy(j):
        s = slot("x", j)
        return remote(x_out.at[s], x_in.at[s], x_sem, s, x_peer)

    def bit_copy(b, j):
        s = slot(("bit", b), j)
        return remote(cut(acc, (held(j),), 0, b + 1, True), bit_in[b].at[s], bit_sem[b], s, (flips[b], f))

    def own_copy(j):
        return pltpu.make_async_copy(cut(acc, (held(j),), 0, bit_count, False),
                                     cut(out_ref, (), j * chunk_rows, bit_count, False),
                                     local_sem.at[1, slot("core", j)])

    def ag_copy(b, j):
        mine = cut(out_ref, (), j * chunk_rows, b + 1, False)
        src = cut(acc, (held(j),), 0, bit_count, False) if b == bit_count - 1 else mine
        return remote(src, mine, ag_sem[b], slot(("ag", b), j), (flips[b], f))

    def guarded(t, delay, action):
        j = t - delay

        @pl.when(jnp.logical_and(j >= 0, j < chunk_count))
        def _():
            action(j)

    def on_ag(b):
        def action(j):
            if b == bit_count - 1:
                own_copy(j).wait()
            ag_copy(b, j).wait()
            if b > 0:
                ag_copy(b - 1, j).start()
        return action

    def on_bit(b):
        def action(j):
            bit_copy(b, j).wait()
            mine = cut(acc, (held(j),), 0, b + 1, False)
            mine[...] = (mine[...].astype(F32) + bit_in[b][slot(("bit", b), j)].astype(F32)).astype(BF16)
            if b + 1 < bit_count:
                bit_copy(b + 1, j).start()
            else:
                ag_copy(b, j).start()
                own_copy(j).start()
        return action

    def on_x(j):
        x_copy(j).wait()
        s = held(j)
        acc[s] = (acc[s].astype(F32) + x_in[slot("x", j)].astype(F32)).astype(BF16)
        bit_copy(0, j).start()

    def on_core(j):
        load_copy(j).wait()
        core_copy(j).wait()
        s = slot("core", j)
        for piece, target in ((1 - across, x_out.at[slot("x", j)]), (across, acc.at[held(j)])):
            target[...] = (load[s, piece].astype(F32) + core_in[s, piece].astype(F32)).astype(BF16)
        x_copy(j).start()

    def on_start(j):
        load_copy(j).start()
        core_copy(j).start()

    def tick(t):
        for b in range(bit_count):
            guarded(t, when["ag", b], on_ag(b))
        for b in reversed(range(bit_count)):
            guarded(t, when["bit", b], on_bit(b))
        guarded(t, when["x"], on_x)
        guarded(t, when["core"], on_core)
        guarded(t, 0, on_start)

    return tick, chunk_count + depth, peers


def dot_nn(a, b):
    return lax.dot_general(a, b, (((1,), (0,)), ((), ())), preferred_element_type=F32)


def dot_nt(a, b):
    return lax.dot_general(a, b, (((1,), (1,)), ((), ())), preferred_element_type=F32)


def lanes(index, width):
    return pl.ds(pl.multiple_of(index * width, width), width)


def half_mask(shape, dim, half):
    spot = lax.broadcasted_iota(jnp.int32, shape, dim)
    return spot < HDIM if half == 0 else spot >= HDIM


def fill_bias(bias, inverse, limit, rows):
    step = 128

    def segments(dim, shape, start):
        place = (lax.broadcasted_iota(jnp.int32, shape, dim) + start).astype(F32)
        return jnp.where(place < limit, jnp.floor((place + 0.5) * inverse), float(rows))

    for i in range(rows // step):
        same = segments(0, (step, rows), i * step) == segments(1, (step, rows), 0)
        bias[i * step : (i + 1) * step, :] = jnp.where(same, 0.0, -1e30)


ERF_TOP = (-2.72614225801306e-10, 2.77068142495902e-08, -2.10102402082508e-06, -5.69250639462346e-05,
           -7.34990630326855e-04, -2.95459980854025e-03, -1.60960333262415e-02)
ERF_BOTTOM = (-1.45660718464996e-05, -2.13374055278905e-04, -1.68282697438203e-03, -7.37332916720468e-03,
              -1.42647390514189e-02)


def erf(v):
    v = jnp.clip(v, -4.0, 4.0)
    square = v * v
    top, bottom = ERF_TOP[0], ERF_BOTTOM[0]
    for c in ERF_TOP[1:]:
        top = top * square + c
    for c in ERF_BOTTOM[1:]:
        bottom = bottom * square + c
    return v * top / bottom


PARTS = 3
PART_ROWS = 336
PIECE_ROWS = 48
PIECES = PART_ROWS // PIECE_ROWS
COUNT = 4 * PIECES
REST = PARTS * PART_ROWS
WINDOW = 4
Y_LAG = Z_LAG = 2


def layer_kernel(rows, chunk_rows, chunk_count, bit_count, share, group_ref, images_ref, counts_ref, tok_hbm, cot_hbm,
                 gain_hbm, shift_hbm, qvb_hbm, outb_hbm, upb_hbm, sqkv, so, su, sd,
                 out_hbm, gtok_hbm, sum_hbm, g_hbm,
                 wqkv, wo, wu, wd, x, h1, qkv, o, x1, h2, z, slope, y, bias, lse, dy, dh, da, stage,
                 smalls, pack, vec, vecs, qv, upb, grads, upg,
                 own_sem, vec_sem, rest_sem, x_sem, y_sem, z_sem, fx_sem, fy_sem, fz_sem, frest_sem, core_sem,
                 load_sem, save_sem, stage_sem, comm):
    tick, tick_count, peers = reduction(chunk_rows, chunk_count, bit_count, g_hbm, sum_hbm, *comm)
    ratio = chunk_rows // 64

    def beat(i):
        if ratio == 1:
            tick(i)
        else:
            @pl.when(lax.rem(i, ratio) == ratio - 1)
            def _():
                tick(i // ratio)

    dp, f = lax.axis_index("dp"), lax.axis_index("fsdp")
    core, across = lax.rem(f, 2), f // 2
    yb, zb = lax.rem(dp, 2), lax.rem(dp // 2, 2)
    core_f, x_f, diag_f = f + 1 - 2 * core, f + 2 - 4 * across, 3 - f
    core_peer, x_peer, diag_peer = (dp, core_f), (dp, x_f), (dp, diag_f)
    y_peer, z_peer = (dp + 1 - 2 * yb, f), (dp + 2 - 4 * zb, f)
    part_x = yb + (1 - yb) * 2 * zb
    part_y = (1 - yb) + yb * 2 * zb
    part_z = 2 - 2 * zb
    shards, full = (sqkv, so, su, sd), (wqkv, wo, wu, wd)

    def order(i):
        return 2 * lax.rem(across + i // 2, 2) + lax.rem(core + i, 2)

    def remote(src, dst, sems, slot, peer):
        return pltpu.make_async_remote_copy(src, dst, sems.at[0, slot], sems.at[1, slot], device_id=peer,
                                            device_id_type=MESH)

    def part(k, index):
        return pl.ds(pl.multiple_of(index * PART_ROWS + (k % PIECES) * PIECE_ROWS, 16), PIECE_ROWS)

    rest = pl.ds(REST, D - REST)

    def x_copy(k):
        w, at = k // PIECES, part(k, part_x)
        return remote(shards[w].at[at, :], full[w].at[f, at, :], x_sem, k, x_peer)

    def hop(k, index, sems, peer):
        w, at = k // PIECES, part(k, index)
        return remote(full[w].at[x_f, at, :], full[w].at[x_f, at, :], sems, k, peer)

    y_copy = lambda k: hop(k, part_x, y_sem, y_peer)
    z_copy = lambda k: hop(k, 2 * zb, z_sem, z_peer)
    fx_copy = lambda k: hop(k, part_x, fx_sem, core_peer)
    fy_copy = lambda k: hop(k, part_y, fy_sem, core_peer)
    fz_copy = lambda k: hop(k, part_z, fz_sem, core_peer)

    def rest_copy(w):
        return remote(shards[w].at[rest, :], full[w].at[f, rest, :], rest_sem, w, x_peer)

    def frest_copy(w):
        return remote(full[w].at[x_f, rest, :], full[w].at[x_f, rest, :], frest_sem, w, core_peer)

    def core_copy(w):
        return remote(shards[w], full[w].at[f], core_sem, w, core_peer)

    def own_copy(w):
        return pltpu.make_async_copy(shards[w], full[w].at[f], own_sem.at[w])

    def service(k):
        i = k - Y_LAG - Z_LAG
        if 0 <= i < COUNT:
            z_copy(i).wait_recv()
            fz_copy(i).start()
        i = k - Y_LAG
        if 0 <= i < COUNT:
            y_copy(i).wait_recv()
            fy_copy(i).start()

            @pl.when(yb == 1)
            def _():
                z_copy(i).start()
        if k < COUNT:
            x_copy(k).wait_recv()
            y_copy(k).start()

            @pl.when(yb == 0)
            def _():
                z_copy(k).start()

            fx_copy(k).start()
            if k + WINDOW < COUNT:
                x_copy(k + WINDOW).start()
            if k % PIECES == 0:
                w = k // PIECES
                rest_copy(w).wait_recv()
                frest_copy(w).start()

    def services(index, plan):
        for i, k in plan:
            @pl.when(index == i)
            def _(k=k):
                service(k)

    def arrived(w):
        frest_copy(w).wait_recv()
        for k in range(w * PIECES, (w + 1) * PIECES):
            fx_copy(k).wait_recv()
            fy_copy(k).wait_recv()
            fz_copy(k).wait_recv()

    loads = [pltpu.make_async_copy(src, dst, load_sem.at[i]) for i, (src, dst) in enumerate(
        [(gain_hbm, smalls[0]), (shift_hbm, smalls[1]), (qvb_hbm, smalls[2]), (outb_hbm, smalls[3]), (upb_hbm, smalls[4]),
         (tok_hbm, x), (cot_hbm, dy)])]
    for copy in loads:
        copy.start()
    for w in range(4):
        own_copy(w).start()
    greet(peers + [diag_peer])
    for k in range(WINDOW):
        x_copy(k).start()
    core_copy(0).start()
    for w in range(4):
        rest_copy(w).start()
    for copy in loads[:5]:
        copy.wait()
    pack[...] = jnp.zeros_like(pack)
    for i in range(4):
        pack[2 * i : 2 * i + 2, :] = smalls[i][...].astype(F32)
    pack[8:12, :] = smalls[4][...].astype(F32)
    vec[f] = pack[...].astype(BF16)
    vec_copies = [remote(vec.at[f], vec.at[f], vec_sem, i, peer)
                  for i, peer in enumerate((core_peer, x_peer, diag_peer))]
    for copy in vec_copies:
        copy.start()
    for w in range(1, 4):
        core_copy(w).start()

    first = group_ref[0] == 0
    length = jnp.where(first, LEN0, LEN1)
    inverse = jnp.where(first, 1.0 / LEN0, 1.0 / LEN1).astype(F32)
    limit = (images_ref[0, 0] * length).astype(F32)
    mine = jnp.where(first, counts_ref[0], counts_ref[1])
    fraction = jnp.full((1, 128), mine, jnp.int32).astype(F32) / jnp.full(
        (1, 128), counts_ref[0] + counts_ref[1], jnp.int32).astype(F32)
    factor = fraction[0:1, 0:1] * share
    fill_bias(bias, inverse, limit, rows)
    for copy in vec_copies:
        copy.wait()
    qv[...] = jnp.zeros_like(qv)
    for g in range(4):
        wide = vec[g].astype(F32)
        for i in range(8):
            vecs[i, :, 256 * g : 256 * g + 256] = wide[i : i + 1, :]
        for i in range(4):
            upb[4 * g + i] = wide[8 + i : 9 + i, :]
        for i in range(2):
            qv[2 * g + i] = wide[4:5, 128 * i : 128 * i + 128]
            qv[16 + 2 * g + i] = wide[5:6, 128 * i : 128 * i + 128]

    step = 64

    def normalize(value, which):
        center = value - jnp.mean(value, axis=-1, keepdims=True)
        spread = jnp.mean(center * center, axis=-1, keepdims=True)
        return (center * lax.rsqrt(spread + EPSILON) * vecs[which] + vecs[2 + which]).astype(BF16)

    loads[5].wait()

    def norm_in(i, carry):
        at = pl.ds(pl.multiple_of(i * step, step), step)
        h1[at, :] = normalize(x[at, :].astype(F32), 0)
        return carry

    lax.fori_loop(0, rows // step, norm_in, 0)

    def project(i):
        product = dot_nn(h1[...], wqkv[order(i)])
        for b in range(6):
            block = 6 * order(i) + b
            scale = jnp.where(block < 8, HDIM ** (-0.5), 1.0).astype(F32)
            qkv[block] = ((product[:, 128 * b : 128 * b + 128] + qv[block]) * scale).astype(BF16)

    own_copy(0).wait()
    project(0)
    service(0)
    core_copy(0).wait_recv()
    service(1)
    project(1)
    for k in range(2, PIECES + Y_LAG + Z_LAG):
        service(k)
    loads[6].wait()
    live = lax.broadcasted_iota(jnp.int32, (rows, D), 0).astype(F32) < limit
    dy[...] = jnp.where(live, dy[...].astype(F32), 0.0).astype(BF16)
    arrived(0)
    project(2)
    for k in range(11, 15):
        service(k)
    project(3)
    for k in range(15, 18):
        service(k)

    def heads(p, carry):
        services(p, ((0, 18), (2, 19), (3, 20), (5, 21), (6, 22)))
        q_pair, k_pair, v_turned = qkv[p], qkv[8 + p], qkv[16 + p].T
        total = jnp.zeros((128, rows), F32)
        for half in range(2):
            q_half = jnp.where(half_mask((rows, 128), 1, half), q_pair, jnp.zeros_like(q_pair))
            v_half = jnp.where(half_mask((128, rows), 0, half), v_turned, jnp.zeros_like(v_turned))
            scores = dot_nt(k_pair, q_half) + bias[...]
            highest = jnp.max(scores, axis=0, keepdims=True)
            weights = jnp.exp(scores - highest)
            sums = jnp.sum(weights, axis=0, keepdims=True)
            total += dot_nn(v_half, (weights * (1.0 / sums)).astype(BF16))
            lse[p, half] = highest + jnp.log(sums)
        o[:, lanes(p, 128)] = total.T.astype(BF16)
        return carry

    lax.fori_loop(0, 8, heads, 0)
    for w in range(1, 4):
        own_copy(w).wait()
        core_copy(w).wait_recv()
    arrived(1)
    for g in range(4):
        at = slice(256 * g, 256 * g + 256)
        x1[:, at] = x[:, at].astype(F32) + dot_nn(o[...], wo[g]) + vecs[6, :, at]
    service(23)

    def norm_mid(i, carry):
        at = pl.ds(pl.multiple_of(i * step, step), step)
        value = x1[at, :]
        h2[at, :] = normalize(value, 1)
        y[at, :] = value + vecs[7]
        return carry

    lax.fori_loop(0, rows // step, norm_mid, 0)
    service(24)

    def hidden(i, carry):
        services(i, ((2, 25), (4, 26), (6, 27)))

        @pl.when(i == 8)
        def _():
            arrived(2)

        q, g = lax.rem(i, 4), order(i // 4)
        n = 4 * q + g
        u = dot_nn(h2[...], wu[g, :, lanes(q, 256)]) + upb[4 * g + q]
        bell = 0.5 + 0.5 * erf(u * (0.5 ** 0.5))
        z[n] = (u * bell).astype(BF16)
        slope[n] = (bell + u * (jnp.exp(-0.5 * u * u) * 0.3989422804014327)).astype(BF16)
        return carry

    lax.fori_loop(0, 16, hidden, 0)

    def stage_copy(which, n):
        s, q, g = lax.rem(n, 2), n // 4, lax.rem(n, 4)
        at = pl.ds(pl.multiple_of(which * D + q * 256, 256), 256)
        return pltpu.make_async_copy(stage.at[s], g_hbm.at[lax.rem(g, 2), g // 2, at, :], stage_sem.at[s])

    def flush(which, n):
        @pl.when(n >= 1)
        def _():
            stage_copy(which, n - 1).wait()

    def down_grad(n, carry):
        services(n, ((1, 28), (4, 29), (8, 30), (12, 31)))
        flush(0, n)
        stage[lax.rem(n, 2)] = (dot_nn(z[n].T, dy[...]) * factor).astype(BF16)
        stage_copy(0, n).start()
        for i in range(4):
            @pl.when(n == 4 + 3 * i)
            def _(i=i):
                beat(i)
        return carry

    lax.fori_loop(0, 16, down_grad, 0)
    stage_copy(0, 15).wait()
    arrived(3)
    dh[...] = jnp.zeros_like(dh)

    def ffn_back(n, carry):
        q, g = n // 4, lax.rem(n, 4)
        flush(1, n)
        beat(4 + n)
        du = dot_nt(dy[...], wd[g, lanes(q, 256), :]) * slope[n].astype(F32)
        low = du.astype(BF16)
        upg[n] = jnp.sum(low.astype(F32), axis=0, keepdims=True)
        stage[lax.rem(n, 2)] = (dot_nn(low.T, h2[...]) * factor).astype(BF16)
        stage_copy(1, n).start()
        dh[...] += dot_nt(low, wu[g, :, lanes(q, 256)])
        y[...] += dot_nn(z[n], wd[g, lanes(q, 256), :])
        return carry

    lax.fori_loop(0, 16, ffn_back, 0)
    stage_copy(1, 15).wait()
    out_copies = []
    for c in range(4):
        slope[c] = y[:, 256 * c : 256 * c + 256].astype(BF16)
        out_copies.append(pltpu.make_async_copy(slope.at[c], out_hbm.at[:, pl.ds(256 * c, 256)], save_sem.at[c]))
        out_copies[-1].start()
    beat(20)
    grads[...] = jnp.zeros_like(grads)

    def norm_back(base_ref, which, first_beat, finish):
        def body(i, carry):
            at = pl.ds(pl.multiple_of(i * step, step), step)
            v = base_ref[at, :].astype(F32)
            center = v - jnp.mean(v, axis=-1, keepdims=True)
            rstd = lax.rsqrt(jnp.mean(center * center, axis=-1, keepdims=True) + EPSILON)
            hat = center * rstd
            grad = dh[at, :]
            grads[which] += jnp.sum(grad * hat, axis=0, keepdims=True)
            grads[2 + which] += jnp.sum(grad, axis=0, keepdims=True)
            scaled = grad * vecs[which]
            finish(at, rstd * (scaled - jnp.mean(scaled, axis=-1, keepdims=True)
                               - hat * jnp.mean(scaled * hat, axis=-1, keepdims=True)))

            @pl.when(i == 4)
            def _():
                beat(first_beat)

            return carry

        lax.fori_loop(0, rows // step, body, 0)

    dx1 = y

    def finish_mlp(at, dx):
        dy_part = dy[at, :].astype(F32)
        total = dy_part + dx
        low = total.astype(BF16)
        dx1[at, :] = total
        da[at, :] = low
        grads[6] += jnp.sum(low.astype(F32), axis=0, keepdims=True)
        grads[7] += jnp.sum(dy_part, axis=0, keepdims=True)

    norm_back(x1, 1, 21, finish_mlp)
    for c in range(4):
        total = jnp.zeros((rows, 256), F32)
        for g in range(4):
            total += dot_nt(da[:, 256 * g : 256 * g + 256], wo[g, 256 * c : 256 * c + 256, :])
        slope[4 + c] = total.astype(BF16)
    beat(22)

    def heads_back(p, carry):
        beat(23 + p)
        at = lanes(lax.rem(p, 2), 128)
        q_pair, k_pair, v_pair, do_pair = qkv[p], qkv[8 + p], qkv[16 + p], slope[4 + p // 2, :, at]
        k_turned = k_pair.T
        dk = jnp.zeros((rows, 128), F32)
        dv = jnp.zeros((rows, 128), F32)
        dq = jnp.zeros((128, rows), F32)
        for half in range(2):
            mask = half_mask((rows, 128), 1, half)
            q_half = jnp.where(mask, q_pair, jnp.zeros_like(q_pair))
            do_half = jnp.where(mask, do_pair, jnp.zeros_like(do_pair))
            k_half = jnp.where(half_mask((128, rows), 0, half), k_turned, jnp.zeros_like(k_turned))
            scores = dot_nt(k_pair, q_half) + bias[...]
            weights = jnp.exp(scores - lse[p, half])
            grad = dot_nt(v_pair, do_half)
            inner = jnp.sum(weights * grad, axis=0, keepdims=True)
            low = weights.astype(BF16)
            ds = (weights * (grad - inner)).astype(BF16)
            dv += dot_nn(low, do_half)
            dk += dot_nn(ds, q_half)
            dq += dot_nn(k_half, ds)
        for i, value in ((0, dq.T * HDIM ** (-0.5)), (1, dk), (2, dv)):
            low = value.astype(BF16)
            z[4 * i + p // 2, :, at] = low
            if i != 1:
                grads[4 + i // 2, :, lanes(p, 128)] = jnp.sum(low.astype(F32), axis=0, keepdims=True)
        return carry

    lax.fori_loop(0, 8, heads_back, 0)

    def proj_grad(n, carry):
        s, q, g = lax.rem(n, 2), n // 4, lax.rem(n, 4)
        flush(2, n)
        left = h1[:, lanes(q, 256)].T
        for b in range(3):
            stage[s, :, 256 * b : 256 * b + 256] = (dot_nn(left, z[3 * g + b]) * factor).astype(BF16)
        stage[s, :, 768:1024] = (dot_nn(o[:, lanes(q, 256)].T, da[:, lanes(g, 256)]) * factor).astype(BF16)
        stage_copy(2, n).start()
        for i in range(5):
            @pl.when(n == (1, 5, 8, 11, 14)[i])
            def _(i=i):
                beat(31 + i)
        return carry

    lax.fori_loop(0, 16, proj_grad, 0)
    stage_copy(2, 15).wait()
    for c in range(4):
        total = jnp.zeros((rows, 256), F32)
        for g in range(4):
            for b in range(3):
                total += dot_nt(z[3 * g + b], wqkv[g, 256 * c : 256 * c + 256, 256 * b : 256 * b + 256])
        dh[:, 256 * c : 256 * c + 256] = total
        if c % 2 == 1:
            beat(36 + c // 2)

    def finish_attn(at, dx):
        x[at, :] = (dx1[at, :] + dx).astype(BF16)

    norm_back(x, 0, 38, finish_attn)
    out_copies.append(pltpu.make_async_copy(x, gtok_hbm, save_sem.at[4]))
    out_copies[-1].start()
    beat(39)
    tail_copies = []
    for g in range(4):
        tail = stage.at[g // 2, pl.ds(128 * (g % 2), chunk_rows), :]
        tail[...] = jnp.zeros((chunk_rows, WIDE), BF16)
        for i in range(8):
            tail[2 * i : 2 * i + 1, 0:256] = (grads[i, :, 256 * g : 256 * g + 256] * factor).astype(BF16)
        for q in range(4):
            tail[16:17, 256 * q : 256 * q + 256] = (upg[4 * q + g] * factor).astype(BF16)
        tail_copies.append(pltpu.make_async_copy(tail, g_hbm.at[g % 2, g // 2, pl.ds(3072, chunk_rows), :],
                                                 save_sem.at[5 + g]))
        tail_copies[-1].start()
    for copy in tail_copies:
        copy.wait()

    def remaining(t, carry):
        tick(t)
        return carry

    lax.fori_loop(40 // ratio, tick_count, remaining, 0)
    for copy in out_copies:
        copy.wait()
    for k in range(COUNT):
        for copy in (x_copy(k), y_copy(k), z_copy(k), fx_copy(k), fy_copy(k), fz_copy(k)):
            copy.wait_send()
    for w in range(4):
        for copy in (rest_copy(w), frest_copy(w), core_copy(w)):
            copy.wait_send()


def layer(dp_size, fsdp_size, group, images, counts, tokens, cotangent, small_params, weights):
    rows = tokens.shape[0]
    chunk_rows = 64 if dp_size <= 32 else 128
    chunk_count = 3072 // chunk_rows + 1
    bit_count = dp_size.bit_length() - 1
    g_rows = 3072 + chunk_rows
    any_space, smem = pl.BlockSpec(memory_space=pl.ANY), pl.BlockSpec(memory_space=pltpu.SMEM)
    sems = lambda *dims: pltpu.SemaphoreType.DMA(dims)
    shape = jax.ShapeDtypeStruct
    return pl.pallas_call(
        functools.partial(layer_kernel, rows, chunk_rows, chunk_count, bit_count, 2.0 / (dp_size * fsdp_size)),
        out_shape=(
            shape((rows, D), BF16), shape((rows, D), BF16), shape((g_rows, WIDE), BF16),
            shape((2, 2, g_rows, WIDE), BF16),
        ),
        in_specs=[smem] * 3 + [any_space] * 11,
        out_specs=(any_space,) * 4,
        scratch_shapes=[pltpu.VMEM((4,) + a.shape, BF16) for a in weights] + [
            pltpu.VMEM((rows, D), BF16),
            pltpu.VMEM((rows, D), BF16),
            pltpu.VMEM((24, rows, 128), BF16),
            pltpu.VMEM((rows, D), BF16),
            pltpu.VMEM((rows, D), F32),
            pltpu.VMEM((rows, D), BF16),
            pltpu.VMEM((16, rows, 256), BF16),
            pltpu.VMEM((16, rows, 256), BF16),
            pltpu.VMEM((rows, D), F32),
            pltpu.VMEM((rows, rows), F32),
            pltpu.VMEM((8, 2, 1, rows), F32),
            pltpu.VMEM((rows, D), BF16),
            pltpu.VMEM((rows, D), F32),
            pltpu.VMEM((rows, D), BF16),
            pltpu.VMEM((2, 256, WIDE), BF16),
            [pltpu.VMEM(a.shape, BF16) for a in small_params],
            pltpu.VMEM((16, 256), F32),
            pltpu.VMEM((4, 16, 256), BF16),
            pltpu.VMEM((8, 1, D), F32),
            pltpu.VMEM((24, 1, 128), F32),
            pltpu.VMEM((16, 1, 256), F32),
            pltpu.VMEM((8, 1, D), F32),
            pltpu.VMEM((16, 1, 256), F32),
            sems(4), sems(2, 3), sems(2, 4),
            sems(2, COUNT), sems(2, COUNT), sems(2, COUNT), sems(2, COUNT), sems(2, COUNT), sems(2, COUNT),
            sems(2, 4), sems(2, 4), sems(7), sems(9), sems(2),
            reduce_scratch(chunk_rows, bit_count),
        ],
        compiler_params=pltpu.CompilerParams(collective_id=1, has_side_effects=True, vmem_limit_bytes=VMEM_BYTES),
        name="layer",
    )(group, images, counts, tokens, cotangent, *small_params, *weights)


def widen_kernel(down_ref, up_ref, proj_ref, small_ref, gain_ref, shift_ref, qkv_ref, qvb_ref, wo_ref, outb_ref, wu_ref,
                 upb_ref, wd_ref):
    wd_ref[...] = down_ref[...].astype(F32)
    wu_ref[...] = up_ref[...].T.astype(F32)
    proj = proj_ref[...].astype(F32)
    qkv_ref[...] = proj[:, :768]
    wo_ref[...] = proj[:, 768:]
    small = small_ref[...].astype(F32)
    for i, ref in enumerate((gain_ref, shift_ref, qvb_ref, outb_ref)):
        for j in range(2):
            ref[j : j + 1, :] = small[4 * i + 2 * j : 4 * i + 2 * j + 1, 0:256]
    upb_ref[...] = small[16:17, :]


def widen(total):
    steps = 4
    block = D // steps
    shape = jax.ShapeDtypeStruct
    fixed = lambda *dims: pl.BlockSpec(dims, lambda i: (0, 0))
    return pl.pallas_call(
        widen_kernel,
        grid=(steps,),
        out_shape=(
            shape((2, 256), F32), shape((2, 256), F32), shape((D, 768), F32), shape((2, 256), F32), shape((D, 256), F32),
            shape((2, 256), F32), shape((D, D), F32), shape((1, D), F32), shape((D, D), F32),
        ),
        in_specs=[
            pl.BlockSpec((block, WIDE), lambda i: (i, 0)),
            pl.BlockSpec((block, WIDE), lambda i: (steps + i, 0)),
            pl.BlockSpec((block, WIDE), lambda i: (2 * steps + i, 0)),
            pl.BlockSpec((32, WIDE), lambda i: (3072 // 32, 0)),
        ],
        out_specs=(
            fixed(2, 256), fixed(2, 256), pl.BlockSpec((block, 768), lambda i: (i, 0)), fixed(2, 256),
            pl.BlockSpec((block, 256), lambda i: (i, 0)), fixed(2, 256), pl.BlockSpec((D, block), lambda i: (0, i)),
            fixed(1, D), pl.BlockSpec((block, D), lambda i: (i, 0)),
        ),
        compiler_params=pltpu.CompilerParams(vmem_limit_bytes=32 * 2**20),
        name="widen",
    )(total, total, total, total)


def local(
    tokens,
    cotangent,
    group,
    images,
    counts,
    ln_gain,
    ln_bias,
    w_qkv,
    qv_bias,
    w_out,
    out_bias,
    w_up,
    up_bias,
    w_down,
):
    output, grad_tokens, total, _ = layer(
        lax.axis_size("dp"), lax.axis_size("fsdp"), group, images, counts, tokens, cotangent,
        (ln_gain, ln_bias, qv_bias, out_bias, up_bias.reshape(4, 256)), (w_qkv, w_out, w_up, w_down))
    grads = list(widen(total))
    grads[7] = grads[7].reshape(D)
    return (output, grad_tokens, *grads)


def solution(mesh):
    return jax.shard_map(
        local,
        mesh=mesh,
        in_specs=(
            P(("dp", "fsdp"), None),
            P(("dp", "fsdp"), None),
            P("dp"),
            P("dp", "fsdp"),
            P(),
            P(None, "fsdp"),
            P(None, "fsdp"),
            P(None, "fsdp"),
            P(None, "fsdp"),
            P(None, "fsdp"),
            P(None, "fsdp"),
            P(None, "fsdp"),
            P("fsdp"),
            P("fsdp", None),
        ),
        out_specs=(
            P(("dp", "fsdp"), None),
            P(("dp", "fsdp"), None),
            P(None, "fsdp"),
            P(None, "fsdp"),
            P(None, "fsdp"),
            P(None, "fsdp"),
            P(None, "fsdp"),
            P(None, "fsdp"),
            P(None, "fsdp"),
            P("fsdp"),
            P("fsdp", None),
        ),
        check_vma=False,
    )
```

time: 510 us -> 285 us (0.56); the launches traced: 504 us -> 285 us
  local copies, waits for them, and re-layouts: 95.4 us -> 6.03 us
  matrix products: 65.8 us -> 0 us
  waiting for transfers between devices: 49.6 us -> 0 us
  Pallas kernels: 238 us -> 277 us
  other arithmetic: 31.1 us -> 0 us
  between operations: 18.3 us -> 1.96 us
  blocking collectives: 6.16 us -> 0 us
    dot_general x6 -> x0, matrix products: 65.8 us -> none  [the longest x4 46.6 us: dot_plain(): return jnp.dot(first_op, second_op, preferred_element_type=jnp.float32)]
    all_gather x4 -> x0, waiting for transfers between devices: 47 us -> none  [local(): gather = lambda a: lax.all_gather(a, 'fsdp', axis=0)]
    pallas_call x1 -> x2, Pallas kernels: 238 us -> 277 us  [the longest x1 272 us: layer(): pl.pallas_call(functools.partial(layer_kernel, rows, chunk_rows, chunk_co...]
    reshape x5 -> x0, local copies, waits for them, and re-layouts: 31.9 us -> none  [the longest x4 27.3 us: local(): a.reshape(rows, 4, 4, 256).transpose(2, 1, 0, 3).reshape(16, rows, 256)]
    transpose x3 -> x0, local copies, waits for them, and re-layouts: 25.7 us -> none  [local(): flat = lambda w: w.transpose(1, 0, 2).reshape(D, -1)]
    slice x14 -> x0, local copies, waits for them, and re-layouts: 18.6 us -> none  [the longest x1 4.28 us: local(): blocks[:, 0].reshape(D, D)]
    convert_element_type x7 -> x0, other arithmetic: 14.8 us -> none  [the longest x1 9.77 us: local(): z = gelu.astype(BF16)]
    reduce_sum x4 -> x0, other arithmetic: 10.2 us -> none  [the longest x1 9.25 us: local(): totals = jnp.sum(weights, axis=-1, keepdims=True)]
  transfers between devices with their start and end apart: 4 -> 0, of which waited for: 2 -> 0; matrix products, arithmetic and copies ran while one was open for 32% -> 0% of each run, Pallas kernels for 0% -> 0%
where the time goes in v3:
time: 285 us
  Pallas kernels  277 us (97%)
  local copies, waits for them, and re-layouts  6.03 us (2%)
    pallas_call x1, Pallas kernels, layer(): pl.pallas_call(functools.partial(layer_kernel, rows, chunk_rows, chunk_co...  272 us

profile of v3, /device:TPU:0, one launch (start us, length us, event | category | flops | bytes accessed | tf_op | source)
XLA Modules:
  0.0 285.0 jit_solution(15413420150096753479)
XLA Ops:
  1.9 1.3 reshape.28.upb_hbm
  3.2 272.3 %layer.1 = (bf16[512,1024]{1,0:T(8,128)(2,1)}, bf16[512,1024]{1,0:T(8,128)(2,1)}, bf16[3136,1024]{1,0:T(8,128)(2,1)}, bf16[2,2,3136,1024]{3,2,1,0:T(8,128)(2,1)}) custom-call(s32[1]{0:T(128)S(6)} %copy.27.group_ref, s32[1,1]{1,0:T(1,128)S(6)} %copy.28.images_ref, s32[2]{0:T(128)} %counts_ref.1, bf16[512,1024]{1,0:T(8,128)(2,1)} %tok_hbm.1, ...), custom_call_target="tpu_custom_call" | custom-call | tf_op jit(solution)/shard_map/layer/pallas_call | solution.py:694
  275.5 0.0 copy-start
  275.5 2.8 copy-done
  278.3 0.0 copy-start.2
  278.3 0.0 copy-start.1
  278.3 4.8 %widen.1 = (f32[2,256]{1,0:T(2,128)}, f32[2,256]{1,0:T(2,128)}, f32[1024,768]{1,0:T(8,128)}, f32[2,256]{1,0:T(2,128)}, f32[1024,256]{1,0:T(8,128)}, /*index=5*/f...) custom-call(bf16[3136,1024]{1,0:T(8,128)(2,1)S(1)} %copy-done, ...), custom_call_target="tpu_custom_call" | custom-call | tf_op jit(solution)/shard_map/widen/pallas_call | solution.py:755
  283.1 0.0 copy-done.2
  283.1 1.0 copy.29
  284.0 0.0 copy-done.1
  284.0 1.0 copy.30
Async XLA Ops:
  275.5 2.8 copy-start
  278.3 4.8 %copy-start.2 = (bf16[512,1024]{1,0:T(8,128)(2,1)S(1)}, bf16[512,1024]{1,0:T(8,128)(2,1)}, u32[]{:S(2)}) copy-start(bf16[512,1024]{1,0:T(8,128)(2,1)} %get-tuple-element.46) | copy-start | bytes 3145732
  278.3 5.7 %copy-start.1 = (bf16[512,1024]{1,0:T(8,128)(2,1)S(1)}, bf16[512,1024]{1,0:T(8,128)(2,1)}, u32[]{:S(2)}) copy-start(bf16[512,1024]{1,0:T(8,128)(2,1)} %get-tuple-element.47) | copy-start | bytes 3145732

commit v4 on v3

--- a/solution.py
+++ b/solution.py
@@ -220,21 +220,17 @@
         bias[i * step : (i + 1) * step, :] = jnp.where(same, 0.0, -1e30)
 
 
-ERF_TOP = (-2.72614225801306e-10, 2.77068142495902e-08, -2.10102402082508e-06, -5.69250639462346e-05,
-           -7.34990630326855e-04, -2.95459980854025e-03, -1.60960333262415e-02)
-ERF_BOTTOM = (-1.45660718464996e-05, -2.13374055278905e-04, -1.68282697438203e-03, -7.37332916720468e-03,
-              -1.42647390514189e-02)
-
-
-def erf(v):
-    v = jnp.clip(v, -4.0, 4.0)
-    square = v * v
-    top, bottom = ERF_TOP[0], ERF_BOTTOM[0]
-    for c in ERF_TOP[1:]:
-        top = top * square + c
-    for c in ERF_BOTTOM[1:]:
-        bottom = bottom * square + c
-    return v * top / bottom
+ERF_TERMS = (1.061405429, -1.453152027, 1.421413741, -0.284496736, 0.254829592)
+
+
+def normal_share(u):
+    fall = jnp.exp(u * u * -0.5)
+    t = 1.0 / (1.0 + jnp.abs(u) * (0.3275911 * 0.5 ** 0.5))
+    series = ERF_TERMS[0] * t
+    for c in ERF_TERMS[1:-1]:
+        series = (series + c) * t
+    tail = 0.5 * (series + ERF_TERMS[-1]) * t * fall
+    return jnp.where(u < 0.0, tail, 1.0 - tail), fall
 
 
 PARTS = 3
@@ -243,7 +239,7 @@
 PIECES = PART_ROWS // PIECE_ROWS
 COUNT = 4 * PIECES
 REST = PARTS * PART_ROWS
-WINDOW = 4
+WINDOWS = (2, 4)
 Y_LAG = Z_LAG = 2
 
 
@@ -314,6 +310,13 @@
     def own_copy(w):
         return pltpu.make_async_copy(shards[w], full[w].at[f], own_sem.at[w])
 
+    sent = []
+
+    def feed(until):
+        while len(sent) < min(until, COUNT):
+            x_copy(len(sent)).start()
+            sent.append(True)
+
     def service(k):
         i = k - Y_LAG - Z_LAG
         if 0 <= i < COUNT:
@@ -336,8 +339,7 @@
                 z_copy(k).start()
 
             fx_copy(k).start()
-            if k + WINDOW < COUNT:
-                x_copy(k + WINDOW).start()
+            feed(k + 1 + WINDOWS[k >= PIECES - 2])
             if k % PIECES == 0:
                 w = k // PIECES
                 rest_copy(w).wait_recv()
@@ -361,14 +363,8 @@
          (tok_hbm, x), (cot_hbm, dy)])]
     for copy in loads:
         copy.start()
-    for w in range(4):
-        own_copy(w).start()
+    own_copy(0).start()
     greet(peers + [diag_peer])
-    for k in range(WINDOW):
-        x_copy(k).start()
-    core_copy(0).start()
-    for w in range(4):
-        rest_copy(w).start()
     for copy in loads[:5]:
         copy.wait()
     pack[...] = jnp.zeros_like(pack)
@@ -380,8 +376,12 @@
                   for i, peer in enumerate((core_peer, x_peer, diag_peer))]
     for copy in vec_copies:
         copy.start()
+    feed(WINDOWS[0])
+    core_copy(0).start()
+    for w in range(4):
+        rest_copy(w).start()
     for w in range(1, 4):
-        core_copy(w).start()
+        own_copy(w).start()
 
     first = group_ref[0] == 0
     length = jnp.where(first, LEN0, LEN1)
@@ -394,6 +394,7 @@
     fill_bias(bias, inverse, limit, rows)
     for copy in vec_copies:
         copy.wait()
+    service(0)
     qv[...] = jnp.zeros_like(qv)
     for g in range(4):
         wide = vec[g].astype(F32)
@@ -420,6 +421,7 @@
         return carry
 
     lax.fori_loop(0, rows // step, norm_in, 0)
+    service(1)
 
     def project(i):
         product = dot_nn(h1[...], wqkv[order(i)])
@@ -430,25 +432,25 @@
 
     own_copy(0).wait()
     project(0)
-    service(0)
+    service(2)
     core_copy(0).wait_recv()
-    service(1)
     project(1)
-    for k in range(2, PIECES + Y_LAG + Z_LAG):
+    for k in range(3, PIECES + Y_LAG + Z_LAG):
         service(k)
+    for w in range(1, 4):
+        core_copy(w).start()
     loads[6].wait()
     live = lax.broadcasted_iota(jnp.int32, (rows, D), 0).astype(F32) < limit
     dy[...] = jnp.where(live, dy[...].astype(F32), 0.0).astype(BF16)
     arrived(0)
     project(2)
-    for k in range(11, 15):
-        service(k)
     project(3)
-    for k in range(15, 18):
-        service(k)
+    service(11)
+    service(12)
+    service(13)
 
     def heads(p, carry):
-        services(p, ((0, 18), (2, 19), (3, 20), (5, 21), (6, 22)))
+        services(p, ((0, 14), (2, 15), (3, 16), (5, 17), (6, 18), (7, 19)))
         q_pair, k_pair, v_turned = qkv[p], qkv[8 + p], qkv[16 + p].T
         total = jnp.zeros((128, rows), F32)
         for half in range(2):
@@ -458,7 +460,7 @@
             highest = jnp.max(scores, axis=0, keepdims=True)
             weights = jnp.exp(scores - highest)
             sums = jnp.sum(weights, axis=0, keepdims=True)
-            total += dot_nn(v_half, (weights * (1.0 / sums)).astype(BF16))
+            total += dot_nn(v_half, weights.astype(BF16)) * (1.0 / sums)
             lse[p, half] = highest + jnp.log(sums)
         o[:, lanes(p, 128)] = total.T.astype(BF16)
         return carry
@@ -471,7 +473,7 @@
     for g in range(4):
         at = slice(256 * g, 256 * g + 256)
         x1[:, at] = x[:, at].astype(F32) + dot_nn(o[...], wo[g]) + vecs[6, :, at]
-    service(23)
+    service(20)
 
     def norm_mid(i, carry):
         at = pl.ds(pl.multiple_of(i * step, step), step)
@@ -481,10 +483,10 @@
         return carry
 
     lax.fori_loop(0, rows // step, norm_mid, 0)
-    service(24)
+    service(21)
 
     def hidden(i, carry):
-        services(i, ((2, 25), (4, 26), (6, 27)))
+        services(i, ((2, 22), (4, 23), (6, 24), (9, 25), (11, 26), (13, 27), (15, 28)))
 
         @pl.when(i == 8)
         def _():
@@ -493,9 +495,9 @@
         q, g = lax.rem(i, 4), order(i // 4)
         n = 4 * q + g
         u = dot_nn(h2[...], wu[g, :, lanes(q, 256)]) + upb[4 * g + q]
-        bell = 0.5 + 0.5 * erf(u * (0.5 ** 0.5))
+        bell, fall = normal_share(u)
         z[n] = (u * bell).astype(BF16)
-        slope[n] = (bell + u * (jnp.exp(-0.5 * u * u) * 0.3989422804014327)).astype(BF16)
+        slope[n] = (bell + u * (fall * 0.3989422804014327)).astype(BF16)
         return carry
 
     lax.fori_loop(0, 16, hidden, 0)
@@ -506,22 +508,23 @@
         return pltpu.make_async_copy(stage.at[s], g_hbm.at[lax.rem(g, 2), g // 2, at, :], stage_sem.at[s])
 
     def flush(which, n):
-        @pl.when(n >= 1)
+        @pl.when(n >= 2)
         def _():
-            stage_copy(which, n - 1).wait()
+            stage_copy(which, n - 2).wait()
 
     def down_grad(n, carry):
-        services(n, ((1, 28), (4, 29), (8, 30), (12, 31)))
+        services(n, ((1, 29), (3, 30), (4, 31)))
         flush(0, n)
         stage[lax.rem(n, 2)] = (dot_nn(z[n].T, dy[...]) * factor).astype(BF16)
         stage_copy(0, n).start()
         for i in range(4):
-            @pl.when(n == 4 + 3 * i)
+            @pl.when(n == 5 + 3 * i)
             def _(i=i):
                 beat(i)
         return carry
 
     lax.fori_loop(0, 16, down_grad, 0)
+    stage_copy(0, 14).wait()
     stage_copy(0, 15).wait()
     arrived(3)
     dh[...] = jnp.zeros_like(dh)
@@ -540,6 +543,7 @@
         return carry
 
     lax.fori_loop(0, 16, ffn_back, 0)
+    stage_copy(1, 14).wait()
     stage_copy(1, 15).wait()
     out_copies = []
     for c in range(4):
@@ -621,22 +625,23 @@
 
     lax.fori_loop(0, 8, heads_back, 0)
 
-    def proj_grad(n, carry):
-        s, q, g = lax.rem(n, 2), n // 4, lax.rem(n, 4)
-        flush(2, n)
-        left = h1[:, lanes(q, 256)].T
-        for b in range(3):
-            stage[s, :, 256 * b : 256 * b + 256] = (dot_nn(left, z[3 * g + b]) * factor).astype(BF16)
-        stage[s, :, 768:1024] = (dot_nn(o[:, lanes(q, 256)].T, da[:, lanes(g, 256)]) * factor).astype(BF16)
-        stage_copy(2, n).start()
-        for i in range(5):
-            @pl.when(n == (1, 5, 8, 11, 14)[i])
-            def _(i=i):
-                beat(31 + i)
+    def proj_grad(q, carry):
+        left, right = h1[:, lanes(q, 256)].T, o[:, lanes(q, 256)].T
+        for g in range(4):
+            n = 4 * q + g
+            flush(2, n)
+            for b in range(3):
+                stage[g % 2, :, 256 * b : 256 * b + 256] = (dot_nn(left, z[3 * g + b]) * factor).astype(BF16)
+            stage[g % 2, :, 768:1024] = (dot_nn(right, da[:, 256 * g : 256 * g + 256]) * factor).astype(BF16)
+            stage_copy(2, n).start()
+            if g == 1:
+                beat(31 + q)
         return carry
 
-    lax.fori_loop(0, 16, proj_grad, 0)
+    lax.fori_loop(0, 4, proj_grad, 0)
+    stage_copy(2, 14).wait()
     stage_copy(2, 15).wait()
+    beat(35)
     for c in range(4):
         total = jnp.zeros((rows, 256), F32)
         for g in range(4):

time: 285 us -> 259 us (0.909)
  Pallas kernels: 277 us -> 251 us
    pallas_call x1, Pallas kernels: 272 us -> 246 us  [layer(): pl.pallas_call(functools.partial(layer_kernel, rows, chunk_rows, chunk_co...]
where the time goes in v4:
time: 259 us
  Pallas kernels  251 us (97%)
  local copies, waits for them, and re-layouts  6.03 us (2%)
    pallas_call x1, Pallas kernels, layer(): pl.pallas_call(functools.partial(layer_kernel, rows, chunk_rows, chunk_co...  246 us

profile of v4, /device:TPU:0, one launch (start us, length us, event | category | flops | bytes accessed | tf_op | source)
XLA Modules:
  0.0 258.6 jit_solution(5073844563190766279)
XLA Ops:
  1.9 1.3 reshape.28.upb_hbm
  3.2 245.9 %layer.1 = (bf16[512,1024]{1,0:T(8,128)(2,1)}, bf16[512,1024]{1,0:T(8,128)(2,1)}, bf16[3136,1024]{1,0:T(8,128)(2,1)}, bf16[2,2,3136,1024]{3,2,1,0:T(8,128)(2,1)}) custom-call(s32[1]{0:T(128)S(6)} %copy.27.group_ref, s32[1,1]{1,0:T(1,128)S(6)} %copy.28.images_ref, s32[2]{0:T(128)} %counts_ref.1, bf16[512,1024]{1,0:T(8,128)(2,1)} %tok_hbm.1, ...), custom_call_target="tpu_custom_call" | custom-call | tf_op jit(solution)/shard_map/layer/pallas_call | solution.py:699
  249.1 0.0 copy-start
  249.1 2.8 %copy-done = bf16[3136,1024]{1,0:T(8,128)(2,1)S(1)} copy-done((bf16[3136,1024]{1,0:T(8,128)(2,1)S(1)}, bf16[3136,1024]{1,0:T(8,128)(2,1)}, u32[]{:S(2)}) %copy-start) | copy-done | bytes 6422552
  251.9 0.0 copy-start.2
  251.9 0.0 copy-start.1
  251.9 4.8 %widen.1 = (f32[2,256]{1,0:T(2,128)}, f32[2,256]{1,0:T(2,128)}, f32[1024,768]{1,0:T(8,128)}, f32[2,256]{1,0:T(2,128)}, f32[1024,256]{1,0:T(8,128)}, /*index=5*/f...) custom-call(bf16[3136,1024]{1,0:T(8,128)(2,1)S(1)} %copy-done, ...), custom_call_target="tpu_custom_call" | custom-call | tf_op jit(solution)/shard_map/widen/pallas_call | solution.py:760
  256.7 0.0 copy-done.2
  256.7 1.0 copy.29
  257.7 0.0 copy-done.1
  257.7 1.0 copy.30
Async XLA Ops:
  249.1 2.8 %copy-start = (bf16[3136,1024]{1,0:T(8,128)(2,1)S(1)}, bf16[3136,1024]{1,0:T(8,128)(2,1)}, u32[]{:S(2)}) copy-start(bf16[3136,1024]{1,0:T(8,128)(2,1)} %get-tuple-element.25.down_ref.up_ref.proj_ref.small_ref) | copy-start | bytes 19267588
  251.9 4.8 %copy-start.2 = (bf16[512,1024]{1,0:T(8,128)(2,1)S(1)}, bf16[512,1024]{1,0:T(8,128)(2,1)}, u32[]{:S(2)}) copy-start(bf16[512,1024]{1,0:T(8,128)(2,1)} %get-tuple-element.46) | copy-start | bytes 3145732
  251.9 5.7 %copy-start.1 = (bf16[512,1024]{1,0:T(8,128)(2,1)S(1)}, bf16[512,1024]{1,0:T(8,128)(2,1)}, u32[]{:S(2)}) copy-start(bf16[512,1024]{1,0:T(8,128)(2,1)} %get-tuple-element.47) | copy-start | bytes 3145732

commit v5 on v4

--- a/solution.py
+++ b/solution.py
@@ -16,7 +16,9 @@
 F32 = jnp.float32
 BF16 = jnp.bfloat16
 MESH = pl.DeviceIdType.MESH
-VMEM_BYTES = 62 * 2**20
+VMEM_BYTES = 64 * 2**20
+STAGE_LAGS = (1, 3, 3, 3, 3, 3, 3, 3)
+PAIR_EVERY = 8
 
 
 def split_plan(chunk_rows, bit_count):
@@ -32,33 +34,38 @@
 
 
 def pipeline_plan(bit_count):
-    lag = 2 if bit_count <= 3 else 1
-    order = ["core", "x"] + [("bit", b) for b in range(bit_count)] + [("ag", b) for b in reversed(range(bit_count))]
-    skews = {stage: 1 if stage == "core" else lag for stage in order}
-    when, now = {}, 0
-    for stage in order:
-        now += skews[stage]
-        when[stage] = now
-    return skews, when, now
+    lags = list(STAGE_LAGS) if bit_count == 3 else [1] * (2 * bit_count + 2)
+    return lags[1:], [sum(lags[: i + 1]) for i in range(len(lags))]
+
+
+def power_of_two(n):
+    return 1 << (n - 1).bit_length()
 
 
 def reduce_scratch(chunk_rows, bit_count):
     plan = split_plan(chunk_rows, bit_count)
-    skews, when, _ = pipeline_plan(bit_count)
-    slots = {stage: 2 * skew for stage, skew in skews.items()}
-    held = when["ag", bit_count - 1] - when["core"] + 1
+    lags, when = pipeline_plan(bit_count)
+    held = power_of_two(when[bit_count + 2] - when[0] + 1)
+    slots = [power_of_two(2 * lag) for lag in lags]
+    half = plan[0][1]
+    stages = 2 * bit_count + 1
     return [
-        pltpu.VMEM((slots["core"], 2, chunk_rows, WIDE), BF16),
-        pltpu.VMEM((slots["core"], 2, chunk_rows, WIDE), BF16),
-        pltpu.VMEM((slots["x"], chunk_rows, WIDE), BF16),
-        pltpu.VMEM((slots["x"], chunk_rows, WIDE), BF16),
+        pltpu.VMEM((2, 2, chunk_rows, WIDE), BF16),
+        pltpu.VMEM((2, 2, chunk_rows, WIDE), BF16),
+        pltpu.VMEM((slots[0], chunk_rows, WIDE), BF16),
+        pltpu.VMEM((slots[0], chunk_rows, WIDE), BF16),
         pltpu.VMEM((held, chunk_rows, WIDE), BF16),
-        [pltpu.VMEM((slots["bit", b], r, c), BF16) for b, (_, r, c) in enumerate(plan)],
-        pltpu.SemaphoreType.DMA((2, slots["core"])),
-        pltpu.SemaphoreType.DMA((2, slots["core"])),
-        pltpu.SemaphoreType.DMA((2, slots["x"])),
-        [pltpu.SemaphoreType.DMA((2, slots["bit", b])) for b in range(bit_count)],
-        [pltpu.SemaphoreType.DMA((2, slots["ag", b])) for b in range(bit_count)],
+        [pltpu.VMEM((slots[1 + b], r, c), BF16) for b, (_, r, c) in enumerate(plan)],
+        pltpu.VMEM((2, 2, chunk_rows, WIDE), BF16),
+        pltpu.VMEM((2, 2, half, WIDE), BF16),
+        pltpu.VMEM((2, half, WIDE), BF16),
+        [pltpu.VMEM((2, r, c), BF16) for _, r, c in plan[1:]],
+        pltpu.SemaphoreType.DMA((2,)),
+        pltpu.SemaphoreType.DMA((2, 2)),
+        [pltpu.SemaphoreType.DMA((2, slots[i])) for i in range(stages)],
+        [pltpu.SemaphoreType.DMA((2, 2)) for _ in range(stages)],
+        pltpu.SemaphoreType.DMA((4,)),
+        pltpu.SemaphoreType.DMA((2,)),
     ]
 
 
@@ -70,32 +77,37 @@
 
 
 def reduction(chunk_rows, chunk_count, bit_count, g_ref, out_ref, load, core_in, x_out, x_in, acc, bit_in,
-              local_sem, core_sem, x_sem, bit_sem, ag_sem):
+              pair, pair_in, pair_x_in, pair_bit_in, load_sem, core_sem, main_sems, pair_sems, main_own_sem, pair_own_sem):
     dp, f = lax.axis_index("dp"), lax.axis_index("fsdp")
     core, across = lax.rem(f, 2), f // 2
     plan = split_plan(chunk_rows, bit_count)
-    skews, when, depth = pipeline_plan(bit_count)
-    slot = lambda stage, j: lax.rem(j, 2 * skews[stage])
+    lags, when = pipeline_plan(bit_count)
+    slot = lambda stage, j: lax.rem(j, power_of_two(2 * lags[stage]))
     held = lambda j: lax.rem(j, acc.shape[0])
+    pair_slot = lambda j: lax.rem(j // PAIR_EVERY, 2)
     bits = [lax.rem(dp // (1 << b), 2) for b in range(bit_count)]
     flips = [dp + (1 - 2 * bits[b]) * (1 << b) for b in range(bit_count)]
     core_peer = (dp, f + 1 - 2 * core)
     x_peer = (dp, f + 2 - 4 * across)
     peers = [core_peer, x_peer] + [(p, f) for p in flips]
-
-    def region(level, other):
+    main_order = list(range(bit_count))
+    pair_order = [1, 0] + main_order[2:]
+
+    def region(level, other, order):
         row, col, rows, cols = 0, 0, chunk_rows, WIDE
-        for b in range(level):
-            kind, rows, cols = plan[b]
-            bit = 1 - bits[b] if other and b == level - 1 else bits[b]
+        for i in range(level):
+            kind, rows, cols = plan[i]
+            bit = bits[order[i]]
+            if other and i == level - 1:
+                bit = 1 - bit
             if kind == "rows":
                 row = row + bit * rows
             else:
                 col = col + bit * cols
         return row, rows, col, cols
 
-    def cut(ref, lead, base, level, other):
-        row, rows, col, cols = region(level, other)
+    def cut(ref, lead, base, level, other, order):
+        row, rows, col, cols = region(level, other, order)
         row_slice = pl.ds(pl.multiple_of(base + row, 16), rows)
         col_slice = slice(None) if cols == WIDE else pl.ds(pl.multiple_of(col, 128), cols)
         return ref.at[lead + (row_slice, col_slice)]
@@ -103,92 +115,129 @@
     def rows_of(j):
         return pl.ds(pl.multiple_of(j * chunk_rows, chunk_rows), chunk_rows)
 
-    def remote(src, dst, sems, slot, peer):
-        return pltpu.make_async_remote_copy(src, dst, sems.at[0, slot], sems.at[1, slot], device_id=peer,
+    def remote(src, dst, sems, s, peer):
+        return pltpu.make_async_remote_copy(src, dst, sems.at[0, s], sems.at[1, s], device_id=peer,
                                             device_id_type=MESH)
 
     def load_copy(j):
-        s = slot("core", j)
-        return pltpu.make_async_copy(g_ref.at[core, :, rows_of(j), :], load.at[s], local_sem.at[0, s])
+        s = lax.rem(j, 2)
+        return pltpu.make_async_copy(g_ref.at[core, :, rows_of(j), :], load.at[s], load_sem.at[s])
 
     def core_copy(j):
-        s = slot("core", j)
+        s = lax.rem(j, 2)
         return remote(g_ref.at[1 - core, :, rows_of(j), :], core_in.at[s], core_sem, s, core_peer)
 
-    def x_copy(j):
-        s = slot("x", j)
-        return remote(x_out.at[s], x_in.at[s], x_sem, s, x_peer)
-
-    def bit_copy(b, j):
-        s = slot(("bit", b), j)
-        return remote(cut(acc, (held(j),), 0, b + 1, True), bit_in[b].at[s], bit_sem[b], s, (flips[b], f))
-
-    def own_copy(j):
-        return pltpu.make_async_copy(cut(acc, (held(j),), 0, bit_count, False),
-                                     cut(out_ref, (), j * chunk_rows, bit_count, False),
-                                     local_sem.at[1, slot("core", j)])
-
-    def ag_copy(b, j):
-        mine = cut(out_ref, (), j * chunk_rows, b + 1, False)
-        src = cut(acc, (held(j),), 0, bit_count, False) if b == bit_count - 1 else mine
-        return remote(src, mine, ag_sem[b], slot(("ag", b), j), (flips[b], f))
-
-    def guarded(t, delay, action):
+    def spread_copy(j, i, source, order, sems, s):
+        mine = cut(out_ref, (), j * chunk_rows, i + 1, False, order)
+        return remote(source if i == bit_count - 1 else mine, mine, sems, s, (flips[order[i]], f))
+
+    def main_part(j, level, other):
+        return cut(acc, (held(j),), 0, level, other, main_order)
+
+    def main_own(j):
+        return pltpu.make_async_copy(main_part(j, bit_count, False),
+                                     cut(out_ref, (), j * chunk_rows, bit_count, False, main_order),
+                                     main_own_sem.at[lax.rem(j, 4)])
+
+    def main_copy(stage, j):
+        s, sems = slot(stage, j), main_sems[stage]
+        if stage == 0:
+            return remote(x_out.at[s], x_in.at[s], sems, s, x_peer)
+        if stage <= bit_count:
+            b = stage - 1
+            return remote(main_part(j, b + 1, True), bit_in[b].at[s], sems, s, (flips[b], f))
+        return spread_copy(j, 2 * bit_count - stage, main_part(j, bit_count, False), main_order, sems, s)
+
+    def main_core(j):
+        s = lax.rem(j, 2)
+        for piece, target in ((1 - across, x_out.at[slot(0, j)]), (across, acc.at[held(j)])):
+            target[...] = load[s, piece] + core_in[s, piece]
+        main_copy(0, j).start()
+
+    def main_take(stage, j):
+        main_copy(stage, j).wait()
+        if stage == 0:
+            acc[held(j)] = acc[held(j)] + x_in[slot(0, j)]
+        elif stage <= bit_count:
+            part = main_part(j, stage, False)
+            part[...] = part[...] + bit_in[stage - 1][slot(stage, j)]
+        elif stage == bit_count + 1:
+            main_own(j).wait()
+        if stage == bit_count:
+            main_own(j).start()
+        if stage < 2 * bit_count:
+            main_copy(stage + 1, j).start()
+
+    def pair_part(j, level, other):
+        return cut(pair, (pair_slot(j), across), 0, level, other, pair_order)
+
+    def pair_own(j):
+        return pltpu.make_async_copy(pair_part(j, bit_count, False),
+                                     cut(out_ref, (), j * chunk_rows, bit_count, False, pair_order),
+                                     pair_own_sem.at[pair_slot(j)])
+
+    def pair_copy(stage, j):
+        s, sems = pair_slot(j), pair_sems[stage]
+        if stage == 0:
+            return remote(cut(pair, (s, slice(None)), 0, 1, True, pair_order), pair_in.at[s], sems, s, (flips[1], f))
+        if stage == 1:
+            return remote(cut(pair, (s, 1 - across), 0, 1, False, pair_order), pair_x_in.at[s], sems, s, x_peer)
+        if stage <= bit_count:
+            return remote(pair_part(j, stage, True), pair_bit_in[stage - 2].at[s], sems, s,
+                          (flips[pair_order[stage - 1]], f))
+        return spread_copy(j, 2 * bit_count - stage, pair_part(j, bit_count, False), pair_order, sems, s)
+
+    def pair_core(j):
+        s = lax.rem(j, 2)
+        pair[pair_slot(j)] = load[s] + core_in[s]
+        pair_copy(0, j).start()
+
+    def pair_take(stage, j):
+        s = pair_slot(j)
+        pair_copy(stage, j).wait()
+        if stage == 0:
+            part = cut(pair, (s, slice(None)), 0, 1, False, pair_order)
+            part[...] = part[...] + pair_in[s]
+        elif stage == 1:
+            part = pair_part(j, 1, False)
+            part[...] = part[...] + pair_x_in[s]
+        elif stage <= bit_count:
+            part = pair_part(j, stage, False)
+            part[...] = part[...] + pair_bit_in[stage - 2][s]
+        elif stage == bit_count + 1:
+            pair_own(j).wait()
+        if stage == bit_count:
+            pair_own(j).start()
+        if stage < 2 * bit_count:
+            pair_copy(stage + 1, j).start()
+
+    def guarded(t, delay, *actions):
         j = t - delay
-
-        @pl.when(jnp.logical_and(j >= 0, j < chunk_count))
-        def _():
-            action(j)
-
-    def on_ag(b):
+        inside = jnp.logical_and(j >= 0, j < chunk_count)
+        chosen = lax.rem(j, PAIR_EVERY) == 3
+        for action, choice in zip(actions, (jnp.logical_not(chosen), chosen)):
+            @pl.when(jnp.logical_and(inside, choice) if len(actions) > 1 else inside)
+            def _(action=action):
+                action(j)
+
+    def on_core(take):
         def action(j):
-            if b == bit_count - 1:
-                own_copy(j).wait()
-            ag_copy(b, j).wait()
-            if b > 0:
-                ag_copy(b - 1, j).start()
+            load_copy(j).wait()
+            core_copy(j).wait()
+            take(j)
         return action
-
-    def on_bit(b):
-        def action(j):
-            bit_copy(b, j).wait()
-            mine = cut(acc, (held(j),), 0, b + 1, False)
-            mine[...] = (mine[...].astype(F32) + bit_in[b][slot(("bit", b), j)].astype(F32)).astype(BF16)
-            if b + 1 < bit_count:
-                bit_copy(b + 1, j).start()
-            else:
-                ag_copy(b, j).start()
-                own_copy(j).start()
-        return action
-
-    def on_x(j):
-        x_copy(j).wait()
-        s = held(j)
-        acc[s] = (acc[s].astype(F32) + x_in[slot("x", j)].astype(F32)).astype(BF16)
-        bit_copy(0, j).start()
-
-    def on_core(j):
-        load_copy(j).wait()
-        core_copy(j).wait()
-        s = slot("core", j)
-        for piece, target in ((1 - across, x_out.at[slot("x", j)]), (across, acc.at[held(j)])):
-            target[...] = (load[s, piece].astype(F32) + core_in[s, piece].astype(F32)).astype(BF16)
-        x_copy(j).start()
 
     def on_start(j):
         load_copy(j).start()
         core_copy(j).start()
 
     def tick(t):
-        for b in range(bit_count):
-            guarded(t, when["ag", b], on_ag(b))
-        for b in reversed(range(bit_count)):
-            guarded(t, when["bit", b], on_bit(b))
-        guarded(t, when["x"], on_x)
-        guarded(t, when["core"], on_core)
+        for stage in reversed(range(2 * bit_count + 1)):
+            guarded(t, when[stage + 1], functools.partial(main_take, stage), functools.partial(pair_take, stage))
+        guarded(t, when[0], on_core(main_core), on_core(pair_core))
         guarded(t, 0, on_start)
 
-    return tick, chunk_count + depth, peers
+    return tick, chunk_count + when[-1], peers
 
 
 def dot_nn(a, b):
@@ -248,7 +297,7 @@
                  out_hbm, gtok_hbm, sum_hbm, g_hbm,
                  wqkv, wo, wu, wd, x, h1, qkv, o, x1, h2, z, slope, y, bias, lse, dy, dh, da, stage,
                  smalls, pack, vec, vecs, qv, upb, grads, upg,
-                 own_sem, vec_sem, rest_sem, x_sem, y_sem, z_sem, fx_sem, fy_sem, fz_sem, frest_sem, core_sem,
+                 own_sem, vec_sem, rest_sem, x_sem, y_sem, z_sem, x_sent, y_sent, z_sent, far_sent, far_sem, core_sem,
                  load_sem, save_sem, stage_sem, comm):
     tick, tick_count, peers = reduction(chunk_rows, chunk_count, bit_count, g_hbm, sum_hbm, *comm)
     ratio = chunk_rows // 64
@@ -284,25 +333,36 @@
 
     rest = pl.ds(REST, D - REST)
 
+    def piece_copy(src, dst, send, receive, peer):
+        return pltpu.make_async_remote_copy(src, dst, send, receive, device_id=peer, device_id_type=MESH)
+
     def x_copy(k):
         w, at = k // PIECES, part(k, part_x)
-        return remote(shards[w].at[at, :], full[w].at[f, at, :], x_sem, k, x_peer)
-
-    def hop(k, index, sems, peer):
-        w, at = k // PIECES, part(k, index)
-        return remote(full[w].at[x_f, at, :], full[w].at[x_f, at, :], sems, k, peer)
-
-    y_copy = lambda k: hop(k, part_x, y_sem, y_peer)
-    z_copy = lambda k: hop(k, 2 * zb, z_sem, z_peer)
-    fx_copy = lambda k: hop(k, part_x, fx_sem, core_peer)
-    fy_copy = lambda k: hop(k, part_y, fy_sem, core_peer)
-    fz_copy = lambda k: hop(k, part_z, fz_sem, core_peer)
+        return piece_copy(shards[w].at[at, :], full[w].at[f, at, :], x_sent.at[w], x_sem.at[k], x_peer)
+
+    def hop(k, index, send, receive, peer):
+        place = full[k // PIECES].at[x_f, part(k, index), :]
+        return piece_copy(place, place, send.at[k // PIECES], receive, peer)
+
+    y_copy = lambda k: hop(k, part_x, y_sent, y_sem.at[k], y_peer)
+    z_copy = lambda k: hop(k, 2 * zb, z_sent, z_sem.at[k], z_peer)
+    fx_copy = lambda k: hop(k, part_x, far_sent, far_sem.at[k // PIECES], core_peer)
+    fy_copy = lambda k: hop(k, part_y, far_sent, far_sem.at[k // PIECES], core_peer)
+    fz_copy = lambda k: hop(k, part_z, far_sent, far_sem.at[k // PIECES], core_peer)
 
     def rest_copy(w):
         return remote(shards[w].at[rest, :], full[w].at[f, rest, :], rest_sem, w, x_peer)
 
     def frest_copy(w):
-        return remote(full[w].at[x_f, rest, :], full[w].at[x_f, rest, :], frest_sem, w, core_peer)
+        place = full[w].at[x_f, rest, :]
+        return piece_copy(place, place, far_sent.at[w], far_sem.at[w], core_peer)
+
+    def far_copy(w):
+        return piece_copy(full[w].at[x_f], full[w].at[x_f], far_sent.at[w], far_sem.at[w], core_peer)
+
+    def part_sent(w, sent, peer):
+        place = full[w].at[x_f, pl.ds(0, PART_ROWS), :]
+        return piece_copy(place, place, sent.at[w], x_sem.at[0], peer)
 
     def core_copy(w):
         return remote(shards[w], full[w].at[f], core_sem, w, core_peer)
@@ -352,11 +412,7 @@
                 service(k)
 
     def arrived(w):
-        frest_copy(w).wait_recv()
-        for k in range(w * PIECES, (w + 1) * PIECES):
-            fx_copy(k).wait_recv()
-            fy_copy(k).wait_recv()
-            fz_copy(k).wait_recv()
+        far_copy(w).wait_recv()
 
     loads = [pltpu.make_async_copy(src, dst, load_sem.at[i]) for i, (src, dst) in enumerate(
         [(gain_hbm, smalls[0]), (shift_hbm, smalls[1]), (qvb_hbm, smalls[2]), (outb_hbm, smalls[3]), (upb_hbm, smalls[4]),
@@ -435,7 +491,7 @@
     service(2)
     core_copy(0).wait_recv()
     project(1)
-    for k in range(3, PIECES + Y_LAG + Z_LAG):
+    for k in range(3, PIECES + Y_LAG + Z_LAG + 1):
         service(k)
     for w in range(1, 4):
         core_copy(w).start()
@@ -444,9 +500,8 @@
     dy[...] = jnp.where(live, dy[...].astype(F32), 0.0).astype(BF16)
     arrived(0)
     project(2)
+    service(12)
     project(3)
-    service(11)
-    service(12)
     service(13)
 
     def heads(p, carry):
@@ -485,45 +540,83 @@
     lax.fori_loop(0, rows // step, norm_mid, 0)
     service(21)
 
-    def hidden(i, carry):
-        services(i, ((2, 22), (4, 23), (6, 24), (9, 25), (11, 26), (13, 27), (15, 28)))
-
-        @pl.when(i == 8)
-        def _():
-            arrived(2)
-
-        q, g = lax.rem(i, 4), order(i // 4)
+    def hidden(q, i):
+        g = order(i)
         n = 4 * q + g
         u = dot_nn(h2[...], wu[g, :, lanes(q, 256)]) + upb[4 * g + q]
         bell, fall = normal_share(u)
         z[n] = (u * bell).astype(BF16)
         slope[n] = (bell + u * (fall * 0.3989422804014327)).astype(BF16)
-        return carry
-
-    lax.fori_loop(0, 16, hidden, 0)
+
+    def hidden_near(i, carry):
+        services(i, ((0, 22), (1, 23), (3, 24)))
+        hidden(i // 2, lax.rem(i, 2))
+        return carry
+
+    lax.fori_loop(0, 4, hidden_near, 0)
+    arrived(2)
+
+    def hidden_far(i, carry):
+        hidden(0, 2 + i)
+        return carry
+
+    lax.fori_loop(0, 2, hidden_far, 0)
+    service(25)
 
     def stage_copy(which, n):
         s, q, g = lax.rem(n, 2), n // 4, lax.rem(n, 4)
         at = pl.ds(pl.multiple_of(which * D + q * 256, 256), 256)
         return pltpu.make_async_copy(stage.at[s], g_hbm.at[lax.rem(g, 2), g // 2, at, :], stage_sem.at[s])
 
-    def flush(which, n):
-        @pl.when(n >= 2)
+    def flush(which, n, start=0):
+        @pl.when(n >= start + 2)
         def _():
             stage_copy(which, n - 2).wait()
 
-    def down_grad(n, carry):
-        services(n, ((1, 29), (3, 30), (4, 31)))
-        flush(0, n)
+    def down_grad(n, start):
+        flush(0, n, start)
         stage[lax.rem(n, 2)] = (dot_nn(z[n].T, dy[...]) * factor).astype(BF16)
         stage_copy(0, n).start()
-        for i in range(4):
-            @pl.when(n == 5 + 3 * i)
-            def _(i=i):
-                beat(i)
-        return carry
-
-    lax.fori_loop(0, 16, down_grad, 0)
+
+    def down_first(n, carry):
+        services(n, ((1, 26), (3, 27)))
+        down_grad(n, 0)
+        return carry
+
+    lax.fori_loop(0, 4, down_first, 0)
+    stage_copy(0, 2).wait()
+    stage_copy(0, 3).wait()
+    beat(0)
+
+    def down_block(q, carry):
+        def units(i, inner):
+            services(4 * q + i, ((6, 28), (7, 29)))
+
+            @pl.when(4 * q + i >= 6)
+            def _():
+                hidden(q, i)
+
+            for spot, t in ((7, 1), (14, 6)):
+                @pl.when(4 * q + i == spot)
+                def _(t=t):
+                    beat(t)
+            return inner
+
+        def grads_of(g, inner):
+            n = 4 * q + g
+            services(n, ((5, 30), (6, 31)))
+            down_grad(n, 4)
+            for spot, t in ((5, 2), (7, 3), (9, 4), (11, 5), (13, 7), (15, 8)):
+                @pl.when(n == spot)
+                def _(t=t):
+                    beat(t)
+            return inner
+
+        lax.fori_loop(0, 4, units, 0)
+        lax.fori_loop(0, 4, grads_of, 0)
+        return carry
+
+    lax.fori_loop(1, 4, down_block, 0)
     stage_copy(0, 14).wait()
     stage_copy(0, 15).wait()
     arrived(3)
@@ -532,7 +625,11 @@
     def ffn_back(n, carry):
         q, g = n // 4, lax.rem(n, 4)
         flush(1, n)
-        beat(4 + n)
+
+        @pl.when(jnp.logical_or(n == 0, lax.rem(n, 5) != 0))
+        def _():
+            beat(9 + n - n // 5)
+
         du = dot_nt(dy[...], wd[g, lanes(q, 256), :]) * slope[n].astype(F32)
         low = du.astype(BF16)
         upg[n] = jnp.sum(low.astype(F32), axis=0, keepdims=True)
@@ -550,7 +647,7 @@
         slope[c] = y[:, 256 * c : 256 * c + 256].astype(BF16)
         out_copies.append(pltpu.make_async_copy(slope.at[c], out_hbm.at[:, pl.ds(256 * c, 256)], save_sem.at[c]))
         out_copies[-1].start()
-    beat(20)
+    beat(22)
     grads[...] = jnp.zeros_like(grads)
 
     def norm_back(base_ref, which, first_beat, finish):
@@ -586,16 +683,19 @@
         grads[6] += jnp.sum(low.astype(F32), axis=0, keepdims=True)
         grads[7] += jnp.sum(dy_part, axis=0, keepdims=True)
 
-    norm_back(x1, 1, 21, finish_mlp)
+    norm_back(x1, 1, 23, finish_mlp)
     for c in range(4):
         total = jnp.zeros((rows, 256), F32)
         for g in range(4):
             total += dot_nt(da[:, 256 * g : 256 * g + 256], wo[g, 256 * c : 256 * c + 256, :])
         slope[4 + c] = total.astype(BF16)
-    beat(22)
+    beat(24)
 
     def heads_back(p, carry):
-        beat(23 + p)
+        @pl.when(lax.rem(p, 4) != 3)
+        def _():
+            beat(25 + p - p // 4)
+
         at = lanes(lax.rem(p, 2), 128)
         q_pair, k_pair, v_pair, do_pair = qkv[p], qkv[8 + p], qkv[16 + p], slope[4 + p // 2, :, at]
         k_turned = k_pair.T
@@ -679,11 +779,9 @@
     lax.fori_loop(40 // ratio, tick_count, remaining, 0)
     for copy in out_copies:
         copy.wait()
-    for k in range(COUNT):
-        for copy in (x_copy(k), y_copy(k), z_copy(k), fx_copy(k), fy_copy(k), fz_copy(k)):
-            copy.wait_send()
     for w in range(4):
-        for copy in (rest_copy(w), frest_copy(w), core_copy(w)):
+        for copy in (part_sent(w, x_sent, x_peer), part_sent(w, y_sent, y_peer), part_sent(w, z_sent, z_peer),
+                     rest_copy(w), far_copy(w), core_copy(w)):
             copy.wait_send()
 
 
@@ -729,8 +827,8 @@
             pltpu.VMEM((8, 1, D), F32),
             pltpu.VMEM((16, 1, 256), F32),
             sems(4), sems(2, 3), sems(2, 4),
-            sems(2, COUNT), sems(2, COUNT), sems(2, COUNT), sems(2, COUNT), sems(2, COUNT), sems(2, COUNT),
-            sems(2, 4), sems(2, 4), sems(7), sems(9), sems(2),
+            sems(COUNT), sems(COUNT), sems(COUNT), sems(4), sems(4), sems(4), sems(4), sems(4),
+            sems(2, 4), sems(7), sems(9), sems(2),
             reduce_scratch(chunk_rows, bit_count),
         ],
         compiler_params=pltpu.CompilerParams(collective_id=1, has_side_effects=True, vmem_limit_bytes=VMEM_BYTES),

time: 259 us -> 253 us (0.977)
  Pallas kernels: 251 us -> 245 us
    pallas_call x1, Pallas kernels: 246 us -> 240 us  [layer(): pl.pallas_call(functools.partial(layer_kernel, rows, chunk_rows, chunk_co...]
where the time goes in v5:
time: 253 us
  Pallas kernels  245 us (97%)
  local copies, waits for them, and re-layouts  6.03 us (2%)
    pallas_call x1, Pallas kernels, layer(): pl.pallas_call(functools.partial(layer_kernel, rows, chunk_rows, chunk_co...  240 us

profile of v5, /device:TPU:0, one launch (start us, length us, event | category | flops | bytes accessed | tf_op | source)
XLA Modules:
  0.0 252.8 jit_solution(12059135442924744403)
XLA Ops:
  1.9 1.3 reshape.28.upb_hbm
  3.2 240.1 %layer.1 = (bf16[512,1024]{1,0:T(8,128)(2,1)}, bf16[512,1024]{1,0:T(8,128)(2,1)}, bf16[3136,1024]{1,0:T(8,128)(2,1)}, bf16[2,2,3136,1024]{3,2,1,0:T(8,128)(2,1)}) custom-call(s32[1]{0:T(128)S(6)} %copy.27.group_ref, s32[1,1]{1,0:T(1,128)S(6)} %copy.28.images_ref, s32[2]{0:T(128)} %counts_ref.1, bf16[512,1024]{1,0:T(8,128)(2,1)} %tok_hbm.1, ...), custom_call_target="tpu_custom_call" | custom-call | tf_op jit(solution)/shard_map/layer/pallas_call | solution.py:797
  243.3 0.0 copy-start
  243.3 2.8 %copy-done = bf16[3136,1024]{1,0:T(8,128)(2,1)S(1)} copy-done((bf16[3136,1024]{1,0:T(8,128)(2,1)S(1)}, bf16[3136,1024]{1,0:T(8,128)(2,1)}, u32[]{:S(2)}) %copy-start) | copy-done | bytes 6422552
  246.1 0.0 copy-start.2
  246.1 0.0 copy-start.1
  246.2 4.8 %widen.1 = (f32[2,256]{1,0:T(2,128)}, f32[2,256]{1,0:T(2,128)}, f32[1024,768]{1,0:T(8,128)}, f32[2,256]{1,0:T(2,128)}, f32[1024,256]{1,0:T(8,128)}, /*index=5*/f...) custom-call(bf16[3136,1024]{1,0:T(8,128)(2,1)S(1)} %copy-done, ...), custom_call_target="tpu_custom_call" | custom-call | tf_op jit(solution)/shard_map/widen/pallas_call | solution.py:858
  250.9 0.0 copy-done.2
  250.9 1.0 copy.29
  251.9 0.0 copy-done.1
  251.9 1.0 copy.30
Async XLA Ops:
  243.3 2.8 %copy-start = (bf16[3136,1024]{1,0:T(8,128)(2,1)S(1)}, bf16[3136,1024]{1,0:T(8,128)(2,1)}, u32[]{:S(2)}) copy-start(bf16[3136,1024]{1,0:T(8,128)(2,1)} %get-tuple-element.25.down_ref.up_ref.proj_ref.small_ref) | copy-start | bytes 19267588
  246.1 4.8 %copy-start.2 = (bf16[512,1024]{1,0:T(8,128)(2,1)S(1)}, bf16[512,1024]{1,0:T(8,128)(2,1)}, u32[]{:S(2)}) copy-start(bf16[512,1024]{1,0:T(8,128)(2,1)} %get-tuple-element.46) | copy-start | bytes 3145732
  246.1 5.7 %copy-start.1 = (bf16[512,1024]{1,0:T(8,128)(2,1)S(1)}, bf16[512,1024]{1,0:T(8,128)(2,1)}, u32[]{:S(2)}) copy-start(bf16[512,1024]{1,0:T(8,128)(2,1)} %get-tuple-element.47) | copy-start | bytes 3145732

commit v6 on v5

--- a/solution.py
+++ b/solution.py
@@ -505,7 +505,7 @@
     service(13)
 
     def heads(p, carry):
-        services(p, ((0, 14), (2, 15), (3, 16), (5, 17), (6, 18), (7, 19)))
+        services(p, ((1, 14), (2, 15), (4, 16), (5, 17), (7, 18)))
         q_pair, k_pair, v_turned = qkv[p], qkv[8 + p], qkv[16 + p].T
         total = jnp.zeros((128, rows), F32)
         for half in range(2):
@@ -524,6 +524,7 @@
     for w in range(1, 4):
         own_copy(w).wait()
         core_copy(w).wait_recv()
+    service(19)
     arrived(1)
     for g in range(4):
         at = slice(256 * g, 256 * g + 256)

time: 253 us -> 252 us (level)
  no operation moved by 1% of the time
where the time goes in v6:
time: 252 us
  Pallas kernels  244 us (97%)
  local copies, waits for them, and re-layouts  6.03 us (2%)
    pallas_call x1, Pallas kernels, layer(): pl.pallas_call(functools.partial(layer_kernel, rows, chunk_rows, chunk_co...  239 us

profile of v6, /device:TPU:0, one launch (start us, length us, event | category | flops | bytes accessed | tf_op | source)
XLA Modules:
  0.0 251.7 jit_solution(9881656776254689511)
XLA Ops:
  1.9 1.3 reshape.28.upb_hbm
  3.2 238.9 %layer.1 = (bf16[512,1024]{1,0:T(8,128)(2,1)}, bf16[512,1024]{1,0:T(8,128)(2,1)}, bf16[3136,1024]{1,0:T(8,128)(2,1)}, bf16[2,2,3136,1024]{3,2,1,0:T(8,128)(2,1)}) custom-call(s32[1]{0:T(128)S(6)} %copy.27.group_ref, s32[1,1]{1,0:T(1,128)S(6)} %copy.28.images_ref, s32[2]{0:T(128)} %counts_ref.1, bf16[512,1024]{1,0:T(8,128)(2,1)} %tok_hbm.1, ...), custom_call_target="tpu_custom_call" | custom-call | tf_op jit(solution)/shard_map/layer/pallas_call | solution.py:798
  242.1 0.0 copy-start
  242.2 2.8 %copy-done = bf16[3136,1024]{1,0:T(8,128)(2,1)S(1)} copy-done((bf16[3136,1024]{1,0:T(8,128)(2,1)S(1)}, bf16[3136,1024]{1,0:T(8,128)(2,1)}, u32[]{:S(2)}) %copy-start) | copy-done | bytes 6422552
  245.0 0.0 copy-start.2
  245.0 0.0 copy-start.1
  245.0 4.8 %widen.1 = (f32[2,256]{1,0:T(2,128)}, f32[2,256]{1,0:T(2,128)}, f32[1024,768]{1,0:T(8,128)}, f32[2,256]{1,0:T(2,128)}, f32[1024,256]{1,0:T(8,128)}, /*index=5*/f...) custom-call(bf16[3136,1024]{1,0:T(8,128)(2,1)S(1)} %copy-done, ...), custom_call_target="tpu_custom_call" | custom-call | tf_op jit(solution)/shard_map/widen/pallas_call | solution.py:859
  249.7 0.0 copy-done.2
  249.7 1.0 copy.29
  250.7 0.0 copy-done.1
  250.7 1.0 copy.30
Async XLA Ops:
  242.1 2.8 %copy-start = (bf16[3136,1024]{1,0:T(8,128)(2,1)S(1)}, bf16[3136,1024]{1,0:T(8,128)(2,1)}, u32[]{:S(2)}) copy-start(bf16[3136,1024]{1,0:T(8,128)(2,1)} %get-tuple-element.25.down_ref.up_ref.proj_ref.small_ref) | copy-start | bytes 19267588
  245.0 4.8 %copy-start.2 = (bf16[512,1024]{1,0:T(8,128)(2,1)S(1)}, bf16[512,1024]{1,0:T(8,128)(2,1)}, u32[]{:S(2)}) copy-start(bf16[512,1024]{1,0:T(8,128)(2,1)} %get-tuple-element.46) | copy-start | bytes 3145732
  245.0 5.7 %copy-start.1 = (bf16[512,1024]{1,0:T(8,128)(2,1)S(1)}, bf16[512,1024]{1,0:T(8,128)(2,1)}, u32[]{:S(2)}) copy-start(bf16[512,1024]{1,0:T(8,128)(2,1)} %get-tuple-element.47) | copy-start | bytes 3145732
